TPU v7x, 32 devices: a whole 2x2x4 slice. The times are simulated.
32 devices in a mesh: op: 4 (over x, core), sec: 8 (over z, y).
Axes of the slice: x: 2, y: 2, z: 4, core: 2. Of those that a mesh axis runs over, the one named last changes fastest.
Arguments:
- wavefunction: bfloat16 [2048, 3, 1024], P('sec'), may hold values from -6 to 6
- left_ops: bfloat16 [2048, 12, 256], P('sec', 'op'), may hold values from -0.375 to 0.375
- right_ops: bfloat16 [12, 8, 128, 128], P('op', 'sec'), may hold values from -0.15625 to 0.15625
- term_shift: int32 [12], P('op'), may hold values from -1 to 1
Outputs:
- applied: bfloat16 [2048, 3, 1024], P('sec', None, 'op')
All inputs are finite; a program needn't handle non-finite values.
Results may differ from a plain program's by a relative error of at most 0.017.
Values may be sent and summed in bfloat16 or wider, within the bound.
No kernel may reach another device: no remote copies, remote signals or barrier semaphores. Data moves between devices by JAX's collectives and lax.ppermute only.
A program may use at most 128 MiB of HBM per device.

v0:
```python
import jax
import jax.numpy as jnp
from jax import lax
from jax.sharding import PartitionSpec as P

ML = 256
MR = 128
VECS = 3


def extended(block, sides, width):
    for axis, dim in sides:
        count = lax.axis_size(axis)
        forward = [(i, i + 1) for i in range(count - 1)]
        backward = [(target, source) for source, target in forward]
        low = lax.ppermute(
            lax.slice_in_dim(block, block.shape[dim] - width, None, axis=dim), axis, forward
        )
        high = lax.ppermute(lax.slice_in_dim(block, 0, width, axis=dim), axis, backward)
        block = jnp.concatenate([low, block, high], axis=dim)
    return block


def on_device(wavefunction, left_ops, right_ops, term_shift):
    columns = wavefunction.shape[2]
    right_count = columns // MR
    term_count = left_ops.shape[1]
    packed = jnp.concatenate(
        [wavefunction.reshape(ML, VECS * columns), left_ops.reshape(ML, term_count * ML)], axis=1
    )
    padded = extended(packed, (("sec", 0),), ML)
    right_all = lax.all_gather(right_ops, "sec", axis=1, tiled=True)
    every_col = jnp.arange(right_count)
    total = jnp.zeros((ML, VECS, columns), jnp.float32)
    for inner in range(term_count):
        offset = term_shift[inner]
        rows_block = lax.dynamic_slice_in_dim(padded, (1 - offset) * ML, ML, 0)
        source = rows_block[:, : VECS * columns].reshape(ML, VECS, columns)
        left_block = rows_block[:, VECS * columns + inner * ML : VECS * columns + (inner + 1) * ML]
        product = jnp.einsum(
            "ij,jvn->ivn", left_block, source, preferred_element_type=jnp.float32
        ).astype(jnp.bfloat16)
        rolled = jnp.roll(product, -offset * MR, axis=2).reshape(ML, VECS, right_count, MR)
        result = jnp.einsum(
            "ivrk,rkm->ivrm", rolled, right_all[inner], preferred_element_type=jnp.float32
        )
        col_valid = (every_col + offset >= 0) & (every_col + offset < right_count)
        result = jnp.where(col_valid[None, None, :, None], result, jnp.zeros((), jnp.float32))
        total = total + result.reshape(ML, VECS, columns)
    row_layout = total.astype(jnp.bfloat16)
    summed = lax.psum_scatter(
        row_layout.astype(jnp.float32).astype(jnp.bfloat16), "op", scatter_dimension=2, tiled=True
    )
    return summed


def solution(mesh):
    in_specs = (P("sec", None, None), P("sec", "op", None), P("op", "sec", None, None), P("op"))
    out_specs = P("sec", None, "op")
    return jax.shard_map(
        on_device, mesh=mesh, in_specs=in_specs, out_specs=out_specs, check_vma=False
    )
```

profile of v0, /device:TPU:17, one launch (start us, length us, event | category | flops | bytes accessed | tf_op | source)
XLA Modules:
  0.0 201.8 jit_solution(192865447512238857)
XLA Ops:
  6.5 1.3 copy.11
  7.8 0.2 copy.13
  8.1 0.7 copy.10
  8.8 0.9 copy.12
  9.7 1.4 pad_maximum_fusion.1
  11.1 3.0 %collective-permute-start.1 = (bf16[256,3840]{1,0:T(8,128)(2,1)}, bf16[256,3840]{1,0:T(8,128)(2,1)}, u32[]{:S(2)}, u32[]{:S(2)}) collective-permute-start(bf16[256,3840]{1,0:T(8,128)(2,1)} %pad_maximum_fusion.1), channel_id=1, source_target_pairs={{1,0},{2,1},{3,2},{4,3},{5,4},{6,5},{7,6},{9,8},{10,9},{11,10},{12... | collective-permute-start | bytes 5898248 | tf_op jit(solution)/shard_map/ppermute | solution.py:19
  14.1 2.2 %collective-permute-start = (bf16[256,3840]{1,0:T(8,128)(2,1)}, bf16[256,3840]{1,0:T(8,128)(2,1)}, u32[]{:S(2)}, u32[]{:S(2)}) collective-permute-start(bf16[256,3840]{1,0:T(8,128)(2,1)} %pad_maximum_fusion.1), channel_id=1, source_target_pairs={{0,1},{1,2},{2,3},{3,4},{4,5},{5,6},{6,7},{8,9},{9,10},{10,11},{11... | collective-permute-start | bytes 5898248 | tf_op jit(solution)/shard_map/ppermute | solution.py:16
  16.4 0.7 fusion.11
  21.2 0.7 compare_and_fusion.2
  21.9 1.3 compare_and_fusion
  23.2 97.0 %all_gather.3 = bf16[3,8,128,128]{2,3,1,0:T(8,128)(2,1)} all-gather(bf16[3,1,128,128]{2,3,1,0:T(8,128)(2,1)S(1)} %copy.17), channel_id=1, replica_groups=mesh['op'=4,'sec'=8] {'sec'}, dimensions={1}, use_global_device_ids=true | all-gather | bytes 884736 | tf_op jit(solution)/shard_map/all_gather | solution.py:32
  120.2 3.2 %pad_maximum_fusion = bf16[768,3840]{1,0:T(8,128)(2,1)S(1)} fusion(bf16[256,3840]{1,0:T(8,128)(2,1)} %collective-permute-done.1, bf16[256,768]{1,0:T(8,128)(2,1)S(1)} %copy.13, bf16[256,3072]{1,0:T(8,128)(2,1)S(1)} %copy.12, bf16[256,3840]{1,0:T(8,128)(2,1)} %collective-permute-done), kind=kLoop, calls=%fused_computation | loop fusion | flops 23592960 | bytes 11796480 | tf_op jit(solution)/shard_map/concatenate | solution.py:20
  123.4 2.2 %constant_dynamic-slice_fusion.2 = (bf16[256,3072]{1,0:T(8,128)(2,1)S(1)}, bf16[256,3072]{1,0:T(8,128)(2,1)S(1)}, bf16[256,3072]{1,0:T(8,128)(2,1)}) fusion(bf16[768,3840]{1,0:T(8,128)(2,1)S(1)} %pad_maximum_fusion, s32[]{:T(128)S(6)} %select_n.32, s32[]{:T(128)S(6)} %select_n.36, s32[]{:T(128)S(6)} %select_n.34), kind=kLoop, calls=%fused_computation.29 | loop fusion | bytes 9437196 | tf_op jit(solution)/shard_map/slice | solution.py:38
  125.7 0.7 copy-done
  126.4 1.6 copy.23
  128.1 2.1 %convolution_convert_fusion = bf16[256,3,1024]{2,0,1:T(8,128)(2,1)S(1)} fusion(bf16[256,3,1024]{0,2,1:T(8,128)(2,1)} %bitcast.48, bf16[768,3840]{1,0:T(8,128)(2,1)} %copy-done, s32[]{:T(128)S(6)} %select_n.36, s32[]{:T(128)S(6)} %add.88), kind=kOutput, calls=%fused_computation.9 | convolution fusion | flops 403439616 | bytes 3276808 | tf_op jit(solution)/shard_map/ij,jvn->ivn/dot_general | solution.py:40
  130.2 2.1 %fusion = bf16[256,3,1024]{2,0,1:T(8,128)(2,1)} fusion(s32[]{:T(128)S(6)} %select_n.47, bf16[256,3,1024]{2,0,1:T(8,128)(2,1)S(1)} %convolution_convert_fusion), kind=kLoop, calls=%fused_computation.12 | loop fusion | flops 3145728 | bytes 3145732 | tf_op jit(solution)/shard_map/jit(_roll_dynamic)/concatenate | solution.py:43
  132.3 1.7 copy.25
  134.0 2.7 %copy.19 = bf16[256,3072]{0,1:T(8,128)(2,1)} copy(bf16[256,3072]{1,0:T(8,128)(2,1)} %get-tuple-element.8) | data formatting | bytes 3145728 | tf_op jit(solution)/shard_map/slice | solution.py:38
  136.7 2.1 %convolution_convert_fusion.1 = bf16[256,3,1024]{2,0,1:T(8,128)(2,1)S(1)} fusion(bf16[256,3,1024]{0,2,1:T(8,128)(2,1)} %bitcast.49, bf16[768,3840]{1,0:T(8,128)(2,1)} %copy-done, s32[]{:T(128)S(6)} %select_n.34, s32[]{:T(128)S(6)} %add.87), kind=kOutput, calls=%fused_computation.10 | convolution fusion | flops 403439616 | bytes 3276808 | tf_op jit(solution)/shard_map/ij,jvn->ivn/dot_general | solution.py:40
  138.8 2.2 %fusion.1 = bf16[256,3,1024]{2,0,1:T(8,128)(2,1)} fusion(s32[]{:T(128)S(6)} %select_n.45, bf16[256,3,1024]{2,0,1:T(8,128)(2,1)S(1)} %convolution_convert_fusion.1), kind=kLoop, calls=%fused_computation.13 | loop fusion | flops 3145728 | bytes 3145732 | tf_op jit(solution)/shard_map/jit(_roll_dynamic)/concatenate | solution.py:43
  140.9 2.6 %copy.21 = bf16[256,3,1024]{0,2,1:T(8,128)(2,1)} copy(bf16[256,3,1024]{2,0,1:T(8,128)(2,1)} %fusion.1) | data formatting | bytes 3145728 | tf_op jit(solution)/shard_map/jit(_roll_dynamic)/dynamic_slice | solution.py:43
  143.6 1.6 copy.14
  145.2 2.1 %convolution_convert_fusion.2 = bf16[256,3,1024]{2,0,1:T(8,128)(2,1)S(1)} fusion(bf16[256,3,1024]{0,2,1:T(8,128)(2,1)} %bitcast.47, bf16[768,3840]{1,0:T(8,128)(2,1)} %copy-done, s32[]{:T(128)S(6)} %select_n.32, s32[]{:T(128)S(6)} %add.86), kind=kOutput, calls=%fused_computation.11 | convolution fusion | flops 403439616 | bytes 3276808 | tf_op jit(solution)/shard_map/ij,jvn->ivn/dot_general | solution.py:40
  147.3 2.1 %fusion.2 = bf16[256,3,1024]{2,0,1:T(8,128)(2,1)} fusion(s32[]{:T(128)S(6)} %select_n.43, bf16[256,3,1024]{2,0,1:T(8,128)(2,1)S(1)} %convolution_convert_fusion.2), kind=kLoop, calls=%fused_computation.14 | loop fusion | flops 3145728 | bytes 3145732 | tf_op jit(solution)/shard_map/jit(_roll_dynamic)/concatenate | solution.py:43
  149.4 2.7 %copy.16 = bf16[256,3,1024]{0,2,1:T(8,128)(2,1)} copy(bf16[256,3,1024]{2,0,1:T(8,128)(2,1)} %fusion.2) | data formatting | bytes 3145728 | tf_op jit(solution)/shard_map/jit(_roll_dynamic)/dynamic_slice | solution.py:43
  152.1 1.7 fusion.4
  153.8 0.6 fusion.6
  154.4 0.8 fusion.8
  155.1 1.3 copy.27
  156.5 36.5 %reduce-scatter.2.cloned.1.call-done = bf16[256,3,256]{0,2,1:T(8,128)(2,1)} async-done(((bf16[256,3,1024]{0,2,1:T(8,128)(2,1)}), bf16[256,3,256]{0,2,1:T(8,128)(2,1)}) %reduce-scatter.2.cloned.1.call-update) | async-done | bytes 393232 | tf_op jit(solution)/shard_map/reduce_scatter | solution.py:51
  193.0 1.9 copy.28
  (18 shorter events, 0.2 us)
Async XLA Ops:
  6.5 1.5 copy-start.4
  6.5 186.5 %reduce-scatter.2.cloned.1.call-start = ((), (), s32[]{:S(2)}) async-start(), calls=%async_computation.1 | async-start | bytes 1966080 | tf_op jit(solution)/shard_map/reduce_scatter | solution.py:51
  9.6 6.7 %copy-start.6 = (s32[3]{0:T(128)S(1)}, s32[3]{0:T(128)}, u32[]{:S(2)}) copy-start(s32[3]{0:T(128)} %param.9) | copy-start | bytes 40
  9.6 11.4 %copy-start.5 = (bf16[3,1,128,128]{3,2,1,0:T(8,128)(2,1)S(1)}, bf16[3,1,128,128]{3,2,1,0:T(8,128)(2,1)}, u32[]{:S(2)}) copy-start(bf16[3,1,128,128]{3,2,1,0:T(8,128)(2,1)} %param.8) | copy-start | bytes 294916
  11.1 109.1 %collective-permute-start.1 = (bf16[256,3840]{1,0:T(8,128)(2,1)}, bf16[256,3840]{1,0:T(8,128)(2,1)}, u32[]{:S(2)}, u32[]{:S(2)}) collective-permute-start(bf16[256,3840]{1,0:T(8,128)(2,1)} %pad_maximum_fusion.1), channel_id=1, source_target_pairs={{1,0},{2,1},{3,2},{4,3},{5,4},{6,5},{7,6},{9,8},{10,9},{11,10},{12... | collective-permute-start | bytes 5898248 | tf_op jit(solution)/shard_map/ppermute | solution.py:19
  14.1 106.1 %collective-permute-start = (bf16[256,3840]{1,0:T(8,128)(2,1)}, bf16[256,3840]{1,0:T(8,128)(2,1)}, u32[]{:S(2)}, u32[]{:S(2)}) collective-permute-start(bf16[256,3840]{1,0:T(8,128)(2,1)} %pad_maximum_fusion.1), channel_id=1, source_target_pairs={{0,1},{1,2},{2,3},{3,4},{4,5},{5,6},{6,7},{8,9},{9,10},{10,11},{11... | collective-permute-start | bytes 5898248 | tf_op jit(solution)/shard_map/ppermute | solution.py:16
  123.4 3.0 %copy-start = (bf16[768,3840]{1,0:T(8,128)(2,1)}, bf16[768,3840]{1,0:T(8,128)(2,1)S(1)}, u32[]{:S(2)}) copy-start(bf16[768,3840]{1,0:T(8,128)(2,1)S(1)} %pad_maximum_fusion) | copy-start | bytes 17694724
  149.4 2.7 %copy-start.1 = (bf16[256,3,1024]{0,2,1:T(8,128)(2,1)S(1)}, bf16[256,3,1024]{0,2,1:T(8,128)(2,1)}, u32[]{:S(2)}) copy-start(bf16[256,3,1024]{0,2,1:T(8,128)(2,1)} %copy.21) | copy-start | bytes 4718596
  152.1 1.7 copy-start.2
  152.1 1.7 copy-start.3
Sparse Core Ops, SparseCore 0:
  156.6 36.3 reduce-scatter.1
where the time goes:
time: 204 us; the launch traced here: 202 us
  blocking collectives  97 us (48%)
  waiting for transfers between devices  36.5 us (18%)
  local copies, waits for them, and re-layouts  23.1 us (11%)
  between operations  17.6 us (9%)
  other arithmetic  13 us (6%)
  matrix products  9.25 us (5%)
  starting transfers between devices  5.27 us (3%)
    all_gather x1, blocking collectives, on_device(): right_all = lax.all_gather(right_ops, 'sec', axis=1, tiled=True)  97 us
    reduce_scatter x1, waiting for transfers between devices, on_device(): lax.psum_scatter(row_layout.astype(jnp.float32).astype(jnp.bfloat16), 'op...  36.5 us
    slice x4, local copies, waits for them, and re-layouts, on_device(): source = rows_block[:, :VECS * columns].reshape(ML, VECS, columns)  8.17 us
    dynamic_slice x3, local copies, waits for them, and re-layouts, on_device(): jnp.roll(product, -offset * MR, axis=2).reshape(ML, VECS, right_count, MR)  7.04 us
    concatenate x3, other arithmetic, on_device(): jnp.roll(product, -offset * MR, axis=2).reshape(ML, VECS, right_count, MR)  6.42 us
    dot_general x3, matrix products, on_device(): jnp.einsum('ij,jvn->ivn', left_block, source, preferred_element_type=jnp....  6.27 us
  transfers between devices with their start and end apart: 3, of which 1 were waited for; matrix products, arithmetic and copies ran while one was open for 1% of the time, Pallas kernels for 0%

commit v1 on v0

v1 whole, which is shorter than its diff:
```python
import functools

import jax
import jax.numpy as jnp
from jax import lax
from jax.experimental import pallas as pl
from jax.experimental.pallas import tpu as pltpu
from jax.sharding import PartitionSpec as P

ML = 256
MR = 128
VECS = 3
VMEM_BYTES = 48 * 1024 * 1024


def over_op(x, n_op, bit):
    return lax.ppermute(x, "op", [(o, o ^ bit) for o in range(n_op)])


def over_sec(x, n_sec, bit):
    return lax.ppermute(x, "sec", [(d, d ^ bit) for d in range(n_sec)])


def doubled(piece, n_op):
    pieces = [piece]
    bit = n_op // 2
    while bit:
        pieces = pieces + [over_op(p, n_op, bit) for p in pieces]
        bit //= 2
    return pieces


def shifts_of(term_shift, n_op):
    held = term_shift[None]
    bit = n_op // 2
    while bit:
        held = jnp.concatenate([held, over_op(held, n_op, bit)])
        bit //= 2
    return held


def right_classes(right_ops, n_op, n_sec):
    per = n_sec // n_op
    op, sec = lax.axis_index("op"), lax.axis_index("sec")
    held = right_ops.reshape((1,) + right_ops.shape[:1] + right_ops.shape[2:])
    bit = n_op // 2
    while bit > 1:
        same = (op & bit) == ((sec // per) & bit)
        first, second = [], []
        for o in range(n_op):
            for d in range(n_sec):
                source = o * n_sec + d
                if (o & bit) == ((d // per) & bit):
                    first.append((source, o * n_sec + (d ^ (bit * per))))
                else:
                    first.append((source, (o ^ bit) * n_sec + d))
                    second.append((source, (o ^ bit) * n_sec + (d ^ (bit * per))))
        one = lax.ppermute(held, ("op", "sec"), first)
        two = lax.ppermute(held, ("op", "sec"), second)
        held = jnp.concatenate([jnp.where(same, held, one), jnp.where(same, one, two)])
        bit //= 2
    classes = [held]
    bit = 1
    while bit < per:
        classes = classes + [over_sec(c, n_sec, bit) for c in classes]
        bit *= 2
    same = (op & 1) == ((sec // per) & 1)
    done = []
    for own in classes:
        other = over_sec(own, n_sec, per)
        mine, theirs = jnp.where(same, own, other), jnp.where(same, other, own)
        done.append([mine, over_op(theirs, n_op, 1)])
    return done


def left_kernel(n_op, place, shift, *refs):
    *lefts, wave, z_ref, window, sems = refs
    width = z_ref.shape[3]
    per = width // MR
    terms = lefts[0].shape[0]
    op = place[0]
    start = pl.multiple_of(op * width, MR)
    middle = pltpu.make_async_copy(
        wave.at[:, :, pl.ds(start, width)], window.at[:, :, pl.ds(MR, width)], sems.at[0]
    )
    middle.start()

    def edge(valid, source, target, sem):
        @pl.when(valid)
        def _():
            copy = pltpu.make_async_copy(
                wave.at[:, :, pl.ds(pl.multiple_of(source, MR), MR)], window.at[:, :, pl.ds(target, MR)], sem
            )
            copy.start()
            copy.wait()

        @pl.when(jnp.logical_not(valid))
        def _():
            window[:, :, pl.ds(target, MR)] = jnp.zeros((VECS, ML, MR), jnp.bfloat16)

    edge(op > 0, start - MR, 0, sems.at[1])
    edge(op < n_op - 1, start + width, MR + width, sems.at[2])
    middle.wait()
    for piece, left in enumerate(lefts):
        for inner in range(terms):
            offset = pl.multiple_of((1 + shift[piece, inner]) * MR, MR)
            for v in range(VECS):
                z_ref[piece * terms + inner, v] = jnp.dot(
                    left[inner], window[v, :, pl.ds(offset, width)], preferred_element_type=jnp.float32
                ).astype(jnp.bfloat16)


def left_products(place, shift, lefts, wave, n_op):
    terms = lefts[0].shape[0]
    width = wave.shape[2] // n_op
    z_shape = (n_op * terms, VECS, ML, width)
    return pl.pallas_call(
        functools.partial(left_kernel, n_op),
        out_shape=jax.ShapeDtypeStruct(z_shape, jnp.bfloat16),
        in_specs=[pl.BlockSpec(memory_space=pltpu.SMEM)] * 2
        + [pl.BlockSpec(memory_space=pltpu.VMEM)] * n_op
        + [pl.BlockSpec(memory_space=pl.ANY)],
        out_specs=pl.BlockSpec(memory_space=pltpu.VMEM),
        scratch_shapes=[pltpu.VMEM((VECS, ML, width + 2 * MR), jnp.bfloat16), pltpu.SemaphoreType.DMA((3,))],
        compiler_params=pltpu.CompilerParams(vmem_limit_bytes=VMEM_BYTES),
        cost_estimate=pl.CostEstimate(
            flops=2 * n_op * terms * VECS * ML * ML * width, bytes_accessed=8 * 1024 * 1024, transcendentals=0
        ),
        name="left_products",
    )(place, shift, *lefts, wave)


def right_kernel(cls, per, place, shift, z_any, mine, theirs, zero_ref, up_ref, down_ref, z_cols, total, sem):
    column = pl.multiple_of(((place[1] % per) ^ cls) * MR, MR)
    copy = pltpu.make_async_copy(z_any.at[:, :, :, pl.ds(column, MR)], z_cols, sem)
    copy.start()
    total[...] = jnp.zeros_like(total)
    copy.wait()
    half, terms = mine.shape[0], mine.shape[1]
    for piece in range(2 * half):
        right = mine if piece < half else theirs
        for inner in range(terms):
            total[1 + shift[piece, inner]] += jnp.dot(
                z_cols[piece * terms + inner].reshape(VECS * ML, MR),
                right[piece % half, inner],
                preferred_element_type=jnp.float32,
            ).reshape(VECS, ML, MR)
    zero_ref[...] = total[1]
    up_ref[...] = total[2].astype(jnp.bfloat16)
    down_ref[...] = total[0].astype(jnp.bfloat16)


def right_products(cls, per, place, shift, z, mine, theirs):
    block = (VECS, ML, MR)
    vmem = pl.BlockSpec(memory_space=pltpu.VMEM)
    smem = pl.BlockSpec(memory_space=pltpu.SMEM)
    return pl.pallas_call(
        functools.partial(right_kernel, cls, per),
        out_shape=[
            jax.ShapeDtypeStruct(block, jnp.float32),
            jax.ShapeDtypeStruct(block, jnp.bfloat16),
            jax.ShapeDtypeStruct(block, jnp.bfloat16),
        ],
        in_specs=[smem, smem, pl.BlockSpec(memory_space=pl.ANY), vmem, vmem],
        out_specs=[vmem] * 3,
        scratch_shapes=[
            pltpu.VMEM((z.shape[0],) + block, jnp.bfloat16),
            pltpu.VMEM((3,) + block, jnp.float32),
            pltpu.SemaphoreType.DMA,
        ],
        compiler_params=pltpu.CompilerParams(vmem_limit_bytes=VMEM_BYTES),
        cost_estimate=pl.CostEstimate(
            flops=2 * z.shape[0] * VECS * ML * MR * MR, bytes_accessed=4 * 1024 * 1024, transcendentals=0
        ),
        name="right_products",
    )(place, shift, z, mine, theirs)


def sum_kernel(per, place, *refs):
    *parts, out_ref, total = refs
    sec = place[1]
    total[...] = jnp.zeros_like(total)
    for index, part in enumerate(parts):
        cls, kind = divmod(index, 3)
        source = sec if kind == 0 else (sec + per - 1 if kind == 1 else sec + 1)
        column = pl.multiple_of(((source % per) ^ cls) * MR, MR)
        total[:, :, pl.ds(column, MR)] += part[...].astype(jnp.float32)
    out_ref[...] = total[...].astype(jnp.bfloat16)


def summed(per, place, parts):
    shape = (VECS, ML, per * MR)
    vmem = pl.BlockSpec(memory_space=pltpu.VMEM)
    return pl.pallas_call(
        functools.partial(sum_kernel, per),
        out_shape=jax.ShapeDtypeStruct(shape, jnp.bfloat16),
        in_specs=[pl.BlockSpec(memory_space=pltpu.SMEM)] + [vmem] * len(parts),
        out_specs=vmem,
        scratch_shapes=[pltpu.VMEM(shape, jnp.float32)],
        compiler_params=pltpu.CompilerParams(vmem_limit_bytes=VMEM_BYTES),
        name="summed",
    )(place, *parts)


def on_device(n_op, n_sec, wavefunction, left_ops, right_ops, term_shift):
    per = n_sec // n_op
    place = jnp.stack([lax.axis_index("op"), lax.axis_index("sec")]).astype(jnp.int32)
    wave = wavefunction.transpose(1, 0, 2)
    lefts = doubled(left_ops.transpose(1, 0, 2), n_op)
    rights = right_classes(right_ops, n_op, n_sec)
    shift = shifts_of(term_shift, n_op)
    z = left_products(place, shift, lefts, wave, n_op)
    forward = [(d, d + 1) for d in range(n_sec - 1)]
    backward = [(d + 1, d) for d in range(n_sec - 1)]
    parts = []
    for cls, (mine, theirs) in enumerate(rights):
        zero, up, down = right_products(cls, per, place, shift, z, mine, theirs)
        parts += [zero, lax.ppermute(up, "sec", forward), lax.ppermute(down, "sec", backward)]
    return summed(per, place, parts).transpose(1, 0, 2)


def solution(mesh):
    in_specs = (P("sec", None, None), P("sec", "op", None), P("op", "sec", None, None), P("op"))
    out_specs = P("sec", None, "op")
    return jax.shard_map(
        functools.partial(on_device, mesh.shape["op"], mesh.shape["sec"]),
        mesh=mesh,
        in_specs=in_specs,
        out_specs=out_specs,
        check_vma=False,
    )
```

time: 204 us -> 63 us (0.31)
  blocking collectives: 97 us -> 0 us
  starting transfers between devices: 5.27 us -> 31.5 us
  waiting for transfers between devices: 36.5 us -> 13.9 us
  local copies, waits for them, and re-layouts: 23.1 us -> 4.73 us
  between operations: 17.6 us -> 0.16 us
  other arithmetic: 13 us -> 2.4 us
  Pallas kernels: 0 us -> 10 us
  matrix products: 9.25 us -> 0 us
    all_gather x1 -> x0, blocking collectives: 97 us -> none  [on_device(): right_all = lax.all_gather(right_ops, 'sec', axis=1, tiled=True)]
    reduce_scatter x1 -> x0, waiting for transfers between devices: 36.5 us -> none  [on_device(): lax.psum_scatter(row_layout.astype(jnp.float32).astype(jnp.bfloat16), 'op...]
    ppermute x2 -> x16, starting transfers between devices: 5.27 us -> 31.5 us  [the longest x7 10.2 us: over_op(): return lax.ppermute(x, 'op', [(o, o ^ bit) for o in range(n_op)])]
    ppermute x2 -> x16, waiting for transfers between devices: 0.01 us -> 13.9 us  [the longest x2 5.8 us: on_device(): lax.ppermute(down, 'sec', backward)]
    pallas_call x0 -> x4, Pallas kernels: none -> 10 us  [the longest x1 4.34 us: left_products(): pl.pallas_call(functools.partial(left_kernel, n_op), out_shape=jax.ShapeD...]
    concatenate x5 -> x3, other arithmetic: 11 us -> 1.35 us  [the longest x2 1.33 us: shifts_of(): held = jnp.concatenate([held, over_op(held, n_op, bit)])]
    dot_general x6 -> x0, matrix products: 9.25 us -> none  [the longest x3 6.27 us: on_device(): jnp.einsum('ij,jvn->ivn', left_block, source, preferred_element_type=jnp....]
    slice x5 -> x0, local copies, waits for them, and re-layouts: 8.84 us -> none  [the longest x4 8.17 us: on_device(): source = rows_block[:, :VECS * columns].reshape(ML, VECS, columns)]
  transfers between devices with their start and end apart: 3 -> 16, of which waited for: 1 -> 6; matrix products, arithmetic and copies ran while one was open for 1% -> 4% of each run, Pallas kernels for 0% -> 13%
where the time goes in v1:
time: 63 us; the launch traced here: 62.7 us
  starting transfers between devices  31.5 us (50%)
  waiting for transfers between devices  13.9 us (22%)
  Pallas kernels  10 us (16%)
  local copies, waits for them, and re-layouts  4.73 us (8%)
  other arithmetic  2.4 us (4%)
    ppermute x7, starting transfers between devices, over_op(): return lax.ppermute(x, 'op', [(o, o ^ bit) for o in range(n_op)])  10.2 us
    ppermute x2, starting transfers between devices, on_device(): lax.ppermute(down, 'sec', backward)  6.97 us
    ppermute x2, waiting for transfers between devices, on_device(): lax.ppermute(down, 'sec', backward)  5.8 us
    ppermute x3, starting transfers between devices, over_sec(): return lax.ppermute(x, 'sec', [(d, d ^ bit) for d in range(n_sec)])  5.8 us
    ppermute x2, starting transfers between devices, on_device(): lax.ppermute(up, 'sec', forward)  5.39 us
    unnamed x6, local copies, waits for them, and re-layouts  4.73 us
    pallas_call x1, Pallas kernels, left_products(): pl.pallas_call(functools.partial(left_kernel, n_op), out_shape=jax.ShapeD...  4.34 us
    pallas_call x2, Pallas kernels, right_products(): pl.pallas_call(functools.partial(right_kernel, cls, per), out_shape=[jax....  4.03 us
  transfers between devices with their start and end apart: 16, of which 6 were waited for; matrix products, arithmetic and copies ran while one was open for 4% of the time, Pallas kernels for 13%

profile of v1, /device:TPU:17, one launch (start us, length us, event | category | flops | bytes accessed | tf_op | source)
XLA Modules:
  0.0 62.7 jit_solution(5629195045609044139)
XLA Ops:
  0.0 1.2 %collective-permute-start.5 = (bf16[1,3,128,128]{3,2,1,0:T(8,128)(2,1)}, bf16[1,3,128,128]{3,2,1,0:T(8,128)(2,1)S(1)}, u32[]{:S(2)}, u32[]{:S(2)}) collective-permute-start(bf16[1,3,128,128]{3,2,1,0:T(8,128)(2,1)} %bitcast.12), channel_id=1, source_target_pairs={{0,4},{1,5},{2,6},{3,7},{4,20},{5,21},{6,22},{7,23},{8,12},{9,13},... | collective-permute-start | bytes 294920 | tf_op jit(solution)/shard_map/ppermute | solution.py:58
  1.2 1.9 %collective-permute-start.6 = (bf16[1,3,128,128]{3,2,1,0:T(8,128)(2,1)}, bf16[1,3,128,128]{3,2,1,0:T(8,128)(2,1)S(1)}, u32[]{:S(2)}, u32[]{:S(2)}) collective-permute-start(bf16[1,3,128,128]{3,2,1,0:T(8,128)(2,1)} %bitcast.13), channel_id=1, source_target_pairs={{4,16},{5,17},{6,18},{7,19},{12,24},{13,25},{14,26},{15,27},{16,4}... | collective-permute-start | bytes 294920 | tf_op jit(solution)/shard_map/ppermute | solution.py:59
  3.2 1.0 %collective-permute-start.3 = (bf16[3,256,256]{2,1,0:T(8,128)(2,1)}, bf16[3,256,256]{2,1,0:T(8,128)(2,1)S(1)}, u32[]{:S(2)}, u32[]{:S(2)}) collective-permute-start(bf16[3,256,256]{2,1,0:T(8,128)(2,1)} %bitcast.10), channel_id=1, source_target_pairs={{0,8},{8,0},{16,24},{24,16},{1,9},{9,1},{17,25},{25,17},{2,10},{10... | collective-permute-start | bytes 1179656 | tf_op jit(solution)/shard_map/ppermute | solution.py:17
  4.2 1.7 %collective-permute-start = (s32[1,3]{1,0:T(1,128)}, s32[1,3]{1,0:T(1,128)S(1)}, u32[]{:S(2)}, u32[]{:S(2)}) collective-permute-start(s32[1,3]{1,0:T(1,128)} %bitcast.14), channel_id=1, source_target_pairs={{0,16},{8,24},{16,0},{24,8},{1,17},{9,25},{17,1},{25,9},{2,18},{10... | collective-permute-start | bytes 44 | tf_op jit(solution)/shard_map/ppermute | solution.py:17
  5.9 2.8 %collective-permute-done.6 = bf16[1,3,128,128]{3,2,1,0:T(8,128)(2,1)S(1)} collective-permute-done((bf16[1,3,128,128]{3,2,1,0:T(8,128)(2,1)}, bf16[1,3,128,128]{3,2,1,0:T(8,128)(2,1)S(1)}, u32[]{:S(2)}, u32[]{:S(2)}) %collective-permute-start.6) | collective-permute-done | bytes 98336 | tf_op jit(solution)/shard_map/ppermute | solution.py:59
  8.7 0.9 %broadcast_select_fusion.5 = (bf16[1,3,128,128]{3,2,1,0:T(8,128)(2,1)S(1)}, bf16[1,3,128,128]{3,2,1,0:T(8,128)(2,1)S(1)}) fusion(bf16[1,3,128,128]{3,2,1,0:T(8,128)(2,1)S(1)} %collective-permute-done.5, pred[]{:T(512)S(6)} %eq.7, bf16[3,1,128,128]{3,2,1,0:T(8,128)(2,1)} %param.6, bf16[1,3,128,128]{3,2,1,0:T(8,128)(2,1)S(1)} %collective-permute-done.6), kind=kLoop, calls=%fused_computation.6 | loop fusion | flops 98304 | bytes 491521 | tf_op jit(solution)/shard_map/jit(_where)/select_n | solution.py:60
  9.7 4.2 %collective-permute-start.7 = (bf16[2,3,128,128]{3,2,1,0:T(8,128)(2,1)S(1)}, bf16[2,3,128,128]{3,2,1,0:T(8,128)(2,1)S(1)}, u32[]{:S(2)}, u32[]{:S(2)}) collective-permute-start(bf16[2,3,128,128]{3,2,1,0:T(8,128)(2,1)S(1)} %pad_maximum_fusion), channel_id=1, source_target_pairs={{0,2},{1,3},{2,0},{3,1},{4,6},{5,7},{6,4},{7,5},{8,10},{9,11},{10,... | collective-permute-start | bytes 589832 | tf_op jit(solution)/shard_map/ppermute | solution.py:21
  13.8 1.2 %collective-permute-start.11 = (bf16[2,3,128,128]{3,2,1,0:T(8,128)(2,1)S(1)}, bf16[2,3,128,128]{3,2,1,0:T(8,128)(2,1)S(1)}, u32[]{:S(2)}, u32[]{:S(2)}) collective-permute-start(bf16[2,3,128,128]{3,2,1,0:T(8,128)(2,1)S(1)} %pad_maximum_fusion), channel_id=1, source_target_pairs={{0,1},{1,0},{2,3},{3,2},{4,5},{5,4},{6,7},{7,6},{8,9},{9,8},{10,11... | collective-permute-start | bytes 589832 | tf_op jit(solution)/shard_map/ppermute | solution.py:21
  15.1 0.1 pad_add_fusion.2.place
  15.2 0.7 %pad_add_fusion.1 = s32[2,3]{1,0:T(2,128)S(1)} fusion(s32[1,3]{1,0:T(1,128)S(1)} %collective-permute-done, s32[1,3]{1,0:T(1,128)} %bitcast.15), kind=kLoop, calls=%fused_computation.8 | loop fusion | flops 6 | bytes 48 | tf_op jit(solution)/shard_map/concatenate | solution.py:37
  15.8 1.9 %collective-permute-start.1 = (s32[2,3]{1,0:T(2,128)S(1)}, s32[2,3]{1,0:T(2,128)S(1)}, u32[]{:S(2)}, u32[]{:S(2)}) collective-permute-start(s32[2,3]{1,0:T(2,128)S(1)} %pad_add_fusion.1), channel_id=1, source_target_pairs={{0,8},{8,0},{16,24},{24,16},{1,9},{9,1},{17,25},{25,17},{2,10},{10... | collective-permute-start | bytes 80 | tf_op jit(solution)/shard_map/ppermute | solution.py:17
  17.8 1.3 %collective-permute-done.11 = bf16[2,3,128,128]{3,2,1,0:T(8,128)(2,1)S(1)} collective-permute-done((bf16[2,3,128,128]{3,2,1,0:T(8,128)(2,1)S(1)}, bf16[2,3,128,128]{3,2,1,0:T(8,128)(2,1)S(1)}, u32[]{:S(2)}, u32[]{:S(2)}) %collective-permute-start.11) | collective-permute-done | bytes 196640 | tf_op jit(solution)/shard_map/ppermute | solution.py:21
  19.0 0.4 collective-permute-start.12
  19.4 2.1 %collective-permute-start.4 = (bf16[3,256,256]{2,1,0:T(8,128)(2,1)S(1)}, bf16[3,256,256]{2,1,0:T(8,128)(2,1)S(1)}, u32[]{:S(2)}, u32[]{:S(2)}) collective-permute-start(bf16[3,256,256]{2,1,0:T(8,128)(2,1)S(1)} %collective-permute-done.2.refs_1_), channel_id=1, source_target_pairs={{0,8},{8,0},{16,24},{24,16},{1,9},{9,1},{17,25},{25,17},{2,10},{10... | collective-permute-start | bytes 1179656 | tf_op jit(solution)/shard_map/ppermute | solution.py:17
  21.6 0.1 collective-permute-start.8
  21.6 1.9 %collective-permute-done.12 = bf16[2,3,128,128]{3,2,1,0:T(8,128)(2,1)S(1)} collective-permute-done((bf16[2,3,128,128]{3,2,1,0:T(8,128)(2,1)S(1)}, bf16[2,3,128,128]{3,2,1,0:T(8,128)(2,1)S(1)}, u32[]{:S(2)}, u32[]{:S(2)}) %collective-permute-start.12) | collective-permute-done | bytes 196640 | tf_op jit(solution)/shard_map/ppermute | solution.py:21
  23.6 3.3 %collective-permute-start.13 = (bf16[2,3,128,128]{3,2,1,0:T(8,128)(2,1)S(1)}, bf16[2,3,128,128]{3,2,1,0:T(8,128)(2,1)S(1)}, u32[]{:S(2)}, u32[]{:S(2)}) collective-permute-start(bf16[2,3,128,128]{3,2,1,0:T(8,128)(2,1)S(1)} %get-tuple-element.17), channel_id=1, source_target_pairs={{0,8},{8,0},{16,24},{24,16},{1,9},{9,1},{17,25},{25,17},{2,10},{10... | collective-permute-start | bytes 589832 | tf_op jit(solution)/shard_map/ppermute | solution.py:17
  26.9 0.7 %pad_add_fusion.shift = s32[4,3]{1,0:T(4,128)S(1)} fusion(s32[2,3]{1,0:T(2,128)S(1)} %collective-permute-done.1, s32[1,3]{1,0:T(1,128)S(1)} %collective-permute-done, s32[1,3]{1,0:T(1,128)} %bitcast.16), kind=kLoop, calls=%fused_computation.7 | loop fusion | flops 24 | bytes 96 | tf_op jit(solution)/shard_map/concatenate | solution.py:37
  27.6 1.4 %copy-done.1 = bf16[256,3,1024]{2,0,1:T(8,128)(2,1)S(1)} copy-done((bf16[256,3,1024]{2,0,1:T(8,128)(2,1)S(1)}, bf16[256,3,1024]{2,0,1:T(8,128)(2,1)}, u32[]{:S(2)}) %copy-start.1) | copy-done | bytes 1572888
  29.0 1.0 %copy-done.2 = bf16[256,3,256]{2,0,1:T(8,128)(2,1)S(1)} copy-done((bf16[256,3,256]{2,0,1:T(8,128)(2,1)S(1)}, bf16[256,3,256]{2,0,1:T(8,128)(2,1)}, u32[]{:S(2)}) %copy-start.2) | copy-done | bytes 393240
  30.0 4.3 %left_products.1.z_any = bf16[12,3,256,256]{3,2,1,0:T(8,128)(2,1)} custom-call(s32[2]{0:T(128)S(1)} %pad_add_fusion.2.place, s32[4,3]{1,0:T(4,128)S(1)} %pad_add_fusion.shift, bf16[3,256,256]{2,1,0:T(8,128)(2,1)S(1)} %bitcast.11, bf16[3,256,256]{2,1,0:T(8,128)(2,1)S(1)} %collective-permute-done.2.refs_1_, ...), custom_call_target="tpu_custom_call" | custom-call | flops 1207959552 | bytes 8388608 | tf_op jit(solution)/shard_map/left_products/pallas_call | solution.py:117
  34.4 2.3 %copy-done = bf16[12,3,256,256]{3,2,1,0:T(8,128)(2,1)S(1)} copy-done((bf16[12,3,256,256]{3,2,1,0:T(8,128)(2,1)S(1)}, bf16[12,3,256,256]{3,2,1,0:T(8,128)(2,1)}, u32[]{:S(2)}) %copy-start) | copy-done | bytes 4718616
  36.7 2.0 %right_products.2 = (f32[3,256,128]{2,1,0:T(8,128)S(1)}, bf16[3,256,128]{2,1,0:T(8,128)(2,1)S(1)}, bf16[3,256,128]{2,1,0:T(8,128)(2,1)S(1)}) custom-call(s32[2]{0:T(128)S(1)} %pad_add_fusion.2.place, s32[4,3]{1,0:T(4,128)S(1)} %pad_add_fusion.shift, bf16[12,3,256,256]{3,2,1,0:T(8,128)(2,1)S(1)} %copy-done, ...), custom_call_target="tpu_custom_call" | custom-call | flops 301989888 | bytes 4194304 | tf_op jit(solution)/shard_map/right_products/pallas_call | solution.py:157
  38.7 3.1 %collective-permute-start.9 = (bf16[3,256,128]{2,1,0:T(8,128)(2,1)S(1)}, bf16[3,256,128]{2,1,0:T(8,128)(2,1)S(1)}, u32[]{:S(2)}, u32[]{:S(2)}) collective-permute-start(bf16[3,256,128]{2,1,0:T(8,128)(2,1)S(1)} %get-tuple-element.12), channel_id=1, source_target_pairs={{0,1},{1,2},{2,3},{3,4},{4,5},{5,6},{6,7},{8,9},{9,10},{10,11},{11... | collective-permute-start | bytes 589832 | tf_op jit(solution)/shard_map/ppermute | solution.py:218
  41.9 3.0 %collective-permute-start.10 = (bf16[3,256,128]{2,1,0:T(8,128)(2,1)S(1)}, bf16[3,256,128]{2,1,0:T(8,128)(2,1)S(1)}, u32[]{:S(2)}, u32[]{:S(2)}) collective-permute-start(bf16[3,256,128]{2,1,0:T(8,128)(2,1)S(1)} %get-tuple-element.13), channel_id=1, source_target_pairs={{1,0},{2,1},{3,2},{4,3},{5,4},{6,5},{7,6},{9,8},{10,9},{11,10},{12... | collective-permute-start | bytes 589832 | tf_op jit(solution)/shard_map/ppermute | solution.py:218
  45.0 2.0 %right_products.3 = (f32[3,256,128]{2,1,0:T(8,128)S(1)}, bf16[3,256,128]{2,1,0:T(8,128)(2,1)S(1)}, bf16[3,256,128]{2,1,0:T(8,128)(2,1)S(1)}) custom-call(s32[2]{0:T(128)S(1)} %pad_add_fusion.2.place, s32[4,3]{1,0:T(4,128)S(1)} %pad_add_fusion.shift, bf16[12,3,256,256]{3,2,1,0:T(8,128)(2,1)S(1)} %copy-done, ...), custom_call_target="tpu_custom_call" | custom-call | flops 301989888 | bytes 4194304 | tf_op jit(solution)/shard_map/right_products/pallas_call | solution.py:157
  47.0 2.2 %collective-permute-start.14 = (bf16[3,256,128]{2,1,0:T(8,128)(2,1)S(1)}, bf16[3,256,128]{2,1,0:T(8,128)(2,1)S(1)}, u32[]{:S(2)}, u32[]{:S(2)}) collective-permute-start(bf16[3,256,128]{2,1,0:T(8,128)(2,1)S(1)} %get-tuple-element.15), channel_id=1, source_target_pairs={{0,1},{1,2},{2,3},{3,4},{4,5},{5,6},{6,7},{8,9},{9,10},{10,11},{11... | collective-permute-start | bytes 589832 | tf_op jit(solution)/shard_map/ppermute | solution.py:218
  49.2 3.9 %collective-permute-start.15 = (bf16[3,256,128]{2,1,0:T(8,128)(2,1)S(1)}, bf16[3,256,128]{2,1,0:T(8,128)(2,1)S(1)}, u32[]{:S(2)}, u32[]{:S(2)}) collective-permute-start(bf16[3,256,128]{2,1,0:T(8,128)(2,1)S(1)} %get-tuple-element.16), channel_id=1, source_target_pairs={{1,0},{2,1},{3,2},{4,3},{5,4},{6,5},{7,6},{9,8},{10,9},{11,10},{12... | collective-permute-start | bytes 589832 | tf_op jit(solution)/shard_map/ppermute | solution.py:218
  53.2 3.6 %collective-permute-done.10.refs_2_ = bf16[3,256,128]{2,1,0:T(8,128)(2,1)S(1)} collective-permute-done((bf16[3,256,128]{2,1,0:T(8,128)(2,1)S(1)}, bf16[3,256,128]{2,1,0:T(8,128)(2,1)S(1)}, u32[]{:S(2)}, u32[]{:S(2)}) %collective-permute-start.10) | collective-permute-done | bytes 196640 | tf_op jit(solution)/shard_map/ppermute | solution.py:218
  56.8 2.0 %collective-permute-done.14.refs_4_ = bf16[3,256,128]{2,1,0:T(8,128)(2,1)S(1)} collective-permute-done((bf16[3,256,128]{2,1,0:T(8,128)(2,1)S(1)}, bf16[3,256,128]{2,1,0:T(8,128)(2,1)S(1)}, u32[]{:S(2)}, u32[]{:S(2)}) %collective-permute-start.14) | collective-permute-done | bytes 196640 | tf_op jit(solution)/shard_map/ppermute | solution.py:218
  58.9 2.2 %collective-permute-done.15.refs_5_ = bf16[3,256,128]{2,1,0:T(8,128)(2,1)S(1)} collective-permute-done((bf16[3,256,128]{2,1,0:T(8,128)(2,1)S(1)}, bf16[3,256,128]{2,1,0:T(8,128)(2,1)S(1)}, u32[]{:S(2)}, u32[]{:S(2)}) %collective-permute-start.15) | collective-permute-done | bytes 196640 | tf_op jit(solution)/shard_map/ppermute | solution.py:218
  61.0 1.7 %summed.1 = bf16[3,256,256]{2,1,0:T(8,128)(2,1)} custom-call(s32[2]{0:T(128)S(1)} %pad_add_fusion.2.place, f32[3,256,128]{2,1,0:T(8,128)S(1)} %get-tuple-element.11.refs_0_, bf16[3,256,128]{2,1,0:T(8,128)(2,1)S(1)} %collective-permute-done.9.refs_1_, bf16[3,256,128]{2,1,0:T(8,128)(2,1)S(1)} %collective-permute-done.10.refs_2_, ...), custom_call_target="tpu_custom_call" | custom-call | tf_op jit(solution)/shard_map/summed/pallas_call | solution.py:194
  (17 shorter events, 0.2 us)
Async XLA Ops:
  0.0 5.9 %collective-permute-start.5 = (bf16[1,3,128,128]{3,2,1,0:T(8,128)(2,1)}, bf16[1,3,128,128]{3,2,1,0:T(8,128)(2,1)S(1)}, u32[]{:S(2)}, u32[]{:S(2)}) collective-permute-start(bf16[1,3,128,128]{3,2,1,0:T(8,128)(2,1)} %bitcast.12), channel_id=1, source_target_pairs={{0,4},{1,5},{2,6},{3,7},{4,20},{5,21},{6,22},{7,23},{8,12},{9,13},... | collective-permute-start | bytes 294920 | tf_op jit(solution)/shard_map/ppermute | solution.py:58
  1.2 7.5 %collective-permute-start.6 = (bf16[1,3,128,128]{3,2,1,0:T(8,128)(2,1)}, bf16[1,3,128,128]{3,2,1,0:T(8,128)(2,1)S(1)}, u32[]{:S(2)}, u32[]{:S(2)}) collective-permute-start(bf16[1,3,128,128]{3,2,1,0:T(8,128)(2,1)} %bitcast.13), channel_id=1, source_target_pairs={{4,16},{5,17},{6,18},{7,19},{12,24},{13,25},{14,26},{15,27},{16,4}... | collective-permute-start | bytes 294920 | tf_op jit(solution)/shard_map/ppermute | solution.py:59
  3.1 16.3 %collective-permute-start.2 = (bf16[3,256,256]{2,1,0:T(8,128)(2,1)}, bf16[3,256,256]{2,1,0:T(8,128)(2,1)S(1)}, u32[]{:S(2)}, u32[]{:S(2)}) collective-permute-start(bf16[3,256,256]{2,1,0:T(8,128)(2,1)} %bitcast.9), channel_id=1, source_target_pairs={{0,16},{8,24},{16,0},{24,8},{1,17},{9,25},{17,1},{25,9},{2,18},{10... | collective-permute-start | bytes 1179656 | tf_op jit(solution)/shard_map/ppermute | solution.py:17
  3.2 24.4 %collective-permute-start.3 = (bf16[3,256,256]{2,1,0:T(8,128)(2,1)}, bf16[3,256,256]{2,1,0:T(8,128)(2,1)S(1)}, u32[]{:S(2)}, u32[]{:S(2)}) collective-permute-start(bf16[3,256,256]{2,1,0:T(8,128)(2,1)} %bitcast.10), channel_id=1, source_target_pairs={{0,8},{8,0},{16,24},{24,16},{1,9},{9,1},{17,25},{25,17},{2,10},{10... | collective-permute-start | bytes 1179656 | tf_op jit(solution)/shard_map/ppermute | solution.py:17
  4.2 10.9 %collective-permute-start = (s32[1,3]{1,0:T(1,128)}, s32[1,3]{1,0:T(1,128)S(1)}, u32[]{:S(2)}, u32[]{:S(2)}) collective-permute-start(s32[1,3]{1,0:T(1,128)} %bitcast.14), channel_id=1, source_target_pairs={{0,16},{8,24},{16,0},{24,8},{1,17},{9,25},{17,1},{25,9},{2,18},{10... | collective-permute-start | bytes 44 | tf_op jit(solution)/shard_map/ppermute | solution.py:17
  9.7 11.9 %collective-permute-start.7 = (bf16[2,3,128,128]{3,2,1,0:T(8,128)(2,1)S(1)}, bf16[2,3,128,128]{3,2,1,0:T(8,128)(2,1)S(1)}, u32[]{:S(2)}, u32[]{:S(2)}) collective-permute-start(bf16[2,3,128,128]{3,2,1,0:T(8,128)(2,1)S(1)} %pad_maximum_fusion), channel_id=1, source_target_pairs={{0,2},{1,3},{2,0},{3,1},{4,6},{5,7},{6,4},{7,5},{8,10},{9,11},{10,... | collective-permute-start | bytes 589832 | tf_op jit(solution)/shard_map/ppermute | solution.py:21
  13.8 5.2 %collective-permute-start.11 = (bf16[2,3,128,128]{3,2,1,0:T(8,128)(2,1)S(1)}, bf16[2,3,128,128]{3,2,1,0:T(8,128)(2,1)S(1)}, u32[]{:S(2)}, u32[]{:S(2)}) collective-permute-start(bf16[2,3,128,128]{3,2,1,0:T(8,128)(2,1)S(1)} %pad_maximum_fusion), channel_id=1, source_target_pairs={{0,1},{1,0},{2,3},{3,2},{4,5},{5,4},{6,7},{7,6},{8,9},{9,8},{10,11... | collective-permute-start | bytes 589832 | tf_op jit(solution)/shard_map/ppermute | solution.py:21
  15.8 11.1 %collective-permute-start.1 = (s32[2,3]{1,0:T(2,128)S(1)}, s32[2,3]{1,0:T(2,128)S(1)}, u32[]{:S(2)}, u32[]{:S(2)}) collective-permute-start(s32[2,3]{1,0:T(2,128)S(1)} %pad_add_fusion.1), channel_id=1, source_target_pairs={{0,8},{8,0},{16,24},{24,16},{1,9},{9,1},{17,25},{25,17},{2,10},{10... | collective-permute-start | bytes 80 | tf_op jit(solution)/shard_map/ppermute | solution.py:17
  19.0 4.5 %collective-permute-start.12 = (bf16[2,3,128,128]{3,2,1,0:T(8,128)(2,1)S(1)}, bf16[2,3,128,128]{3,2,1,0:T(8,128)(2,1)S(1)}, u32[]{:S(2)}, u32[]{:S(2)}) collective-permute-start(bf16[2,3,128,128]{3,2,1,0:T(8,128)(2,1)S(1)} %collective-permute-done.11), channel_id=1, source_target_pairs={{0,2},{1,3},{2,0},{3,1},{4,6},{5,7},{6,4},{7,5},{8,10},{9,11},{10,... | collective-permute-start | bytes 589832 | tf_op jit(solution)/shard_map/ppermute | solution.py:21
  19.4 8.2 %collective-permute-start.4 = (bf16[3,256,256]{2,1,0:T(8,128)(2,1)S(1)}, bf16[3,256,256]{2,1,0:T(8,128)(2,1)S(1)}, u32[]{:S(2)}, u32[]{:S(2)}) collective-permute-start(bf16[3,256,256]{2,1,0:T(8,128)(2,1)S(1)} %collective-permute-done.2.refs_1_), channel_id=1, source_target_pairs={{0,8},{8,0},{16,24},{24,16},{1,9},{9,1},{17,25},{25,17},{2,10},{10... | collective-permute-start | bytes 1179656 | tf_op jit(solution)/shard_map/ppermute | solution.py:17
  21.6 12.8 %collective-permute-start.8 = (bf16[2,3,128,128]{3,2,1,0:T(8,128)(2,1)S(1)}, bf16[2,3,128,128]{3,2,1,0:T(8,128)(2,1)S(1)}, u32[]{:S(2)}, u32[]{:S(2)}) collective-permute-start(bf16[2,3,128,128]{3,2,1,0:T(8,128)(2,1)S(1)} %get-tuple-element.19), channel_id=1, source_target_pairs={{0,8},{8,0},{16,24},{24,16},{1,9},{9,1},{17,25},{25,17},{2,10},{10... | collective-permute-start | bytes 589832 | tf_op jit(solution)/shard_map/ppermute | solution.py:17
  23.6 21.4 %collective-permute-start.13 = (bf16[2,3,128,128]{3,2,1,0:T(8,128)(2,1)S(1)}, bf16[2,3,128,128]{3,2,1,0:T(8,128)(2,1)S(1)}, u32[]{:S(2)}, u32[]{:S(2)}) collective-permute-start(bf16[2,3,128,128]{3,2,1,0:T(8,128)(2,1)S(1)} %get-tuple-element.17), channel_id=1, source_target_pairs={{0,8},{8,0},{16,24},{24,16},{1,9},{9,1},{17,25},{25,17},{2,10},{10... | collective-permute-start | bytes 589832 | tf_op jit(solution)/shard_map/ppermute | solution.py:17
  27.6 1.4 %copy-start.1 = (bf16[256,3,1024]{2,0,1:T(8,128)(2,1)S(1)}, bf16[256,3,1024]{2,0,1:T(8,128)(2,1)}, u32[]{:S(2)}) copy-start(bf16[256,3,1024]{2,0,1:T(8,128)(2,1)} %param.4) | copy-start | bytes 4718596
  29.0 1.0 %copy-start.2 = (bf16[256,3,256]{2,0,1:T(8,128)(2,1)S(1)}, bf16[256,3,256]{2,0,1:T(8,128)(2,1)}, u32[]{:S(2)}) copy-start(bf16[256,3,256]{2,0,1:T(8,128)(2,1)} %param.5) | copy-start | bytes 1179652
  34.4 2.3 %copy-start = (bf16[12,3,256,256]{3,2,1,0:T(8,128)(2,1)S(1)}, bf16[12,3,256,256]{3,2,1,0:T(8,128)(2,1)}, u32[]{:S(2)}) copy-start(bf16[12,3,256,256]{3,2,1,0:T(8,128)(2,1)} %left_products.1.z_any) | copy-start | bytes 14155780
  38.7 14.4 %collective-permute-start.9 = (bf16[3,256,128]{2,1,0:T(8,128)(2,1)S(1)}, bf16[3,256,128]{2,1,0:T(8,128)(2,1)S(1)}, u32[]{:S(2)}, u32[]{:S(2)}) collective-permute-start(bf16[3,256,128]{2,1,0:T(8,128)(2,1)S(1)} %get-tuple-element.12), channel_id=1, source_target_pairs={{0,1},{1,2},{2,3},{3,4},{4,5},{5,6},{6,7},{8,9},{9,10},{10,11},{11... | collective-permute-start | bytes 589832 | tf_op jit(solution)/shard_map/ppermute | solution.py:218
  41.9 14.9 %collective-permute-start.10 = (bf16[3,256,128]{2,1,0:T(8,128)(2,1)S(1)}, bf16[3,256,128]{2,1,0:T(8,128)(2,1)S(1)}, u32[]{:S(2)}, u32[]{:S(2)}) collective-permute-start(bf16[3,256,128]{2,1,0:T(8,128)(2,1)S(1)} %get-tuple-element.13), channel_id=1, source_target_pairs={{1,0},{2,1},{3,2},{4,3},{5,4},{6,5},{7,6},{9,8},{10,9},{11,10},{12... | collective-permute-start | bytes 589832 | tf_op jit(solution)/shard_map/ppermute | solution.py:218
  47.0 11.9 %collective-permute-start.14 = (bf16[3,256,128]{2,1,0:T(8,128)(2,1)S(1)}, bf16[3,256,128]{2,1,0:T(8,128)(2,1)S(1)}, u32[]{:S(2)}, u32[]{:S(2)}) collective-permute-start(bf16[3,256,128]{2,1,0:T(8,128)(2,1)S(1)} %get-tuple-element.15), channel_id=1, source_target_pairs={{0,1},{1,2},{2,3},{3,4},{4,5},{5,6},{6,7},{8,9},{9,10},{10,11},{11... | collective-permute-start | bytes 589832 | tf_op jit(solution)/shard_map/ppermute | solution.py:218
  49.2 11.8 %collective-permute-start.15 = (bf16[3,256,128]{2,1,0:T(8,128)(2,1)S(1)}, bf16[3,256,128]{2,1,0:T(8,128)(2,1)S(1)}, u32[]{:S(2)}, u32[]{:S(2)}) collective-permute-start(bf16[3,256,128]{2,1,0:T(8,128)(2,1)S(1)} %get-tuple-element.16), channel_id=1, source_target_pairs={{1,0},{2,1},{3,2},{4,3},{5,4},{6,5},{7,6},{9,8},{10,9},{11,10},{12... | collective-permute-start | bytes 589832 | tf_op jit(solution)/shard_map/ppermute | solution.py:218

commit v2 on v0

v2 whole, which is shorter than its diff:
```python
import functools

import jax
import jax.numpy as jnp
from jax import lax
from jax.experimental import pallas as pl
from jax.experimental.pallas import tpu as pltpu
from jax.sharding import PartitionSpec as P

ML = 256
MR = 128
VECS = 3
TILE = 16
SMEM = pl.BlockSpec(memory_space=pltpu.SMEM)
VMEM = pl.BlockSpec(memory_space=pltpu.VMEM)
HBM = pl.BlockSpec(memory_space=pltpu.HBM)


def in_vmem(shape, dtype=jnp.bfloat16):
    return pltpu.VMEM(shape, dtype)


def grant(mebibytes):
    return pltpu.CompilerParams(vmem_limit_bytes=mebibytes * 1024 * 1024)


def over_op(x, n_op, bit):
    return lax.ppermute(x, "op", [(o, o ^ bit) for o in range(n_op)])


def over_sec(x, n_sec, bit):
    return lax.ppermute(x, "sec", [(d, d ^ bit) for d in range(n_sec)])


def right_first(held, n_op, n_sec, bit):
    per = n_sec // n_op
    first, second = [], []
    for o in range(n_op):
        for d in range(n_sec):
            source = o * n_sec + d
            if (o & bit) == ((d // per) & bit):
                first.append((source, o * n_sec + (d ^ (bit * per))))
            else:
                first.append((source, (o ^ bit) * n_sec + d))
                second.append((source, (o ^ bit) * n_sec + (d ^ (bit * per))))
    return lax.ppermute(held, ("op", "sec"), first), lax.ppermute(held, ("op", "sec"), second)


def pack_kernel(n_op, place, shift, left, wave, packed, window, sems):
    terms = left.shape[0]
    width = window.shape[2] - 2 * MR
    op = place[0]
    start = pl.multiple_of(op * width, MR)
    copies = [
        pltpu.make_async_copy(wave.at[:, :, pl.ds(start, width)], window.at[:, :, pl.ds(MR, width)], sems.at[0]),
        pltpu.make_async_copy(left, packed.at[:, pl.ds(0, ML)], sems.at[1]),
    ]
    for copy in copies:
        copy.start()

    def edge(valid, source, target, sem):
        @pl.when(valid)
        def _():
            copy = pltpu.make_async_copy(
                wave.at[:, :, pl.ds(pl.multiple_of(source, MR), MR)], window.at[:, :, pl.ds(target, MR)], sem
            )
            copy.start()
            copy.wait()

        @pl.when(jnp.logical_not(valid))
        def _():
            window[:, :, pl.ds(target, MR)] = jnp.zeros((VECS, ML, MR), jnp.bfloat16)

    for inner in range(terms):
        packed[inner, ML:] = jnp.full((TILE, ML), shift[inner].astype(jnp.float32)).astype(jnp.bfloat16)
    edge(op > 0, start - MR, 0, sems.at[2])
    edge(op < n_op - 1, start + width, MR + width, sems.at[3])
    for copy in copies:
        copy.wait()


def pack(place, shift, left, wave, n_op):
    width = wave.shape[2] // n_op
    return pl.pallas_call(
        functools.partial(pack_kernel, n_op),
        out_shape=[in_vmem((left.shape[0], ML + TILE, ML)), in_vmem((VECS, ML, width + 2 * MR))],
        in_specs=[SMEM, SMEM, HBM, HBM],
        out_specs=[VMEM] * 2,
        scratch_shapes=[pltpu.SemaphoreType.DMA((4,))],
        compiler_params=grant(8),
        cost_estimate=pl.CostEstimate(flops=0, bytes_accessed=32 * 1024 * 1024, transcendentals=0),
        name="pack",
    )(place, shift, pltpu.with_memory_space_constraint(left, pltpu.HBM), pltpu.with_memory_space_constraint(wave, pltpu.HBM))


def left_kernel(*refs):
    *lefts, window, z_ref, shift_ref = refs
    per = z_ref.shape[0]
    width = per * MR
    terms = lefts[0].shape[0]
    for piece, left in enumerate(lefts):
        for inner in range(terms):
            term = piece * terms + inner
            shift = jnp.max(left[inner, ML:, :MR].astype(jnp.float32)).astype(jnp.int32)
            shift_ref[term] = shift
            offset = pl.multiple_of((1 + shift) * MR, MR)
            for v in range(VECS):
                z = jnp.dot(
                    left[inner, :ML], window[v, :, pl.ds(offset, width)], preferred_element_type=jnp.float32
                ).astype(jnp.bfloat16)
                for column in range(per):
                    z_ref[column, v, :, term * MR : (term + 1) * MR] = z[:, column * MR : (column + 1) * MR]


def left_products(lefts, window):
    terms = len(lefts) * lefts[0].shape[0]
    width = window.shape[2] - 2 * MR
    return pl.pallas_call(
        left_kernel,
        out_shape=[in_vmem((width // MR, VECS, ML, terms * MR)), jax.ShapeDtypeStruct((terms,), jnp.int32)],
        in_specs=[VMEM] * (len(lefts) + 1),
        out_specs=[VMEM, SMEM],
        compiler_params=grant(8 + 4 * width // MR),
        cost_estimate=pl.CostEstimate(
            flops=2 * terms * VECS * ML * ML * width, bytes_accessed=1024 * 1024, transcendentals=0
        ),
        name="left_products",
    )(*lefts, window)


def right_kernel(cls, per, place, shift, z_ref, own, other, received, zero_ref, up_ref, down_ref, right):
    column = (place[1] % per) ^ cls
    same = place[2] == 1
    half, terms = own.shape[0], own.shape[1]
    for piece in range(2 * half):
        for inner in range(terms):
            term = piece * terms + inner
            if piece < half:
                block = jnp.where(same, own[piece, inner], other[piece, inner])
            else:
                block = received[piece - half, inner]
            for kind in range(3):
                right[term * MR : (term + 1) * MR, kind * MR : (kind + 1) * MR] = jnp.where(
                    shift[term] == kind - 1, block, jnp.zeros_like(block)
                )
    for v in range(VECS):
        y = jnp.dot(z_ref[column, v], right[...], preferred_element_type=jnp.float32)
        down_ref[v] = y[:, :MR].astype(jnp.bfloat16)
        zero_ref[v] = y[:, MR : 2 * MR]
        up_ref[v] = y[:, 2 * MR :].astype(jnp.bfloat16)


def right_products(cls, per, place, shift, z, own, other, received):
    block = (VECS, ML, MR)
    depth = z.shape[3]
    return pl.pallas_call(
        functools.partial(right_kernel, cls, per),
        out_shape=[jax.ShapeDtypeStruct(block, dtype) for dtype in (jnp.float32, jnp.bfloat16, jnp.bfloat16)],
        in_specs=[SMEM, SMEM] + [VMEM] * 4,
        out_specs=[VMEM] * 3,
        scratch_shapes=[in_vmem((depth, 3 * MR))],
        compiler_params=grant(16),
        cost_estimate=pl.CostEstimate(flops=0, bytes_accessed=0, transcendentals=0),
        name="right_products",
    )(place, shift, z, own, other, received)


def sum_kernel(per, place, *refs):
    *parts, out_ref = refs
    zeros, ups, downs = parts[::3], parts[1::3], parts[2::3]
    sec = place[1]
    below, above = (sec ^ (sec + per - 1)) % per, (sec ^ (sec + 1)) % per

    def add(low, high):
        @pl.when((below == low) & (above == high))
        def _():
            for cls in range(per):
                column = pl.multiple_of(((sec % per) ^ cls) * MR, MR)
                for v in range(VECS):
                    total = zeros[cls][v] + ups[cls ^ low][v].astype(jnp.float32)
                    total = total + downs[cls ^ high][v].astype(jnp.float32)
                    out_ref[v, :, pl.ds(column, MR)] = total.astype(jnp.bfloat16)

    carry = 1
    while carry < per:
        add(1, carry)
        if carry > 1:
            add(carry, 1)
        carry = 2 * carry + 1


def summed(per, place, parts):
    return pl.pallas_call(
        functools.partial(sum_kernel, per),
        out_shape=jax.ShapeDtypeStruct((VECS, ML, per * MR), jnp.bfloat16),
        in_specs=[SMEM] + [VMEM] * len(parts),
        out_specs=VMEM,
        compiler_params=grant(16),
        name="summed",
    )(place, *parts)


def on_device(n_op, n_sec, wavefunction, left_ops, right_ops, term_shift):
    per = n_sec // n_op
    tie = lax.optimization_barrier
    op, sec = lax.axis_index("op"), lax.axis_index("sec")
    matching = op ^ (sec // per)
    place = jnp.stack([op, sec, (matching & 1) ^ 1]).astype(jnp.int32)
    held = right_ops.reshape((1,) + right_ops.shape[:1] + right_ops.shape[2:])
    packed, window = pack(place, term_shift, left_ops.transpose(1, 0, 2), wavefunction.transpose(1, 0, 2), n_op)
    lefts = [packed]
    bit = n_op // 2
    while bit > 1:
        one, two = tie(right_first(held, n_op, n_sec, bit))
        same = (matching & bit) == 0
        held = jnp.concatenate([jnp.where(same, held, one), jnp.where(same, one, two)])
        lefts = lefts + [over_op(x, n_op, bit) for x in lefts]
        bit //= 2
    lefts = lefts + [over_op(x, n_op, 1) for x in lefts]
    owns = [held]
    bit = 1
    while bit < per:
        owns = owns + [over_sec(c, n_sec, bit) for c in owns]
        bit *= 2
    other, owns = tie((over_sec(owns[0], n_sec, per), owns))
    z, shift = left_products(lefts, window)
    forward = [(d, d + 1) for d in range(n_sec - 1)]
    backward = [(d + 1, d) for d in range(n_sec - 1)]
    same = (matching & 1) == 0
    parts = []
    for cls, own in enumerate(owns):
        received = over_op(jnp.where(same, other, own), n_op, 1)
        later = over_sec(owns[cls + 1], n_sec, per) if cls + 1 < per else None
        zero, up, down = right_products(cls, per, place, shift, z, own, other, received)
        parts += [zero, lax.ppermute(up, "sec", forward), lax.ppermute(down, "sec", backward)]
        if later is not None:
            other, _ = tie((later, up))
    return summed(per, place, parts).transpose(1, 0, 2)


def solution(mesh):
    in_specs = (P("sec", None, None), P("sec", "op", None), P("op", "sec", None, None), P("op"))
    out_specs = P("sec", None, "op")
    return jax.shard_map(
        functools.partial(on_device, mesh.shape["op"], mesh.shape["sec"]),
        mesh=mesh,
        in_specs=in_specs,
        out_specs=out_specs,
        check_vma=False,
    )
```

time: 204 us -> 52.6 us (0.26)
  blocking collectives: 97 us -> 0 us
  local copies, waits for them, and re-layouts: 23.1 us -> 0.66 us
  waiting for transfers between devices: 36.5 us -> 14.4 us
  starting transfers between devices: 5.27 us -> 26.1 us
  between operations: 17.6 us -> 0.16 us
  other arithmetic: 13 us -> 1.06 us
  Pallas kernels: 0 us -> 9.99 us
  matrix products: 9.25 us -> 0 us
    all_gather x1 -> x0, blocking collectives: 97 us -> none  [on_device(): right_all = lax.all_gather(right_ops, 'sec', axis=1, tiled=True)]
    reduce_scatter x1 -> x0, waiting for transfers between devices: 36.5 us -> none  [on_device(): lax.psum_scatter(row_layout.astype(jnp.float32).astype(jnp.bfloat16), 'op...]
    ppermute x2 -> x14, starting transfers between devices: 5.27 us -> 26.1 us  [the longest x2 6.97 us: on_device(): lax.ppermute(down, 'sec', backward)]
    ppermute x2 -> x14, waiting for transfers between devices: 0.01 us -> 14.4 us  [the longest x2 5.98 us: on_device(): lax.ppermute(down, 'sec', backward)]
    concatenate x5 -> x1, other arithmetic: 11 us -> 0.02 us  [on_device(): jnp.concatenate([jnp.where(same, held, one), jnp.where(same, one, two)])]
    pallas_call x0 -> x5, Pallas kernels: none -> 9.99 us  [the longest x2 4.03 us: right_products(): pl.pallas_call(functools.partial(right_kernel, cls, per), out_shape=[jax....]
    dot_general x6 -> x0, matrix products: 9.25 us -> none  [the longest x3 6.27 us: on_device(): jnp.einsum('ij,jvn->ivn', left_block, source, preferred_element_type=jnp....]
    slice x5 -> x0, local copies, waits for them, and re-layouts: 8.84 us -> none  [the longest x4 8.17 us: on_device(): source = rows_block[:, :VECS * columns].reshape(ML, VECS, columns)]
  transfers between devices with their start and end apart: 3 -> 14, of which waited for: 1 -> 6; matrix products, arithmetic and copies ran while one was open for 1% -> 2% of each run, Pallas kernels for 0% -> 16%
where the time goes in v2:
time: 52.6 us; the launch traced here: 52.3 us
  starting transfers between devices  26.1 us (50%)
  waiting for transfers between devices  14.4 us (27%)
  Pallas kernels  9.99 us (19%)
  other arithmetic  1.06 us (2%)
  local copies, waits for them, and re-layouts  0.66 us (1%)
    ppermute x2, starting transfers between devices, on_device(): lax.ppermute(down, 'sec', backward)  6.97 us
    ppermute x3, starting transfers between devices, over_sec(): return lax.ppermute(x, 'sec', [(d, d ^ bit) for d in range(n_sec)])  6.14 us
    ppermute x2, waiting for transfers between devices, on_device(): lax.ppermute(down, 'sec', backward)  5.98 us
    ppermute x2, starting transfers between devices, on_device(): lax.ppermute(up, 'sec', forward)  5.38 us
    ppermute x5, starting transfers between devices, over_op(): return lax.ppermute(x, 'op', [(o, o ^ bit) for o in range(n_op)])  4.47 us
    pallas_call x2, Pallas kernels, right_products(): pl.pallas_call(functools.partial(right_kernel, cls, per), out_shape=[jax....  4.03 us
    pallas_call x1, Pallas kernels, pack(): pl.pallas_call(functools.partial(pack_kernel, n_op), out_shape=[in_vmem((...  2.68 us
    ppermute x5, waiting for transfers between devices, over_op(): return lax.ppermute(x, 'op', [(o, o ^ bit) for o in range(n_op)])  2.66 us
  transfers between devices with their start and end apart: 14, of which 6 were waited for; matrix products, arithmetic and copies ran while one was open for 2% of the time, Pallas kernels for 16%

profile of v2, /device:TPU:17, one launch (start us, length us, event | category | flops | bytes accessed | tf_op | source)
XLA Modules:
  0.0 52.3 jit_solution(7077069112764998804)
XLA Ops:
  0.0 1.2 %collective-permute-start.3 = (bf16[1,3,128,128]{3,2,1,0:T(8,128)(2,1)}, bf16[1,3,128,128]{3,2,1,0:T(8,128)(2,1)S(1)}, u32[]{:S(2)}, u32[]{:S(2)}) collective-permute-start(bf16[1,3,128,128]{3,2,1,0:T(8,128)(2,1)} %bitcast.10), channel_id=1, source_target_pairs={{0,4},{1,5},{2,6},{3,7},{4,20},{5,21},{6,22},{7,23},{8,12},{9,13},... | collective-permute-start | bytes 294920 | tf_op jit(solution)/shard_map/ppermute | solution.py:46
  1.2 1.9 %collective-permute-start.4 = (bf16[1,3,128,128]{3,2,1,0:T(8,128)(2,1)}, bf16[1,3,128,128]{3,2,1,0:T(8,128)(2,1)S(1)}, u32[]{:S(2)}, u32[]{:S(2)}) collective-permute-start(bf16[1,3,128,128]{3,2,1,0:T(8,128)(2,1)} %bitcast.11), channel_id=1, source_target_pairs={{4,16},{5,17},{6,18},{7,19},{12,24},{13,25},{14,26},{15,27},{16,4}... | collective-permute-start | bytes 294920 | tf_op jit(solution)/shard_map/ppermute | solution.py:46
  3.1 0.1 pad_add_fusion.place
  3.2 0.7 %copy-done = s32[3]{0:T(128)S(1)} copy-done((s32[3]{0:T(128)S(1)}, s32[3]{0:T(128)}, u32[]{:S(2)}) %copy-start) | copy-done | bytes 36
  3.9 2.7 %pack.1 = (bf16[3,272,256]{2,1,0:T(8,128)(2,1)S(1)}, bf16[3,256,512]{2,1,0:T(8,128)(2,1)S(1)}) custom-call(s32[3]{0:T(128)S(1)} %pad_add_fusion.place, s32[3]{0:T(128)S(1)} %copy-done, bf16[3,256,256]{2,1,0:T(8,128)(2,1)} %bitcast.9, bf16[3,256,1024]{2,1,0:T(8,128)(2,1)} %bitcast.8), custom_call_target="tpu_custom_call" | custom-call | bytes 33554432 | tf_op jit(solution)/shard_map/pack/pallas_call | solution.py:84
  6.6 0.1 collective-permute-start
  6.7 0.0 collective-permute-done.3
  6.7 2.0 %collective-permute-done.4 = bf16[1,3,128,128]{3,2,1,0:T(8,128)(2,1)S(1)} collective-permute-done((bf16[1,3,128,128]{3,2,1,0:T(8,128)(2,1)}, bf16[1,3,128,128]{3,2,1,0:T(8,128)(2,1)S(1)}, u32[]{:S(2)}, u32[]{:S(2)}) %collective-permute-start.4) | collective-permute-done | bytes 98336 | tf_op jit(solution)/shard_map/ppermute | solution.py:46
  8.7 0.9 %broadcast_select_fusion.3 = (bf16[1,3,128,128]{3,2,1,0:T(8,128)(2,1)S(1)}, bf16[1,3,128,128]{3,2,1,0:T(8,128)(2,1)S(1)}) fusion(bf16[1,3,128,128]{3,2,1,0:T(8,128)(2,1)S(1)} %collective-permute-done.3, pred[]{:T(512)S(6)} %eq.6, bf16[3,1,128,128]{3,2,1,0:T(8,128)(2,1)} %param.6, bf16[1,3,128,128]{3,2,1,0:T(8,128)(2,1)S(1)} %collective-permute-done.4), kind=kLoop, calls=%fused_computation.4 | loop fusion | flops 98304 | bytes 491521 | tf_op jit(solution)/shard_map/jit(_where)/select_n | solution.py:216
  9.6 4.2 %collective-permute-start.5 = (bf16[2,3,128,128]{3,2,1,0:T(8,128)(2,1)S(1)}, bf16[2,3,128,128]{3,2,1,0:T(8,128)(2,1)S(1)}, u32[]{:S(2)}, u32[]{:S(2)}) collective-permute-start(bf16[2,3,128,128]{3,2,1,0:T(8,128)(2,1)S(1)} %pad_maximum_fusion.own), channel_id=1, source_target_pairs={{0,2},{1,3},{2,0},{3,1},{4,6},{5,7},{6,4},{7,5},{8,10},{9,11},{10,... | collective-permute-start | bytes 589832 | tf_op jit(solution)/shard_map/ppermute | solution.py:32
  13.8 1.2 %collective-permute-start.6 = (bf16[2,3,128,128]{3,2,1,0:T(8,128)(2,1)S(1)}, bf16[2,3,128,128]{3,2,1,0:T(8,128)(2,1)S(1)}, u32[]{:S(2)}, u32[]{:S(2)}) collective-permute-start(bf16[2,3,128,128]{3,2,1,0:T(8,128)(2,1)S(1)} %pad_maximum_fusion.own), channel_id=1, source_target_pairs={{0,1},{1,0},{2,3},{3,2},{4,5},{5,4},{6,7},{7,6},{8,9},{9,8},{10,11... | collective-permute-start | bytes 589832 | tf_op jit(solution)/shard_map/ppermute | solution.py:32
  15.0 1.5 %collective-permute-start.1 = (bf16[3,272,256]{2,1,0:T(8,128)(2,1)S(1)}, bf16[3,272,256]{2,1,0:T(8,128)(2,1)S(1)}, u32[]{:S(2)}, u32[]{:S(2)}) collective-permute-start(bf16[3,272,256]{2,1,0:T(8,128)(2,1)S(1)} %get-tuple-element.21.refs_0_), channel_id=1, source_target_pairs={{0,8},{8,0},{16,24},{24,16},{1,9},{9,1},{17,25},{25,17},{2,10},{10... | collective-permute-start | bytes 1253384 | tf_op jit(solution)/shard_map/ppermute | solution.py:28
  16.5 2.6 %collective-permute-done.refs_1_ = bf16[3,272,256]{2,1,0:T(8,128)(2,1)S(1)} collective-permute-done((bf16[3,272,256]{2,1,0:T(8,128)(2,1)S(1)}, bf16[3,272,256]{2,1,0:T(8,128)(2,1)S(1)}, u32[]{:S(2)}, u32[]{:S(2)}) %collective-permute-start) | collective-permute-done | bytes 417824 | tf_op jit(solution)/shard_map/ppermute | solution.py:28
  19.2 0.4 collective-permute-start.2
  19.6 0.0 collective-permute-done.5.other
  19.6 0.0 collective-permute-done.6.own
  19.7 1.5 %collective-permute-start.7 = (bf16[2,3,128,128]{3,2,1,0:T(8,128)(2,1)S(1)}, bf16[2,3,128,128]{3,2,1,0:T(8,128)(2,1)S(1)}, u32[]{:S(2)}, u32[]{:S(2)}) collective-permute-start(bf16[2,3,128,128]{3,2,1,0:T(8,128)(2,1)S(1)} %broadcast_select_fusion.1), channel_id=1, source_target_pairs={{0,8},{8,0},{16,24},{24,16},{1,9},{9,1},{17,25},{25,17},{2,10},{10... | collective-permute-start | bytes 589832 | tf_op jit(solution)/shard_map/ppermute | solution.py:28
  21.2 0.7 %collective-permute-start.10 = (bf16[2,3,128,128]{3,2,1,0:T(8,128)(2,1)S(1)}, bf16[2,3,128,128]{3,2,1,0:T(8,128)(2,1)S(1)}, u32[]{:S(2)}, u32[]{:S(2)}) collective-permute-start(bf16[2,3,128,128]{3,2,1,0:T(8,128)(2,1)S(1)} %collective-permute-done.6.own), channel_id=1, source_target_pairs={{0,2},{1,3},{2,0},{3,1},{4,6},{5,7},{6,4},{7,5},{8,10},{9,11},{10,... | collective-permute-start | bytes 589832 | tf_op jit(solution)/shard_map/ppermute | solution.py:32
  21.9 0.0 collective-permute-done.2.refs_3_
  21.9 1.9 %left_products.1 = (bf16[2,3,256,1536]{3,2,1,0:T(8,128)(2,1)S(1)}, s32[12]{0:T(128)S(1)}) custom-call(bf16[3,272,256]{2,1,0:T(8,128)(2,1)S(1)} %get-tuple-element.21.refs_0_, bf16[3,272,256]{2,1,0:T(8,128)(2,1)S(1)} %collective-permute-done.refs_1_, bf16[3,272,256]{2,1,0:T(8,128)(2,1)S(1)} %collective-permute-done.1.refs_2_, ...), custom_call_target="tpu_custom_call" | custom-call | flops 1207959552 | bytes 1048576 | tf_op jit(solution)/shard_map/left_products/pallas_call | solution.py:118
  23.8 2.0 %right_products.2 = (f32[3,256,128]{2,1,0:T(8,128)S(1)}, bf16[3,256,128]{2,1,0:T(8,128)(2,1)S(1)}, bf16[3,256,128]{2,1,0:T(8,128)(2,1)S(1)}) custom-call(s32[3]{0:T(128)S(1)} %pad_add_fusion.place, s32[12]{0:T(128)S(1)} %get-tuple-element.23.shift, bf16[2,3,256,1536]{3,2,1,0:T(8,128)(2,1)S(1)} %get-tuple-element.24.z_ref, ...), custom_call_target="tpu_custom_call" | custom-call | tf_op jit(solution)/shard_map/right_products/pallas_call | solution.py:156
  25.8 1.9 %collective-permute-done.10.other = bf16[2,3,128,128]{3,2,1,0:T(8,128)(2,1)S(1)} collective-permute-done((bf16[2,3,128,128]{3,2,1,0:T(8,128)(2,1)S(1)}, bf16[2,3,128,128]{3,2,1,0:T(8,128)(2,1)S(1)}, u32[]{:S(2)}, u32[]{:S(2)}) %collective-permute-start.10) | collective-permute-done | bytes 196640 | tf_op jit(solution)/shard_map/ppermute | solution.py:32
  27.7 0.9 %collective-permute-start.11 = (bf16[2,3,128,128]{3,2,1,0:T(8,128)(2,1)S(1)}, bf16[2,3,128,128]{3,2,1,0:T(8,128)(2,1)S(1)}, u32[]{:S(2)}, u32[]{:S(2)}) collective-permute-start(bf16[2,3,128,128]{3,2,1,0:T(8,128)(2,1)S(1)} %broadcast_select_fusion), channel_id=1, source_target_pairs={{0,8},{8,0},{16,24},{24,16},{1,9},{9,1},{17,25},{25,17},{2,10},{10... | collective-permute-start | bytes 589832 | tf_op jit(solution)/shard_map/ppermute | solution.py:28
  28.6 3.1 %collective-permute-start.8 = (bf16[3,256,128]{2,1,0:T(8,128)(2,1)S(1)}, bf16[3,256,128]{2,1,0:T(8,128)(2,1)S(1)}, u32[]{:S(2)}, u32[]{:S(2)}) collective-permute-start(bf16[3,256,128]{2,1,0:T(8,128)(2,1)S(1)} %get-tuple-element.30), channel_id=1, source_target_pairs={{0,1},{1,2},{2,3},{3,4},{4,5},{5,6},{6,7},{8,9},{9,10},{10,11},{11... | collective-permute-start | bytes 589832 | tf_op jit(solution)/shard_map/ppermute | solution.py:235
  31.8 3.0 %collective-permute-start.9 = (bf16[3,256,128]{2,1,0:T(8,128)(2,1)S(1)}, bf16[3,256,128]{2,1,0:T(8,128)(2,1)S(1)}, u32[]{:S(2)}, u32[]{:S(2)}) collective-permute-start(bf16[3,256,128]{2,1,0:T(8,128)(2,1)S(1)} %get-tuple-element.31), channel_id=1, source_target_pairs={{1,0},{2,1},{3,2},{4,3},{5,4},{6,5},{7,6},{9,8},{10,9},{11,10},{12... | collective-permute-start | bytes 589832 | tf_op jit(solution)/shard_map/ppermute | solution.py:235
  34.8 2.0 %right_products.3 = (f32[3,256,128]{2,1,0:T(8,128)S(1)}, bf16[3,256,128]{2,1,0:T(8,128)(2,1)S(1)}, bf16[3,256,128]{2,1,0:T(8,128)(2,1)S(1)}) custom-call(s32[3]{0:T(128)S(1)} %pad_add_fusion.place, s32[12]{0:T(128)S(1)} %get-tuple-element.23.shift, bf16[2,3,256,1536]{3,2,1,0:T(8,128)(2,1)S(1)} %get-tuple-element.24.z_ref, ...), custom_call_target="tpu_custom_call" | custom-call | tf_op jit(solution)/shard_map/right_products/pallas_call | solution.py:156
  36.9 2.2 %collective-permute-start.12 = (bf16[3,256,128]{2,1,0:T(8,128)(2,1)S(1)}, bf16[3,256,128]{2,1,0:T(8,128)(2,1)S(1)}, u32[]{:S(2)}, u32[]{:S(2)}) collective-permute-start(bf16[3,256,128]{2,1,0:T(8,128)(2,1)S(1)} %get-tuple-element.35), channel_id=1, source_target_pairs={{0,1},{1,2},{2,3},{3,4},{4,5},{5,6},{6,7},{8,9},{9,10},{10,11},{11... | collective-permute-start | bytes 589832 | tf_op jit(solution)/shard_map/ppermute | solution.py:235
  39.1 3.9 %collective-permute-start.13 = (bf16[3,256,128]{2,1,0:T(8,128)(2,1)S(1)}, bf16[3,256,128]{2,1,0:T(8,128)(2,1)S(1)}, u32[]{:S(2)}, u32[]{:S(2)}) collective-permute-start(bf16[3,256,128]{2,1,0:T(8,128)(2,1)S(1)} %get-tuple-element.36), channel_id=1, source_target_pairs={{1,0},{2,1},{3,2},{4,3},{5,4},{6,5},{7,6},{9,8},{10,9},{11,10},{12... | collective-permute-start | bytes 589832 | tf_op jit(solution)/shard_map/ppermute | solution.py:235
  43.1 3.6 %collective-permute-done.9.refs_2_ = bf16[3,256,128]{2,1,0:T(8,128)(2,1)S(1)} collective-permute-done((bf16[3,256,128]{2,1,0:T(8,128)(2,1)S(1)}, bf16[3,256,128]{2,1,0:T(8,128)(2,1)S(1)}, u32[]{:S(2)}, u32[]{:S(2)}) %collective-permute-start.9) | collective-permute-done | bytes 196640 | tf_op jit(solution)/shard_map/ppermute | solution.py:235
  46.7 1.9 %collective-permute-done.12.refs_4_ = bf16[3,256,128]{2,1,0:T(8,128)(2,1)S(1)} collective-permute-done((bf16[3,256,128]{2,1,0:T(8,128)(2,1)S(1)}, bf16[3,256,128]{2,1,0:T(8,128)(2,1)S(1)}, u32[]{:S(2)}, u32[]{:S(2)}) %collective-permute-start.12) | collective-permute-done | bytes 196640 | tf_op jit(solution)/shard_map/ppermute | solution.py:235
  48.6 2.3 %collective-permute-done.13.refs_5_ = bf16[3,256,128]{2,1,0:T(8,128)(2,1)S(1)} collective-permute-done((bf16[3,256,128]{2,1,0:T(8,128)(2,1)S(1)}, bf16[3,256,128]{2,1,0:T(8,128)(2,1)S(1)}, u32[]{:S(2)}, u32[]{:S(2)}) %collective-permute-start.13) | collective-permute-done | bytes 196640 | tf_op jit(solution)/shard_map/ppermute | solution.py:235
  50.9 1.4 %summed.1 = bf16[3,256,256]{2,1,0:T(8,128)(2,1)} custom-call(s32[3]{0:T(128)S(1)} %pad_add_fusion.place, f32[3,256,128]{2,1,0:T(8,128)S(1)} %get-tuple-element.29.refs_0_, bf16[3,256,128]{2,1,0:T(8,128)(2,1)S(1)} %collective-permute-done.8.refs_1_, bf16[3,256,128]{2,1,0:T(8,128)(2,1)S(1)} %collective-permute-done.9.refs_2_, ...), custom_call_target="tpu_custom_call" | custom-call | tf_op jit(solution)/shard_map/summed/pallas_call | solution.py:193
  (8 shorter events, 0.1 us)
Async XLA Ops:
  0.0 6.7 %collective-permute-start.3 = (bf16[1,3,128,128]{3,2,1,0:T(8,128)(2,1)}, bf16[1,3,128,128]{3,2,1,0:T(8,128)(2,1)S(1)}, u32[]{:S(2)}, u32[]{:S(2)}) collective-permute-start(bf16[1,3,128,128]{3,2,1,0:T(8,128)(2,1)} %bitcast.10), channel_id=1, source_target_pairs={{0,4},{1,5},{2,6},{3,7},{4,20},{5,21},{6,22},{7,23},{8,12},{9,13},... | collective-permute-start | bytes 294920 | tf_op jit(solution)/shard_map/ppermute | solution.py:46
  1.2 7.5 %collective-permute-start.4 = (bf16[1,3,128,128]{3,2,1,0:T(8,128)(2,1)}, bf16[1,3,128,128]{3,2,1,0:T(8,128)(2,1)S(1)}, u32[]{:S(2)}, u32[]{:S(2)}) collective-permute-start(bf16[1,3,128,128]{3,2,1,0:T(8,128)(2,1)} %bitcast.11), channel_id=1, source_target_pairs={{4,16},{5,17},{6,18},{7,19},{12,24},{13,25},{14,26},{15,27},{16,4}... | collective-permute-start | bytes 294920 | tf_op jit(solution)/shard_map/ppermute | solution.py:46
  3.2 0.7 %copy-start = (s32[3]{0:T(128)S(1)}, s32[3]{0:T(128)}, u32[]{:S(2)}) copy-start(s32[3]{0:T(128)} %shift.1) | copy-start | bytes 40
  6.6 12.6 %collective-permute-start = (bf16[3,272,256]{2,1,0:T(8,128)(2,1)S(1)}, bf16[3,272,256]{2,1,0:T(8,128)(2,1)S(1)}, u32[]{:S(2)}, u32[]{:S(2)}) collective-permute-start(bf16[3,272,256]{2,1,0:T(8,128)(2,1)S(1)} %get-tuple-element.21.refs_0_), channel_id=1, source_target_pairs={{0,16},{8,24},{16,0},{24,8},{1,17},{9,25},{17,1},{25,9},{2,18},{10... | collective-permute-start | bytes 1253384 | tf_op jit(solution)/shard_map/ppermute | solution.py:28
  9.6 10.0 %collective-permute-start.5 = (bf16[2,3,128,128]{3,2,1,0:T(8,128)(2,1)S(1)}, bf16[2,3,128,128]{3,2,1,0:T(8,128)(2,1)S(1)}, u32[]{:S(2)}, u32[]{:S(2)}) collective-permute-start(bf16[2,3,128,128]{3,2,1,0:T(8,128)(2,1)S(1)} %pad_maximum_fusion.own), channel_id=1, source_target_pairs={{0,2},{1,3},{2,0},{3,1},{4,6},{5,7},{6,4},{7,5},{8,10},{9,11},{10,... | collective-permute-start | bytes 589832 | tf_op jit(solution)/shard_map/ppermute | solution.py:32
  13.8 5.8 %collective-permute-start.6 = (bf16[2,3,128,128]{3,2,1,0:T(8,128)(2,1)S(1)}, bf16[2,3,128,128]{3,2,1,0:T(8,128)(2,1)S(1)}, u32[]{:S(2)}, u32[]{:S(2)}) collective-permute-start(bf16[2,3,128,128]{3,2,1,0:T(8,128)(2,1)S(1)} %pad_maximum_fusion.own), channel_id=1, source_target_pairs={{0,1},{1,0},{2,3},{3,2},{4,5},{5,4},{6,7},{7,6},{8,9},{9,8},{10,11... | collective-permute-start | bytes 589832 | tf_op jit(solution)/shard_map/ppermute | solution.py:32
  15.0 6.9 %collective-permute-start.1 = (bf16[3,272,256]{2,1,0:T(8,128)(2,1)S(1)}, bf16[3,272,256]{2,1,0:T(8,128)(2,1)S(1)}, u32[]{:S(2)}, u32[]{:S(2)}) collective-permute-start(bf16[3,272,256]{2,1,0:T(8,128)(2,1)S(1)} %get-tuple-element.21.refs_0_), channel_id=1, source_target_pairs={{0,8},{8,0},{16,24},{24,16},{1,9},{9,1},{17,25},{25,17},{2,10},{10... | collective-permute-start | bytes 1253384 | tf_op jit(solution)/shard_map/ppermute | solution.py:28
  19.2 2.7 %collective-permute-start.2 = (bf16[3,272,256]{2,1,0:T(8,128)(2,1)S(1)}, bf16[3,272,256]{2,1,0:T(8,128)(2,1)S(1)}, u32[]{:S(2)}, u32[]{:S(2)}) collective-permute-start(bf16[3,272,256]{2,1,0:T(8,128)(2,1)S(1)} %collective-permute-done.refs_1_), channel_id=1, source_target_pairs={{0,8},{8,0},{16,24},{24,16},{1,9},{9,1},{17,25},{25,17},{2,10},{10... | collective-permute-start | bytes 1253384 | tf_op jit(solution)/shard_map/ppermute | solution.py:28
  19.7 4.1 %collective-permute-start.7 = (bf16[2,3,128,128]{3,2,1,0:T(8,128)(2,1)S(1)}, bf16[2,3,128,128]{3,2,1,0:T(8,128)(2,1)S(1)}, u32[]{:S(2)}, u32[]{:S(2)}) collective-permute-start(bf16[2,3,128,128]{3,2,1,0:T(8,128)(2,1)S(1)} %broadcast_select_fusion.1), channel_id=1, source_target_pairs={{0,8},{8,0},{16,24},{24,16},{1,9},{9,1},{17,25},{25,17},{2,10},{10... | collective-permute-start | bytes 589832 | tf_op jit(solution)/shard_map/ppermute | solution.py:28
  21.2 6.5 %collective-permute-start.10 = (bf16[2,3,128,128]{3,2,1,0:T(8,128)(2,1)S(1)}, bf16[2,3,128,128]{3,2,1,0:T(8,128)(2,1)S(1)}, u32[]{:S(2)}, u32[]{:S(2)}) collective-permute-start(bf16[2,3,128,128]{3,2,1,0:T(8,128)(2,1)S(1)} %collective-permute-done.6.own), channel_id=1, source_target_pairs={{0,2},{1,3},{2,0},{3,1},{4,6},{5,7},{6,4},{7,5},{8,10},{9,11},{10,... | collective-permute-start | bytes 589832 | tf_op jit(solution)/shard_map/ppermute | solution.py:32
  27.7 7.1 %collective-permute-start.11 = (bf16[2,3,128,128]{3,2,1,0:T(8,128)(2,1)S(1)}, bf16[2,3,128,128]{3,2,1,0:T(8,128)(2,1)S(1)}, u32[]{:S(2)}, u32[]{:S(2)}) collective-permute-start(bf16[2,3,128,128]{3,2,1,0:T(8,128)(2,1)S(1)} %broadcast_select_fusion), channel_id=1, source_target_pairs={{0,8},{8,0},{16,24},{24,16},{1,9},{9,1},{17,25},{25,17},{2,10},{10... | collective-permute-start | bytes 589832 | tf_op jit(solution)/shard_map/ppermute | solution.py:28
  28.6 14.4 %collective-permute-start.8 = (bf16[3,256,128]{2,1,0:T(8,128)(2,1)S(1)}, bf16[3,256,128]{2,1,0:T(8,128)(2,1)S(1)}, u32[]{:S(2)}, u32[]{:S(2)}) collective-permute-start(bf16[3,256,128]{2,1,0:T(8,128)(2,1)S(1)} %get-tuple-element.30), channel_id=1, source_target_pairs={{0,1},{1,2},{2,3},{3,4},{4,5},{5,6},{6,7},{8,9},{9,10},{10,11},{11... | collective-permute-start | bytes 589832 | tf_op jit(solution)/shard_map/ppermute | solution.py:235
  31.8 14.9 %collective-permute-start.9 = (bf16[3,256,128]{2,1,0:T(8,128)(2,1)S(1)}, bf16[3,256,128]{2,1,0:T(8,128)(2,1)S(1)}, u32[]{:S(2)}, u32[]{:S(2)}) collective-permute-start(bf16[3,256,128]{2,1,0:T(8,128)(2,1)S(1)} %get-tuple-element.31), channel_id=1, source_target_pairs={{1,0},{2,1},{3,2},{4,3},{5,4},{6,5},{7,6},{9,8},{10,9},{11,10},{12... | collective-permute-start | bytes 589832 | tf_op jit(solution)/shard_map/ppermute | solution.py:235
  36.9 11.7 %collective-permute-start.12 = (bf16[3,256,128]{2,1,0:T(8,128)(2,1)S(1)}, bf16[3,256,128]{2,1,0:T(8,128)(2,1)S(1)}, u32[]{:S(2)}, u32[]{:S(2)}) collective-permute-start(bf16[3,256,128]{2,1,0:T(8,128)(2,1)S(1)} %get-tuple-element.35), channel_id=1, source_target_pairs={{0,1},{1,2},{2,3},{3,4},{4,5},{5,6},{6,7},{8,9},{9,10},{10,11},{11... | collective-permute-start | bytes 589832 | tf_op jit(solution)/shard_map/ppermute | solution.py:235
  39.1 11.8 %collective-permute-start.13 = (bf16[3,256,128]{2,1,0:T(8,128)(2,1)S(1)}, bf16[3,256,128]{2,1,0:T(8,128)(2,1)S(1)}, u32[]{:S(2)}, u32[]{:S(2)}) collective-permute-start(bf16[3,256,128]{2,1,0:T(8,128)(2,1)S(1)} %get-tuple-element.36), channel_id=1, source_target_pairs={{1,0},{2,1},{3,2},{4,3},{5,4},{6,5},{7,6},{9,8},{10,9},{11,10},{12... | collective-permute-start | bytes 589832 | tf_op jit(solution)/shard_map/ppermute | solution.py:235

commit v3 on v2

v3 whole, which is shorter than its diff:
```python
import functools

import jax
import jax.numpy as jnp
from jax import lax
from jax.experimental import pallas as pl
from jax.experimental.pallas import tpu as pltpu
from jax.sharding import PartitionSpec as P

ML = 256
MR = 128
VECS = 3
TILE = 16
VMEM = pl.BlockSpec(memory_space=pltpu.VMEM)
HBM = pl.BlockSpec(memory_space=pltpu.HBM)


def in_vmem(shape, dtype=jnp.bfloat16):
    return pltpu.VMEM(shape, dtype)


def in_hbm(x):
    return pltpu.with_memory_space_constraint(x, pltpu.HBM)


def grant(mebibytes):
    return pltpu.CompilerParams(vmem_limit_bytes=mebibytes * 1024 * 1024)


def cost(flops, bytes_accessed):
    return pl.CostEstimate(flops=flops, bytes_accessed=bytes_accessed, transcendentals=0)


def over_op(x, n_op, bit):
    return lax.ppermute(x, "op", [(o, o ^ bit) for o in range(n_op)])


def over_sec(x, n_sec, bit):
    return lax.ppermute(x, "sec", [(d, d ^ bit) for d in range(n_sec)])


def on_own_side(per, bit):
    return ((lax.axis_index("op") ^ (lax.axis_index("sec") // per)) & bit) == 0


def towards_owner(held, n_op, n_sec, bit):
    per = n_sec // n_op
    first, second = [], []
    for o in range(n_op):
        for d in range(n_sec):
            source = o * n_sec + d
            far = d ^ (bit * per)
            if (o & bit) == ((d // per) & bit):
                first.append((source, o * n_sec + far))
            else:
                first.append((source, (o ^ bit) * n_sec + d))
                second.append((source, (o ^ bit) * n_sec + far))
    return lax.ppermute(held, ("op", "sec"), first), lax.ppermute(held, ("op", "sec"), second)


def route_kernel(per, bit, held, one, two, out_ref):
    half = held.shape[0]
    own = on_own_side(per, bit)
    out_ref[:half] = jnp.where(own, held[...], one[...])
    out_ref[half:] = jnp.where(own, one[...], two[...])


def route(held, one, two, per, bit):
    return pl.pallas_call(
        functools.partial(route_kernel, per, bit),
        out_shape=in_vmem((2 * held.shape[0],) + held.shape[1:]),
        in_specs=[VMEM] * 3,
        out_specs=VMEM,
        compiler_params=grant(4),
        cost_estimate=cost(0, 0),
        name="route",
    )(held, one, two)


def pick_kernel(per, own, other, out_ref):
    out_ref[...] = jnp.where(on_own_side(per, 1), other[...], own[...])


def pick(own, other, per):
    return pl.pallas_call(
        functools.partial(pick_kernel, per),
        out_shape=in_vmem(own.shape),
        in_specs=[VMEM] * 2,
        out_specs=VMEM,
        compiler_params=grant(4),
        cost_estimate=cost(0, 0),
        name="pick",
    )(own, other)


def shift_of(left, inner):
    return jnp.max(left[inner, ML:, :MR].astype(jnp.float32)).astype(jnp.int32)


def pack_kernel(n_op, shift, left, wave, packed, window, shift_ref, sems):
    width = window.shape[2] - 2 * MR
    op = lax.axis_index("op")
    start = pl.multiple_of(op * width, MR)
    copies = [
        pltpu.make_async_copy(shift, shift_ref, sems.at[0]),
        pltpu.make_async_copy(left, packed.at[:, pl.ds(0, ML)], sems.at[1]),
        pltpu.make_async_copy(wave.at[:, :, pl.ds(start, width)], window.at[:, :, pl.ds(MR, width)], sems.at[2]),
    ]
    for copy in copies:
        copy.start()

    def edge(valid, source, target, sem):
        @pl.when(valid)
        def _():
            copy = pltpu.make_async_copy(
                wave.at[:, :, pl.ds(pl.multiple_of(source, MR), MR)], window.at[:, :, pl.ds(target, MR)], sem
            )
            copy.start()
            copy.wait()

        @pl.when(jnp.logical_not(valid))
        def _():
            window[:, :, pl.ds(target, MR)] = jnp.zeros((VECS, ML, MR), jnp.bfloat16)

    edge(op > 0, start - MR, 0, sems.at[3])
    edge(op < n_op - 1, start + width, MR + width, sems.at[4])
    copies[0].wait()
    for inner in range(left.shape[0]):
        tag = jnp.full((TILE, ML), shift_ref[inner].astype(jnp.float32)).astype(jnp.bfloat16)
        packed[inner, ML:] = tag
    copies[1].wait()
    copies[2].wait()


def pack(shift, left, wave, n_op):
    width = wave.shape[2] // n_op
    return pl.pallas_call(
        functools.partial(pack_kernel, n_op),
        out_shape=[in_vmem((left.shape[0], ML + TILE, ML)), in_vmem((VECS, ML, width + 2 * MR))],
        in_specs=[HBM] * 3,
        out_specs=[VMEM] * 2,
        scratch_shapes=[pltpu.SMEM(shift.shape, jnp.int32), pltpu.SemaphoreType.DMA((5,))],
        compiler_params=grant(8),
        cost_estimate=cost(0, 32 * 1024 * 1024),
        name="pack",
    )(in_hbm(shift), in_hbm(left), in_hbm(wave))


def left_kernel(*refs):
    *lefts, window, z_ref = refs
    per = z_ref.shape[0]
    width = per * MR
    terms = lefts[0].shape[0]
    for piece, left in enumerate(lefts):
        for inner in range(terms):
            term = piece * terms + inner
            offset = pl.multiple_of((1 + shift_of(left, inner)) * MR, MR)
            for v in range(VECS):
                z = jnp.dot(
                    left[inner, :ML], window[v, :, pl.ds(offset, width)], preferred_element_type=jnp.float32
                ).astype(jnp.bfloat16)
                for column in range(per):
                    z_ref[column, v, :, term * MR : (term + 1) * MR] = z[:, column * MR : (column + 1) * MR]


def left_products(lefts, window):
    terms = len(lefts) * lefts[0].shape[0]
    width = window.shape[2] - 2 * MR
    return pl.pallas_call(
        left_kernel,
        out_shape=in_vmem((width // MR, VECS, ML, terms * MR)),
        in_specs=[VMEM] * (len(lefts) + 1),
        out_specs=VMEM,
        compiler_params=grant(8 + 4 * width // MR),
        cost_estimate=cost(2 * terms * VECS * ML * ML * width, 1024 * 1024),
        name="left_products",
    )(*lefts, window)


def right_kernel(cls, per, z_ref, own, other, received, *refs):
    *lefts, zero_ref, low_ref, high_ref, total = refs
    sec = lax.axis_index("sec")
    column = (sec % per) ^ cls
    even = sec % 2 == 0
    settled = on_own_side(per, 1)
    half, terms = own.shape[0], own.shape[1]
    total[...] = jnp.zeros_like(total)
    for piece, left in enumerate(lefts):
        for inner in range(terms):
            term = piece * terms + inner
            kind = 1 + shift_of(left, inner)
            if piece < half:
                block = jnp.where(settled, own[piece, inner], other[piece, inner])
            else:
                block = received[piece - half, inner]
            for v in range(VECS):
                total[kind, v] += jnp.dot(
                    z_ref[column, v, :, term * MR : (term + 1) * MR], block, preferred_element_type=jnp.float32
                )
    for v in range(VECS):
        down, up = total[0, v].astype(jnp.bfloat16), total[2, v].astype(jnp.bfloat16)
        zero_ref[v] = total[1, v]
        low_ref[v] = jnp.where(even, up, down)
        high_ref[v] = jnp.where(even, down, up)


def right_products(cls, per, z, own, other, received, lefts):
    block = (VECS, ML, MR)
    return pl.pallas_call(
        functools.partial(right_kernel, cls, per),
        out_shape=[jax.ShapeDtypeStruct(block, dtype) for dtype in (jnp.float32, jnp.bfloat16, jnp.bfloat16)],
        in_specs=[VMEM] * (4 + len(lefts)),
        out_specs=[VMEM] * 3,
        scratch_shapes=[in_vmem((3,) + block, jnp.float32)],
        compiler_params=grant(8),
        cost_estimate=cost(0, 0),
        name="right_products",
    )(z, own, other, received, *lefts)


def sum_kernel(per, *refs):
    *parts, out_ref = refs
    zeros, lows, highs = parts[::3], parts[1::3], parts[2::3]
    sec = lax.axis_index("sec")
    beyond = (sec ^ ((((sec + 1) ^ 1) + per - 1) % per)) % per

    def add(high):
        @pl.when(beyond == high)
        def _():
            for cls in range(per):
                column = pl.multiple_of(((sec % per) ^ cls) * MR, MR)
                for v in range(VECS):
                    total = zeros[cls][v] + lows[cls ^ 1][v].astype(jnp.float32)
                    total = total + highs[cls ^ high][v].astype(jnp.float32)
                    out_ref[v, :, pl.ds(column, MR)] = total.astype(jnp.bfloat16)

    carry = 1
    while carry < per:
        add(carry)
        carry = 2 * carry + 1


def summed(per, parts):
    return pl.pallas_call(
        functools.partial(sum_kernel, per),
        out_shape=jax.ShapeDtypeStruct((VECS, ML, per * MR), jnp.bfloat16),
        in_specs=[VMEM] * len(parts),
        out_specs=VMEM,
        compiler_params=grant(8),
        name="summed",
    )(*parts)


def on_device(n_op, n_sec, wavefunction, left_ops, right_ops, term_shift):
    per = n_sec // n_op
    tie = lax.optimization_barrier
    matching = lax.axis_index("op") ^ (lax.axis_index("sec") // per)
    held = right_ops.reshape((1,) + right_ops.shape[:1] + right_ops.shape[2:])
    packed, window = pack(term_shift, left_ops.transpose(1, 0, 2), wavefunction.transpose(1, 0, 2), n_op)
    lefts = [packed]
    bit = n_op // 2
    while bit > 1:
        one, two = tie(towards_owner(held, n_op, n_sec, bit))
        same = (matching & bit) == 0
        held = jnp.concatenate([jnp.where(same, held, one), jnp.where(same, one, two)])
        lefts = lefts + [over_op(x, n_op, bit) for x in lefts]
        bit //= 2
    lefts = lefts + [over_op(x, n_op, 1) for x in lefts]
    owns = [held]
    bit = 1
    while bit < per:
        owns = owns + [over_sec(c, n_sec, bit) for c in owns]
        bit *= 2
    other, owns = tie((over_sec(owns[0], n_sec, per), owns))
    z = left_products(lefts, window)
    low = [(d, d ^ 1) for d in range(n_sec)]
    high = [(d, ((d + 1) ^ 1) - 1) for d in range(1, n_sec - 1)]
    settled = (matching & 1) == 0
    parts = []
    for cls, own in enumerate(owns):
        received = over_op(jnp.where(settled, other, own), n_op, 1)
        later = over_sec(owns[cls + 1], n_sec, per) if cls + 1 < per else None
        zero, to_low, to_high = right_products(cls, per, z, own, other, received, lefts)
        parts += [zero, lax.ppermute(to_low, "sec", low), lax.ppermute(to_high, "sec", high)]
        if later is not None:
            other, _ = tie((later, zero))
    return summed(per, parts).transpose(1, 0, 2)


def solution(mesh):
    in_specs = (P("sec", None, None), P("sec", "op", None), P("op", "sec", None, None), P("op"))
    out_specs = P("sec", None, "op")
    return jax.shard_map(
        functools.partial(on_device, mesh.shape["op"], mesh.shape["sec"]),
        mesh=mesh,
        in_specs=in_specs,
        out_specs=out_specs,
        check_vma=False,
    )
```

time: 52.6 us -> 48.1 us (0.914)
  Pallas kernels: 9.99 us -> 6.58 us
  starting transfers between devices: 26.1 us -> 24.4 us
  waiting for transfers between devices: 14.4 us -> 15.4 us
  local copies, waits for them, and re-layouts: 0.66 us -> 0 us
    ppermute x6, starting transfers between devices: 15.5 us -> 10.1 us  [the longest x2 4.18 us: on_device(): lax.ppermute(to_high, 'sec', high)]
    ppermute x5, starting transfers between devices: 4.47 us -> 7.48 us  [over_op(): return lax.ppermute(x, 'op', [(o, o ^ bit) for o in range(n_op)])]
    ppermute x6, waiting for transfers between devices: 9.86 us -> 12 us  [the longest x2 11 us: on_device(): lax.ppermute(to_low, 'sec', low)]
    pallas_call x2, Pallas kernels: 4.03 us -> 1.93 us  [right_products(): pl.pallas_call(functools.partial(right_kernel, cls, per), out_shape=[jax....]
    ppermute x5, waiting for transfers between devices: 2.66 us -> 0.75 us  [over_op(): return lax.ppermute(x, 'op', [(o, o ^ bit) for o in range(n_op)])]
    ppermute x3, waiting for transfers between devices: 1.87 us -> 2.71 us  [over_sec(): return lax.ppermute(x, 'sec', [(d, d ^ bit) for d in range(n_sec)])]
    ppermute x3, starting transfers between devices: 6.14 us -> 6.87 us  [over_sec(): return lax.ppermute(x, 'sec', [(d, d ^ bit) for d in range(n_sec)])]
    unnamed x2 -> x0, local copies, waits for them, and re-layouts: 0.66 us -> none
  transfers between devices with their start and end apart: 14 -> 14, of which waited for: 6 -> 7; matrix products, arithmetic and copies ran while one was open for 2% -> 2% of each run, Pallas kernels for 16% -> 12%
where the time goes in v3:
time: 48.1 us; the launch traced here: 47.5 us
  starting transfers between devices  24.4 us (51%)
  waiting for transfers between devices  15.4 us (32%)
  Pallas kernels  6.58 us (14%)
  other arithmetic  0.98 us (2%)
    ppermute x2, waiting for transfers between devices, on_device(): lax.ppermute(to_low, 'sec', low)  11 us
    ppermute x5, starting transfers between devices, over_op(): return lax.ppermute(x, 'op', [(o, o ^ bit) for o in range(n_op)])  7.48 us
    ppermute x3, starting transfers between devices, over_sec(): return lax.ppermute(x, 'sec', [(d, d ^ bit) for d in range(n_sec)])  6.87 us
    ppermute x2, starting transfers between devices, on_device(): lax.ppermute(to_high, 'sec', high)  4.18 us
    ppermute x2, starting transfers between devices, on_device(): lax.ppermute(to_low, 'sec', low)  2.93 us
    ppermute x1, starting transfers between devices, towards_owner(): lax.ppermute(held, ('op', 'sec'), second)  2.88 us
    ppermute x3, waiting for transfers between devices, over_sec(): return lax.ppermute(x, 'sec', [(d, d ^ bit) for d in range(n_sec)])  2.71 us
    pallas_call x1, Pallas kernels, pack(): pl.pallas_call(functools.partial(pack_kernel, n_op), out_shape=[in_vmem((...  2.16 us
  transfers between devices with their start and end apart: 14, of which 7 were waited for; matrix products, arithmetic and copies ran while one was open for 2% of the time, Pallas kernels for 12%

profile of v3, /device:TPU:17, one launch (start us, length us, event | category | flops | bytes accessed | tf_op | source)
XLA Modules:
  0.0 47.5 jit_solution(13661381800435164991)
XLA Ops:
  0.0 2.9 %collective-permute-start.4 = (bf16[1,3,128,128]{3,2,1,0:T(8,128)(2,1)}, bf16[1,3,128,128]{3,2,1,0:T(8,128)(2,1)S(1)}, u32[]{:S(2)}, u32[]{:S(2)}) collective-permute-start(bf16[1,3,128,128]{3,2,1,0:T(8,128)(2,1)} %bitcast.7), channel_id=1, source_target_pairs={{4,16},{5,17},{6,18},{7,19},{12,24},{13,25},{14,26},{15,27},{16,4}... | collective-permute-start | bytes 294920 | tf_op jit(solution)/shard_map/ppermute | solution.py:58
  2.9 0.1 collective-permute-start.3
  3.0 2.2 %pack.1 = (bf16[3,272,256]{2,1,0:T(8,128)(2,1)S(1)}, bf16[3,256,512]{2,1,0:T(8,128)(2,1)S(1)}) custom-call(s32[3]{0:T(128)} %shift.1, bf16[3,256,256]{2,1,0:T(8,128)(2,1)} %bitcast.6, bf16[3,256,1024]{2,1,0:T(8,128)(2,1)} %bitcast.5), custom_call_target="tpu_custom_call" | custom-call | bytes 33554432 | tf_op jit(solution)/shard_map/pack/pallas_call | solution.py:137
  5.1 1.7 %collective-permute-start = (bf16[3,272,256]{2,1,0:T(8,128)(2,1)S(1)}, bf16[3,272,256]{2,1,0:T(8,128)(2,1)S(1)}, u32[]{:S(2)}, u32[]{:S(2)}) collective-permute-start(bf16[3,272,256]{2,1,0:T(8,128)(2,1)S(1)} %get-tuple-element.19.refs_0_), channel_id=1, source_target_pairs={{0,16},{8,24},{16,0},{24,8},{1,17},{9,25},{17,1},{25,9},{2,18},{10... | collective-permute-start | bytes 1253384 | tf_op jit(solution)/shard_map/ppermute | solution.py:35
  6.8 0.6 %collective-permute-done.4 = bf16[1,3,128,128]{3,2,1,0:T(8,128)(2,1)S(1)} collective-permute-done((bf16[1,3,128,128]{3,2,1,0:T(8,128)(2,1)}, bf16[1,3,128,128]{3,2,1,0:T(8,128)(2,1)S(1)}, u32[]{:S(2)}, u32[]{:S(2)}) %collective-permute-start.4) | collective-permute-done | bytes 98336 | tf_op jit(solution)/shard_map/ppermute | solution.py:58
  7.5 0.4 collective-permute-done.3
  7.8 0.9 %broadcast_select_fusion.3 = (bf16[1,3,128,128]{3,2,1,0:T(8,128)(2,1)S(1)}, bf16[1,3,128,128]{3,2,1,0:T(8,128)(2,1)S(1)}) fusion(bf16[1,3,128,128]{3,2,1,0:T(8,128)(2,1)S(1)} %collective-permute-done.3, pred[]{:T(512)S(6)} %eq.6, bf16[3,1,128,128]{3,2,1,0:T(8,128)(2,1)} %param.6, bf16[1,3,128,128]{3,2,1,0:T(8,128)(2,1)S(1)} %collective-permute-done.4), kind=kLoop, calls=%fused_computation.4 | loop fusion | flops 98304 | bytes 491521 | tf_op jit(solution)/shard_map/jit(_where)/select_n | solution.py:265
  8.8 1.3 %collective-permute-start.6 = (bf16[2,3,128,128]{3,2,1,0:T(8,128)(2,1)S(1)}, bf16[2,3,128,128]{3,2,1,0:T(8,128)(2,1)S(1)}, u32[]{:S(2)}, u32[]{:S(2)}) collective-permute-start(bf16[2,3,128,128]{3,2,1,0:T(8,128)(2,1)S(1)} %pad_maximum_fusion.own), channel_id=1, source_target_pairs={{0,1},{1,0},{2,3},{3,2},{4,5},{5,4},{6,7},{7,6},{8,9},{9,8},{10,11... | collective-permute-start | bytes 589832 | tf_op jit(solution)/shard_map/ppermute | solution.py:39
  10.1 4.1 %collective-permute-start.5 = (bf16[2,3,128,128]{3,2,1,0:T(8,128)(2,1)S(1)}, bf16[2,3,128,128]{3,2,1,0:T(8,128)(2,1)S(1)}, u32[]{:S(2)}, u32[]{:S(2)}) collective-permute-start(bf16[2,3,128,128]{3,2,1,0:T(8,128)(2,1)S(1)} %pad_maximum_fusion.own), channel_id=1, source_target_pairs={{0,2},{1,3},{2,0},{3,1},{4,6},{5,7},{6,4},{7,5},{8,10},{9,11},{10,... | collective-permute-start | bytes 589832 | tf_op jit(solution)/shard_map/ppermute | solution.py:39
  14.2 1.2 %collective-permute-start.1 = (bf16[3,272,256]{2,1,0:T(8,128)(2,1)S(1)}, bf16[3,272,256]{2,1,0:T(8,128)(2,1)S(1)}, u32[]{:S(2)}, u32[]{:S(2)}) collective-permute-start(bf16[3,272,256]{2,1,0:T(8,128)(2,1)S(1)} %get-tuple-element.19.refs_0_), channel_id=1, source_target_pairs={{0,8},{8,0},{16,24},{24,16},{1,9},{9,1},{17,25},{25,17},{2,10},{10... | collective-permute-start | bytes 1253384 | tf_op jit(solution)/shard_map/ppermute | solution.py:35
  15.4 0.7 %collective-permute-done.refs_1_ = bf16[3,272,256]{2,1,0:T(8,128)(2,1)S(1)} collective-permute-done((bf16[3,272,256]{2,1,0:T(8,128)(2,1)S(1)}, bf16[3,272,256]{2,1,0:T(8,128)(2,1)S(1)}, u32[]{:S(2)}, u32[]{:S(2)}) %collective-permute-start) | collective-permute-done | bytes 417824 | tf_op jit(solution)/shard_map/ppermute | solution.py:35
  16.1 2.1 %collective-permute-start.2 = (bf16[3,272,256]{2,1,0:T(8,128)(2,1)S(1)}, bf16[3,272,256]{2,1,0:T(8,128)(2,1)S(1)}, u32[]{:S(2)}, u32[]{:S(2)}) collective-permute-start(bf16[3,272,256]{2,1,0:T(8,128)(2,1)S(1)} %collective-permute-done.refs_1_), channel_id=1, source_target_pairs={{0,8},{8,0},{16,24},{24,16},{1,9},{9,1},{17,25},{25,17},{2,10},{10... | collective-permute-start | bytes 1253384 | tf_op jit(solution)/shard_map/ppermute | solution.py:35
  18.2 0.0 collective-permute-done.6.own
  18.2 0.3 collective-permute-done.5.other
  18.5 1.6 %collective-permute-start.7 = (bf16[2,3,128,128]{3,2,1,0:T(8,128)(2,1)S(1)}, bf16[2,3,128,128]{3,2,1,0:T(8,128)(2,1)S(1)}, u32[]{:S(2)}, u32[]{:S(2)}) collective-permute-start(bf16[2,3,128,128]{3,2,1,0:T(8,128)(2,1)S(1)} %broadcast_select_fusion.1), channel_id=1, source_target_pairs={{0,8},{8,0},{16,24},{24,16},{1,9},{9,1},{17,25},{25,17},{2,10},{10... | collective-permute-start | bytes 589832 | tf_op jit(solution)/shard_map/ppermute | solution.py:35
  20.1 1.5 %collective-permute-start.10 = (bf16[2,3,128,128]{3,2,1,0:T(8,128)(2,1)S(1)}, bf16[2,3,128,128]{3,2,1,0:T(8,128)(2,1)S(1)}, u32[]{:S(2)}, u32[]{:S(2)}) collective-permute-start(bf16[2,3,128,128]{3,2,1,0:T(8,128)(2,1)S(1)} %collective-permute-done.6.own), channel_id=1, source_target_pairs={{0,2},{1,3},{2,0},{3,1},{4,6},{5,7},{6,4},{7,5},{8,10},{9,11},{10,... | collective-permute-start | bytes 589832 | tf_op jit(solution)/shard_map/ppermute | solution.py:39
  21.6 0.0 collective-permute-done.1.refs_2_
  21.6 0.0 collective-permute-done.2.refs_3_
  21.6 1.6 %left_products.1.z_ref = bf16[2,3,256,1536]{3,2,1,0:T(8,128)(2,1)S(1)} custom-call(bf16[3,272,256]{2,1,0:T(8,128)(2,1)S(1)} %get-tuple-element.19.refs_0_, bf16[3,272,256]{2,1,0:T(8,128)(2,1)S(1)} %collective-permute-done.refs_1_, bf16[3,272,256]{2,1,0:T(8,128)(2,1)S(1)} %collective-permute-done.1.refs_2_, ...), custom_call_target="tpu_custom_call" | custom-call | flops 1207959552 | bytes 1048576 | tf_op jit(solution)/shard_map/left_products/pallas_call | solution.py:169
  23.2 0.0 collective-permute-done.7.received
  23.2 1.0 %right_products.2 = (f32[3,256,128]{2,1,0:T(8,128)S(1)}, bf16[3,256,128]{2,1,0:T(8,128)(2,1)S(1)}, bf16[3,256,128]{2,1,0:T(8,128)(2,1)S(1)}) custom-call(bf16[2,3,256,1536]{3,2,1,0:T(8,128)(2,1)S(1)} %left_products.1.z_ref, bf16[2,3,128,128]{3,2,1,0:T(8,128)(2,1)S(1)} %pad_maximum_fusion.own, bf16[2,3,128,128]{3,2,1,0:T(8,128)(2,1)S(1)} %collective-permute-done.5.other, ...), custom_call_target="tpu_custom_call" | custom-call | tf_op jit(solution)/shard_map/right_products/pallas_call | solution.py:209
  24.2 2.4 %collective-permute-done.10.other = bf16[2,3,128,128]{3,2,1,0:T(8,128)(2,1)S(1)} collective-permute-done((bf16[2,3,128,128]{3,2,1,0:T(8,128)(2,1)S(1)}, bf16[2,3,128,128]{3,2,1,0:T(8,128)(2,1)S(1)}, u32[]{:S(2)}, u32[]{:S(2)}) %collective-permute-start.10) | collective-permute-done | bytes 196640 | tf_op jit(solution)/shard_map/ppermute | solution.py:39
  26.6 0.9 %collective-permute-start.11 = (bf16[2,3,128,128]{3,2,1,0:T(8,128)(2,1)S(1)}, bf16[2,3,128,128]{3,2,1,0:T(8,128)(2,1)S(1)}, u32[]{:S(2)}, u32[]{:S(2)}) collective-permute-start(bf16[2,3,128,128]{3,2,1,0:T(8,128)(2,1)S(1)} %broadcast_select_fusion), channel_id=1, source_target_pairs={{0,8},{8,0},{16,24},{24,16},{1,9},{9,1},{17,25},{25,17},{2,10},{10... | collective-permute-start | bytes 589832 | tf_op jit(solution)/shard_map/ppermute | solution.py:35
  27.5 0.6 %collective-permute-start.8 = (bf16[3,256,128]{2,1,0:T(8,128)(2,1)S(1)}, bf16[3,256,128]{2,1,0:T(8,128)(2,1)S(1)}, u32[]{:S(2)}, u32[]{:S(2)}) collective-permute-start(bf16[3,256,128]{2,1,0:T(8,128)(2,1)S(1)} %get-tuple-element.26), channel_id=1, source_target_pairs={{0,1},{1,0},{2,3},{3,2},{4,5},{5,4},{6,7},{7,6},{8,9},{9,8},{10,11... | collective-permute-start | bytes 589832 | tf_op jit(solution)/shard_map/ppermute | solution.py:284
  28.1 2.3 %collective-permute-start.9 = (bf16[3,256,128]{2,1,0:T(8,128)(2,1)S(1)}, bf16[3,256,128]{2,1,0:T(8,128)(2,1)S(1)}, u32[]{:S(2)}, u32[]{:S(2)}) collective-permute-start(bf16[3,256,128]{2,1,0:T(8,128)(2,1)S(1)} %get-tuple-element.27), channel_id=1, source_target_pairs={{1,2},{2,1},{3,4},{4,3},{5,6},{6,5},{9,10},{10,9},{11,12},{12,11},... | collective-permute-start | bytes 589832 | tf_op jit(solution)/shard_map/ppermute | solution.py:284
  30.4 0.0 collective-permute-done.11.received
  30.4 1.0 %right_products.3 = (f32[3,256,128]{2,1,0:T(8,128)S(1)}, bf16[3,256,128]{2,1,0:T(8,128)(2,1)S(1)}, bf16[3,256,128]{2,1,0:T(8,128)(2,1)S(1)}) custom-call(bf16[2,3,256,1536]{3,2,1,0:T(8,128)(2,1)S(1)} %left_products.1.z_ref, bf16[2,3,128,128]{3,2,1,0:T(8,128)(2,1)S(1)} %collective-permute-done.6.own, ...), custom_call_target="tpu_custom_call" | custom-call | tf_op jit(solution)/shard_map/right_products/pallas_call | solution.py:209
  31.4 2.3 %collective-permute-start.12 = (bf16[3,256,128]{2,1,0:T(8,128)(2,1)S(1)}, bf16[3,256,128]{2,1,0:T(8,128)(2,1)S(1)}, u32[]{:S(2)}, u32[]{:S(2)}) collective-permute-start(bf16[3,256,128]{2,1,0:T(8,128)(2,1)S(1)} %get-tuple-element.31), channel_id=1, source_target_pairs={{0,1},{1,0},{2,3},{3,2},{4,5},{5,4},{6,7},{7,6},{8,9},{9,8},{10,11... | collective-permute-start | bytes 589832 | tf_op jit(solution)/shard_map/ppermute | solution.py:284
  33.7 1.9 %collective-permute-start.13 = (bf16[3,256,128]{2,1,0:T(8,128)(2,1)S(1)}, bf16[3,256,128]{2,1,0:T(8,128)(2,1)S(1)}, u32[]{:S(2)}, u32[]{:S(2)}) collective-permute-start(bf16[3,256,128]{2,1,0:T(8,128)(2,1)S(1)} %get-tuple-element.32), channel_id=1, source_target_pairs={{1,2},{2,1},{3,4},{4,3},{5,6},{6,5},{9,10},{10,9},{11,12},{12,11},... | collective-permute-start | bytes 589832 | tf_op jit(solution)/shard_map/ppermute | solution.py:284
  35.6 2.6 %collective-permute-done.8.refs_1_ = bf16[3,256,128]{2,1,0:T(8,128)(2,1)S(1)} collective-permute-done((bf16[3,256,128]{2,1,0:T(8,128)(2,1)S(1)}, bf16[3,256,128]{2,1,0:T(8,128)(2,1)S(1)}, u32[]{:S(2)}, u32[]{:S(2)}) %collective-permute-start.8) | collective-permute-done | bytes 196640 | tf_op jit(solution)/shard_map/ppermute | solution.py:284
  38.2 8.4 %collective-permute-done.12.refs_4_ = bf16[3,256,128]{2,1,0:T(8,128)(2,1)S(1)} collective-permute-done((bf16[3,256,128]{2,1,0:T(8,128)(2,1)S(1)}, bf16[3,256,128]{2,1,0:T(8,128)(2,1)S(1)}, u32[]{:S(2)}, u32[]{:S(2)}) %collective-permute-start.12) | collective-permute-done | bytes 196640 | tf_op jit(solution)/shard_map/ppermute | solution.py:284
  46.6 0.9 %summed.1 = bf16[3,256,256]{2,1,0:T(8,128)(2,1)} custom-call(f32[3,256,128]{2,1,0:T(8,128)S(1)} %get-tuple-element.25.refs_0_, bf16[3,256,128]{2,1,0:T(8,128)(2,1)S(1)} %collective-permute-done.8.refs_1_, bf16[3,256,128]{2,1,0:T(8,128)(2,1)S(1)} %collective-permute-done.9.refs_2_, f32[3,256,128]{2,1,0:T(8,128)S(1)} %get-tuple-element.30.refs_3_, ...), custom_call_target="tpu_custom_call" | custom-call | tf_op jit(solution)/shard_map/summed/pallas_call | solution.py:244
  (5 shorter events, 0.1 us)
Async XLA Ops:
  0.0 7.5 %collective-permute-start.4 = (bf16[1,3,128,128]{3,2,1,0:T(8,128)(2,1)}, bf16[1,3,128,128]{3,2,1,0:T(8,128)(2,1)S(1)}, u32[]{:S(2)}, u32[]{:S(2)}) collective-permute-start(bf16[1,3,128,128]{3,2,1,0:T(8,128)(2,1)} %bitcast.7), channel_id=1, source_target_pairs={{4,16},{5,17},{6,18},{7,19},{12,24},{13,25},{14,26},{15,27},{16,4}... | collective-permute-start | bytes 294920 | tf_op jit(solution)/shard_map/ppermute | solution.py:58
  2.9 4.9 %collective-permute-start.3 = (bf16[1,3,128,128]{3,2,1,0:T(8,128)(2,1)}, bf16[1,3,128,128]{3,2,1,0:T(8,128)(2,1)S(1)}, u32[]{:S(2)}, u32[]{:S(2)}) collective-permute-start(bf16[1,3,128,128]{3,2,1,0:T(8,128)(2,1)} %bitcast.8), channel_id=1, source_target_pairs={{0,4},{1,5},{2,6},{3,7},{4,20},{5,21},{6,22},{7,23},{8,12},{9,13},... | collective-permute-start | bytes 294920 | tf_op jit(solution)/shard_map/ppermute | solution.py:58
  5.1 11.0 %collective-permute-start = (bf16[3,272,256]{2,1,0:T(8,128)(2,1)S(1)}, bf16[3,272,256]{2,1,0:T(8,128)(2,1)S(1)}, u32[]{:S(2)}, u32[]{:S(2)}) collective-permute-start(bf16[3,272,256]{2,1,0:T(8,128)(2,1)S(1)} %get-tuple-element.19.refs_0_), channel_id=1, source_target_pairs={{0,16},{8,24},{16,0},{24,8},{1,17},{9,25},{17,1},{25,9},{2,18},{10... | collective-permute-start | bytes 1253384 | tf_op jit(solution)/shard_map/ppermute | solution.py:35
  8.8 9.4 %collective-permute-start.6 = (bf16[2,3,128,128]{3,2,1,0:T(8,128)(2,1)S(1)}, bf16[2,3,128,128]{3,2,1,0:T(8,128)(2,1)S(1)}, u32[]{:S(2)}, u32[]{:S(2)}) collective-permute-start(bf16[2,3,128,128]{3,2,1,0:T(8,128)(2,1)S(1)} %pad_maximum_fusion.own), channel_id=1, source_target_pairs={{0,1},{1,0},{2,3},{3,2},{4,5},{5,4},{6,7},{7,6},{8,9},{9,8},{10,11... | collective-permute-start | bytes 589832 | tf_op jit(solution)/shard_map/ppermute | solution.py:39
  10.1 8.4 %collective-permute-start.5 = (bf16[2,3,128,128]{3,2,1,0:T(8,128)(2,1)S(1)}, bf16[2,3,128,128]{3,2,1,0:T(8,128)(2,1)S(1)}, u32[]{:S(2)}, u32[]{:S(2)}) collective-permute-start(bf16[2,3,128,128]{3,2,1,0:T(8,128)(2,1)S(1)} %pad_maximum_fusion.own), channel_id=1, source_target_pairs={{0,2},{1,3},{2,0},{3,1},{4,6},{5,7},{6,4},{7,5},{8,10},{9,11},{10,... | collective-permute-start | bytes 589832 | tf_op jit(solution)/shard_map/ppermute | solution.py:39
  14.2 7.4 %collective-permute-start.1 = (bf16[3,272,256]{2,1,0:T(8,128)(2,1)S(1)}, bf16[3,272,256]{2,1,0:T(8,128)(2,1)S(1)}, u32[]{:S(2)}, u32[]{:S(2)}) collective-permute-start(bf16[3,272,256]{2,1,0:T(8,128)(2,1)S(1)} %get-tuple-element.19.refs_0_), channel_id=1, source_target_pairs={{0,8},{8,0},{16,24},{24,16},{1,9},{9,1},{17,25},{25,17},{2,10},{10... | collective-permute-start | bytes 1253384 | tf_op jit(solution)/shard_map/ppermute | solution.py:35
  16.1 5.5 %collective-permute-start.2 = (bf16[3,272,256]{2,1,0:T(8,128)(2,1)S(1)}, bf16[3,272,256]{2,1,0:T(8,128)(2,1)S(1)}, u32[]{:S(2)}, u32[]{:S(2)}) collective-permute-start(bf16[3,272,256]{2,1,0:T(8,128)(2,1)S(1)} %collective-permute-done.refs_1_), channel_id=1, source_target_pairs={{0,8},{8,0},{16,24},{24,16},{1,9},{9,1},{17,25},{25,17},{2,10},{10... | collective-permute-start | bytes 1253384 | tf_op jit(solution)/shard_map/ppermute | solution.py:35
  18.5 4.7 %collective-permute-start.7 = (bf16[2,3,128,128]{3,2,1,0:T(8,128)(2,1)S(1)}, bf16[2,3,128,128]{3,2,1,0:T(8,128)(2,1)S(1)}, u32[]{:S(2)}, u32[]{:S(2)}) collective-permute-start(bf16[2,3,128,128]{3,2,1,0:T(8,128)(2,1)S(1)} %broadcast_select_fusion.1), channel_id=1, source_target_pairs={{0,8},{8,0},{16,24},{24,16},{1,9},{9,1},{17,25},{25,17},{2,10},{10... | collective-permute-start | bytes 589832 | tf_op jit(solution)/shard_map/ppermute | solution.py:35
  20.1 6.5 %collective-permute-start.10 = (bf16[2,3,128,128]{3,2,1,0:T(8,128)(2,1)S(1)}, bf16[2,3,128,128]{3,2,1,0:T(8,128)(2,1)S(1)}, u32[]{:S(2)}, u32[]{:S(2)}) collective-permute-start(bf16[2,3,128,128]{3,2,1,0:T(8,128)(2,1)S(1)} %collective-permute-done.6.own), channel_id=1, source_target_pairs={{0,2},{1,3},{2,0},{3,1},{4,6},{5,7},{6,4},{7,5},{8,10},{9,11},{10,... | collective-permute-start | bytes 589832 | tf_op jit(solution)/shard_map/ppermute | solution.py:39
  26.6 3.8 %collective-permute-start.11 = (bf16[2,3,128,128]{3,2,1,0:T(8,128)(2,1)S(1)}, bf16[2,3,128,128]{3,2,1,0:T(8,128)(2,1)S(1)}, u32[]{:S(2)}, u32[]{:S(2)}) collective-permute-start(bf16[2,3,128,128]{3,2,1,0:T(8,128)(2,1)S(1)} %broadcast_select_fusion), channel_id=1, source_target_pairs={{0,8},{8,0},{16,24},{24,16},{1,9},{9,1},{17,25},{25,17},{2,10},{10... | collective-permute-start | bytes 589832 | tf_op jit(solution)/shard_map/ppermute | solution.py:35
  27.5 10.7 %collective-permute-start.8 = (bf16[3,256,128]{2,1,0:T(8,128)(2,1)S(1)}, bf16[3,256,128]{2,1,0:T(8,128)(2,1)S(1)}, u32[]{:S(2)}, u32[]{:S(2)}) collective-permute-start(bf16[3,256,128]{2,1,0:T(8,128)(2,1)S(1)} %get-tuple-element.26), channel_id=1, source_target_pairs={{0,1},{1,0},{2,3},{3,2},{4,5},{5,4},{6,7},{7,6},{8,9},{9,8},{10,11... | collective-permute-start | bytes 589832 | tf_op jit(solution)/shard_map/ppermute | solution.py:284
  28.1 10.1 %collective-permute-start.9 = (bf16[3,256,128]{2,1,0:T(8,128)(2,1)S(1)}, bf16[3,256,128]{2,1,0:T(8,128)(2,1)S(1)}, u32[]{:S(2)}, u32[]{:S(2)}) collective-permute-start(bf16[3,256,128]{2,1,0:T(8,128)(2,1)S(1)} %get-tuple-element.27), channel_id=1, source_target_pairs={{1,2},{2,1},{3,4},{4,3},{5,6},{6,5},{9,10},{10,9},{11,12},{12,11},... | collective-permute-start | bytes 589832 | tf_op jit(solution)/shard_map/ppermute | solution.py:284
  31.4 15.3 %collective-permute-start.12 = (bf16[3,256,128]{2,1,0:T(8,128)(2,1)S(1)}, bf16[3,256,128]{2,1,0:T(8,128)(2,1)S(1)}, u32[]{:S(2)}, u32[]{:S(2)}) collective-permute-start(bf16[3,256,128]{2,1,0:T(8,128)(2,1)S(1)} %get-tuple-element.31), channel_id=1, source_target_pairs={{0,1},{1,0},{2,3},{3,2},{4,5},{5,4},{6,7},{7,6},{8,9},{9,8},{10,11... | collective-permute-start | bytes 589832 | tf_op jit(solution)/shard_map/ppermute | solution.py:284
  33.7 12.9 %collective-permute-start.13 = (bf16[3,256,128]{2,1,0:T(8,128)(2,1)S(1)}, bf16[3,256,128]{2,1,0:T(8,128)(2,1)S(1)}, u32[]{:S(2)}, u32[]{:S(2)}) collective-permute-start(bf16[3,256,128]{2,1,0:T(8,128)(2,1)S(1)} %get-tuple-element.32), channel_id=1, source_target_pairs={{1,2},{2,1},{3,4},{4,3},{5,6},{6,5},{9,10},{10,9},{11,12},{12,11},... | collective-permute-start | bytes 589832 | tf_op jit(solution)/shard_map/ppermute | solution.py:284

commit v4 on v3

--- a/solution.py
+++ b/solution.py
@@ -97,17 +97,43 @@
     return jnp.max(left[inner, ML:, :MR].astype(jnp.float32)).astype(jnp.int32)
 
 
-def pack_kernel(n_op, shift, left, wave, packed, window, shift_ref, sems):
+def pack_kernel(shift, left, right, packed, kept, shift_ref, sems):
+    copies = [
+        pltpu.make_async_copy(shift, shift_ref, sems.at[0]),
+        pltpu.make_async_copy(left, packed.at[:, pl.ds(0, ML)], sems.at[1]),
+        pltpu.make_async_copy(right, kept, sems.at[2]),
+    ]
+    for copy in copies:
+        copy.start()
+    copies[0].wait()
+    for inner in range(left.shape[0]):
+        tag = jnp.full((TILE, ML), shift_ref[inner].astype(jnp.float32)).astype(jnp.bfloat16)
+        packed[inner, ML:] = tag
+    for copy in copies[1:]:
+        copy.wait()
+
+
+def pack(shift, left, right):
+    return pl.pallas_call(
+        pack_kernel,
+        out_shape=[in_vmem((left.shape[0], ML + TILE, ML)), in_vmem(right.shape)],
+        in_specs=[HBM] * 3,
+        out_specs=[VMEM] * 2,
+        scratch_shapes=[pltpu.SMEM(shift.shape, jnp.int32), pltpu.SemaphoreType.DMA((3,))],
+        compiler_params=grant(8),
+        cost_estimate=cost(0, 32 * 1024 * 1024),
+        name="pack",
+    )(in_hbm(shift), in_hbm(left), in_hbm(right))
+
+
+def window_kernel(n_op, wave, window, sems):
     width = window.shape[2] - 2 * MR
     op = lax.axis_index("op")
     start = pl.multiple_of(op * width, MR)
-    copies = [
-        pltpu.make_async_copy(shift, shift_ref, sems.at[0]),
-        pltpu.make_async_copy(left, packed.at[:, pl.ds(0, ML)], sems.at[1]),
-        pltpu.make_async_copy(wave.at[:, :, pl.ds(start, width)], window.at[:, :, pl.ds(MR, width)], sems.at[2]),
-    ]
-    for copy in copies:
-        copy.start()
+    middle = pltpu.make_async_copy(
+        wave.at[:, :, pl.ds(start, width)], window.at[:, :, pl.ds(MR, width)], sems.at[0]
+    )
+    middle.start()
 
     def edge(valid, source, target, sem):
         @pl.when(valid)
@@ -122,28 +148,23 @@
         def _():
             window[:, :, pl.ds(target, MR)] = jnp.zeros((VECS, ML, MR), jnp.bfloat16)
 
-    edge(op > 0, start - MR, 0, sems.at[3])
-    edge(op < n_op - 1, start + width, MR + width, sems.at[4])
-    copies[0].wait()
-    for inner in range(left.shape[0]):
-        tag = jnp.full((TILE, ML), shift_ref[inner].astype(jnp.float32)).astype(jnp.bfloat16)
-        packed[inner, ML:] = tag
-    copies[1].wait()
-    copies[2].wait()
-
-
-def pack(shift, left, wave, n_op):
+    edge(op > 0, start - MR, 0, sems.at[1])
+    edge(op < n_op - 1, start + width, MR + width, sems.at[2])
+    middle.wait()
+
+
+def window_of(wave, n_op):
     width = wave.shape[2] // n_op
     return pl.pallas_call(
-        functools.partial(pack_kernel, n_op),
-        out_shape=[in_vmem((left.shape[0], ML + TILE, ML)), in_vmem((VECS, ML, width + 2 * MR))],
-        in_specs=[HBM] * 3,
-        out_specs=[VMEM] * 2,
-        scratch_shapes=[pltpu.SMEM(shift.shape, jnp.int32), pltpu.SemaphoreType.DMA((5,))],
-        compiler_params=grant(8),
-        cost_estimate=cost(0, 32 * 1024 * 1024),
-        name="pack",
-    )(in_hbm(shift), in_hbm(left), in_hbm(wave))
+        functools.partial(window_kernel, n_op),
+        out_shape=in_vmem((VECS, ML, width + 2 * MR)),
+        in_specs=[HBM],
+        out_specs=VMEM,
+        scratch_shapes=[pltpu.SemaphoreType.DMA((3,))],
+        compiler_params=grant(4),
+        cost_estimate=cost(0, 2 * 1024 * 1024),
+        name="window",
+    )(in_hbm(wave))
 
 
 def left_kernel(*refs):
@@ -256,13 +277,14 @@
     tie = lax.optimization_barrier
     matching = lax.axis_index("op") ^ (lax.axis_index("sec") // per)
     held = right_ops.reshape((1,) + right_ops.shape[:1] + right_ops.shape[2:])
-    packed, window = pack(term_shift, left_ops.transpose(1, 0, 2), wavefunction.transpose(1, 0, 2), n_op)
+    packed, kept = pack(term_shift, left_ops.transpose(1, 0, 2), held)
+    window = window_of(wavefunction.transpose(1, 0, 2), n_op)
     lefts = [packed]
     bit = n_op // 2
     while bit > 1:
-        one, two = tie(towards_owner(held, n_op, n_sec, bit))
+        one, two, window = tie((*towards_owner(held, n_op, n_sec, bit), window))
         same = (matching & bit) == 0
-        held = jnp.concatenate([jnp.where(same, held, one), jnp.where(same, one, two)])
+        held = kept = jnp.concatenate([jnp.where(same, kept, one), jnp.where(same, one, two)])
         lefts = lefts + [over_op(x, n_op, bit) for x in lefts]
         bit //= 2
     lefts = lefts + [over_op(x, n_op, 1) for x in lefts]
@@ -276,14 +298,23 @@
     low = [(d, d ^ 1) for d in range(n_sec)]
     high = [(d, ((d + 1) ^ 1) - 1) for d in range(1, n_sec - 1)]
     settled = (matching & 1) == 0
-    parts = []
+    parts, others = [], [other]
     for cls, own in enumerate(owns):
         received = over_op(jnp.where(settled, other, own), n_op, 1)
-        later = over_sec(owns[cls + 1], n_sec, per) if cls + 1 < per else None
+        later = None
+        if cls + 1 < per:
+            half = own.shape[0] // 2
+            step = (cls + 1) & -(cls + 1)
+            later = [
+                over_sec(owns[cls + 1][:half], n_sec, per),
+                over_sec(others[(cls + 1) ^ step][half:], n_sec, step),
+            ]
         zero, to_low, to_high = right_products(cls, per, z, own, other, received, lefts)
         parts += [zero, lax.ppermute(to_low, "sec", low), lax.ppermute(to_high, "sec", high)]
         if later is not None:
-            other, _ = tie((later, zero))
+            later, _ = tie((later, zero))
+            other = jnp.concatenate(later)
+            others.append(other)
     return summed(per, parts).transpose(1, 0, 2)
 
 

time: 48.1 us -> 46.9 us (0.975)
  waiting for transfers between devices: 15.4 us -> 13.8 us
  Pallas kernels: 6.58 us -> 7.48 us
  other arithmetic: 0.98 us -> 0.09 us
  starting transfers between devices: 24.4 us -> 25 us
    ppermute x3 -> x4, waiting for transfers between devices: 2.71 us -> 0.01 us  [over_sec(): return lax.ppermute(x, 'sec', [(d, d ^ bit) for d in range(n_sec)])]
    ppermute x5, waiting for transfers between devices: 0.75 us -> 2.77 us  [over_op(): return lax.ppermute(x, 'op', [(o, o ^ bit) for o in range(n_op)])]
    ppermute x2, starting transfers between devices: 4.18 us -> 5.1 us  [on_device(): lax.ppermute(to_high, 'sec', high)]
    select_n x1, other arithmetic: 0.91 us -> 0.03 us  [on_device(): jnp.where(same, kept, one)]
    pallas_call x1 -> x2, Pallas kernels: 2.16 us -> 3.04 us  [the longest x1 2 us: window_of(): pl.pallas_call(functools.partial(window_kernel, n_op), out_shape=in_vmem(...]
    ppermute x1, waiting for transfers between devices: 0.62 us -> 0.01 us  [towards_owner(): lax.ppermute(held, ('op', 'sec'), second)]
    ppermute x2, starting transfers between devices: 2.93 us -> 2.4 us  [on_device(): lax.ppermute(to_low, 'sec', low)]
    ppermute x3 -> x4, starting transfers between devices: 6.87 us -> 7.29 us  [over_sec(): return lax.ppermute(x, 'sec', [(d, d ^ bit) for d in range(n_sec)])]
  transfers between devices with their start and end apart: 14 -> 15, of which waited for: 7 -> 3; matrix products, arithmetic and copies ran while one was open for 2% -> 0% of each run, Pallas kernels for 12% -> 14%
where the time goes in v4:
time: 46.9 us; the launch traced here: 46.7 us
  starting transfers between devices  25 us (53%)
  waiting for transfers between devices  13.8 us (29%)
  Pallas kernels  7.48 us (16%)
    ppermute x2, waiting for transfers between devices, on_device(): lax.ppermute(to_low, 'sec', low)  11 us
    ppermute x5, starting transfers between devices, over_op(): return lax.ppermute(x, 'op', [(o, o ^ bit) for o in range(n_op)])  7.31 us
    ppermute x4, starting transfers between devices, over_sec(): return lax.ppermute(x, 'sec', [(d, d ^ bit) for d in range(n_sec)])  7.29 us
    ppermute x2, starting transfers between devices, on_device(): lax.ppermute(to_high, 'sec', high)  5.1 us
    ppermute x1, starting transfers between devices, towards_owner(): lax.ppermute(held, ('op', 'sec'), second)  2.88 us
    ppermute x5, waiting for transfers between devices, over_op(): return lax.ppermute(x, 'op', [(o, o ^ bit) for o in range(n_op)])  2.77 us
    ppermute x2, starting transfers between devices, on_device(): lax.ppermute(to_low, 'sec', low)  2.4 us
    pallas_call x1, Pallas kernels, window_of(): pl.pallas_call(functools.partial(window_kernel, n_op), out_shape=in_vmem(...  2 us
  transfers between devices with their start and end apart: 15, of which 3 were waited for; matrix products, arithmetic and copies ran while one was open for 0% of the time, Pallas kernels for 14%

profile of v4, /device:TPU:17, one launch (start us, length us, event | category | flops | bytes accessed | tf_op | source)
XLA Modules:
  0.0 46.7 jit_solution(13265768931280931627)
XLA Ops:
  0.0 2.9 %collective-permute-start.4 = (bf16[1,3,128,128]{3,2,1,0:T(8,128)(2,1)}, bf16[1,3,128,128]{3,2,1,0:T(8,128)(2,1)S(1)}, u32[]{:S(2)}, u32[]{:S(2)}) collective-permute-start(bf16[1,3,128,128]{3,2,1,0:T(8,128)(2,1)} %bitcast.6), channel_id=1, source_target_pairs={{4,16},{5,17},{6,18},{7,19},{12,24},{13,25},{14,26},{15,27},{16,4}... | collective-permute-start | bytes 294920 | tf_op jit(solution)/shard_map/ppermute | solution.py:58
  2.9 0.1 collective-permute-start.3
  3.0 1.0 %pack.1 = (bf16[3,272,256]{2,1,0:T(8,128)(2,1)S(1)}, bf16[1,3,128,128]{3,2,1,0:T(8,128)(2,1)S(1)}) custom-call(s32[3]{0:T(128)} %shift.1, bf16[3,256,256]{2,1,0:T(8,128)(2,1)} %bitcast.5, bf16[1,3,128,128]{3,2,1,0:T(8,128)(2,1)} %bitcast.8), custom_call_target="tpu_custom_call" | custom-call | bytes 33554432 | tf_op jit(solution)/shard_map/pack/pallas_call | solution.py:117
  4.0 2.6 %collective-permute-start = (bf16[3,272,256]{2,1,0:T(8,128)(2,1)S(1)}, bf16[3,272,256]{2,1,0:T(8,128)(2,1)S(1)}, u32[]{:S(2)}, u32[]{:S(2)}) collective-permute-start(bf16[3,272,256]{2,1,0:T(8,128)(2,1)S(1)} %get-tuple-element.21.refs_0_), channel_id=1, source_target_pairs={{0,16},{8,24},{16,0},{24,8},{1,17},{9,25},{17,1},{25,9},{2,18},{10... | collective-permute-start | bytes 1253384 | tf_op jit(solution)/shard_map/ppermute | solution.py:35
  6.6 2.0 %window.1.refs_4_ = bf16[3,256,512]{2,1,0:T(8,128)(2,1)S(1)} custom-call(bf16[3,256,1024]{2,1,0:T(8,128)(2,1)} %bitcast.4), custom_call_target="tpu_custom_call" | custom-call | bytes 2097152 | tf_op jit(solution)/shard_map/window/pallas_call | solution.py:158
  8.6 0.0 collective-permute-done.4
  8.6 0.0 collective-permute-done.3
  8.7 1.3 %collective-permute-start.6 = (bf16[2,3,128,128]{3,2,1,0:T(8,128)(2,1)S(1)}, bf16[2,3,128,128]{3,2,1,0:T(8,128)(2,1)S(1)}, u32[]{:S(2)}, u32[]{:S(2)}) collective-permute-start(bf16[2,3,128,128]{3,2,1,0:T(8,128)(2,1)S(1)} %pad_maximum_fusion.own), channel_id=1, source_target_pairs={{0,1},{1,0},{2,3},{3,2},{4,5},{5,4},{6,7},{7,6},{8,9},{9,8},{10,11... | collective-permute-start | bytes 589832 | tf_op jit(solution)/shard_map/ppermute | solution.py:39
  10.0 3.2 %collective-permute-start.5 = (bf16[2,3,128,128]{3,2,1,0:T(8,128)(2,1)S(1)}, bf16[2,3,128,128]{3,2,1,0:T(8,128)(2,1)S(1)}, u32[]{:S(2)}, u32[]{:S(2)}) collective-permute-start(bf16[2,3,128,128]{3,2,1,0:T(8,128)(2,1)S(1)} %pad_maximum_fusion.own), channel_id=1, source_target_pairs={{0,2},{1,3},{2,0},{3,1},{4,6},{5,7},{6,4},{7,5},{8,10},{9,11},{10,... | collective-permute-start | bytes 589832 | tf_op jit(solution)/shard_map/ppermute | solution.py:39
  13.3 1.2 %collective-permute-start.1 = (bf16[3,272,256]{2,1,0:T(8,128)(2,1)S(1)}, bf16[3,272,256]{2,1,0:T(8,128)(2,1)S(1)}, u32[]{:S(2)}, u32[]{:S(2)}) collective-permute-start(bf16[3,272,256]{2,1,0:T(8,128)(2,1)S(1)} %get-tuple-element.21.refs_0_), channel_id=1, source_target_pairs={{0,8},{8,0},{16,24},{24,16},{1,9},{9,1},{17,25},{25,17},{2,10},{10... | collective-permute-start | bytes 1253384 | tf_op jit(solution)/shard_map/ppermute | solution.py:35
  14.5 2.8 %collective-permute-done.refs_1_ = bf16[3,272,256]{2,1,0:T(8,128)(2,1)S(1)} collective-permute-done((bf16[3,272,256]{2,1,0:T(8,128)(2,1)S(1)}, bf16[3,272,256]{2,1,0:T(8,128)(2,1)S(1)}, u32[]{:S(2)}, u32[]{:S(2)}) %collective-permute-start) | collective-permute-done | bytes 417824 | tf_op jit(solution)/shard_map/ppermute | solution.py:35
  17.2 0.9 %collective-permute-start.2 = (bf16[3,272,256]{2,1,0:T(8,128)(2,1)S(1)}, bf16[3,272,256]{2,1,0:T(8,128)(2,1)S(1)}, u32[]{:S(2)}, u32[]{:S(2)}) collective-permute-start(bf16[3,272,256]{2,1,0:T(8,128)(2,1)S(1)} %collective-permute-done.refs_1_), channel_id=1, source_target_pairs={{0,8},{8,0},{16,24},{24,16},{1,9},{9,1},{17,25},{25,17},{2,10},{10... | collective-permute-start | bytes 1253384 | tf_op jit(solution)/shard_map/ppermute | solution.py:35
  18.2 0.0 collective-permute-done.6.own
  18.2 0.0 collective-permute-done.5.other
  18.2 1.0 %collective-permute-start.7 = (bf16[2,3,128,128]{3,2,1,0:T(8,128)(2,1)S(1)}, bf16[2,3,128,128]{3,2,1,0:T(8,128)(2,1)S(1)}, u32[]{:S(2)}, u32[]{:S(2)}) collective-permute-start(bf16[2,3,128,128]{3,2,1,0:T(8,128)(2,1)S(1)} %broadcast_select_fusion.1), channel_id=1, source_target_pairs={{0,8},{8,0},{16,24},{24,16},{1,9},{9,1},{17,25},{25,17},{2,10},{10... | collective-permute-start | bytes 589832 | tf_op jit(solution)/shard_map/ppermute | solution.py:35
  19.2 1.5 %collective-permute-start.10 = (bf16[1,3,128,128]{3,2,1,0:T(8,128)(2,1)S(1)}, bf16[1,3,128,128]{3,2,1,0:T(8,128)(2,1)S(1)}, u32[]{:S(2)}, u32[]{:S(2)}) collective-permute-start(bf16[1,3,128,128]{3,2,1,0:T(8,128)(2,1)S(1)} %slice.6), channel_id=1, source_target_pairs={{0,2},{1,3},{2,0},{3,1},{4,6},{5,7},{6,4},{7,5},{8,10},{9,11},{10,... | collective-permute-start | bytes 294920 | tf_op jit(solution)/shard_map/ppermute | solution.py:39
  20.8 1.2 %collective-permute-start.11 = (bf16[1,3,128,128]{3,2,1,0:T(8,128)(2,1)S(1)}, bf16[1,3,128,128]{3,2,1,0:T(8,128)(2,1)S(1)}, u32[]{:S(2)}, u32[]{:S(2)}) collective-permute-start(bf16[1,3,128,128]{3,2,1,0:T(8,128)(2,1)S(1)} %slice.7), channel_id=1, source_target_pairs={{0,1},{1,0},{2,3},{3,2},{4,5},{5,4},{6,7},{7,6},{8,9},{9,8},{10,11... | collective-permute-start | bytes 294920 | tf_op jit(solution)/shard_map/ppermute | solution.py:39
  22.0 0.0 collective-permute-done.2.refs_3_
  22.0 1.6 %left_products.1.z_ref = bf16[2,3,256,1536]{3,2,1,0:T(8,128)(2,1)S(1)} custom-call(bf16[3,272,256]{2,1,0:T(8,128)(2,1)S(1)} %get-tuple-element.21.refs_0_, bf16[3,272,256]{2,1,0:T(8,128)(2,1)S(1)} %collective-permute-done.refs_1_, bf16[3,272,256]{2,1,0:T(8,128)(2,1)S(1)} %collective-permute-done.1.refs_2_, ...), custom_call_target="tpu_custom_call" | custom-call | flops 1207959552 | bytes 1048576 | tf_op jit(solution)/shard_map/left_products/pallas_call | solution.py:190
  23.6 1.0 %right_products.2 = (f32[3,256,128]{2,1,0:T(8,128)S(1)}, bf16[3,256,128]{2,1,0:T(8,128)(2,1)S(1)}, bf16[3,256,128]{2,1,0:T(8,128)(2,1)S(1)}) custom-call(bf16[2,3,256,1536]{3,2,1,0:T(8,128)(2,1)S(1)} %left_products.1.z_ref, bf16[2,3,128,128]{3,2,1,0:T(8,128)(2,1)S(1)} %pad_maximum_fusion.own, bf16[2,3,128,128]{3,2,1,0:T(8,128)(2,1)S(1)} %collective-permute-done.5.other, ...), custom_call_target="tpu_custom_call" | custom-call | tf_op jit(solution)/shard_map/right_products/pallas_call | solution.py:230
  24.6 0.0 collective-permute-done.11
  24.7 1.5 %collective-permute-start.12 = (bf16[2,3,128,128]{3,2,1,0:T(8,128)(2,1)S(1)}, bf16[2,3,128,128]{3,2,1,0:T(8,128)(2,1)S(1)}, u32[]{:S(2)}, u32[]{:S(2)}) collective-permute-start(bf16[2,3,128,128]{3,2,1,0:T(8,128)(2,1)S(1)} %broadcast_select_fusion), channel_id=1, source_target_pairs={{0,8},{8,0},{16,24},{24,16},{1,9},{9,1},{17,25},{25,17},{2,10},{10... | collective-permute-start | bytes 589832 | tf_op jit(solution)/shard_map/ppermute | solution.py:35
  26.2 1.3 %collective-permute-start.8 = (bf16[3,256,128]{2,1,0:T(8,128)(2,1)S(1)}, bf16[3,256,128]{2,1,0:T(8,128)(2,1)S(1)}, u32[]{:S(2)}, u32[]{:S(2)}) collective-permute-start(bf16[3,256,128]{2,1,0:T(8,128)(2,1)S(1)} %get-tuple-element.29), channel_id=1, source_target_pairs={{0,1},{1,0},{2,3},{3,2},{4,5},{5,4},{6,7},{7,6},{8,9},{9,8},{10,11... | collective-permute-start | bytes 589832 | tf_op jit(solution)/shard_map/ppermute | solution.py:313
  27.5 1.9 %collective-permute-start.9 = (bf16[3,256,128]{2,1,0:T(8,128)(2,1)S(1)}, bf16[3,256,128]{2,1,0:T(8,128)(2,1)S(1)}, u32[]{:S(2)}, u32[]{:S(2)}) collective-permute-start(bf16[3,256,128]{2,1,0:T(8,128)(2,1)S(1)} %get-tuple-element.30), channel_id=1, source_target_pairs={{1,2},{2,1},{3,4},{4,3},{5,6},{6,5},{9,10},{10,9},{11,12},{12,11},... | collective-permute-start | bytes 589832 | tf_op jit(solution)/shard_map/ppermute | solution.py:313
  29.4 0.0 collective-permute-done.12.received
  29.4 1.0 %right_products.3 = (f32[3,256,128]{2,1,0:T(8,128)S(1)}, bf16[3,256,128]{2,1,0:T(8,128)(2,1)S(1)}, bf16[3,256,128]{2,1,0:T(8,128)(2,1)S(1)}) custom-call(bf16[2,3,256,1536]{3,2,1,0:T(8,128)(2,1)S(1)} %left_products.1.z_ref, bf16[2,3,128,128]{3,2,1,0:T(8,128)(2,1)S(1)} %collective-permute-done.6.own, ...), custom_call_target="tpu_custom_call" | custom-call | tf_op jit(solution)/shard_map/right_products/pallas_call | solution.py:230
  30.4 1.1 %collective-permute-start.13 = (bf16[3,256,128]{2,1,0:T(8,128)(2,1)S(1)}, bf16[3,256,128]{2,1,0:T(8,128)(2,1)S(1)}, u32[]{:S(2)}, u32[]{:S(2)}) collective-permute-start(bf16[3,256,128]{2,1,0:T(8,128)(2,1)S(1)} %get-tuple-element.35), channel_id=1, source_target_pairs={{0,1},{1,0},{2,3},{3,2},{4,5},{5,4},{6,7},{7,6},{8,9},{9,8},{10,11... | collective-permute-start | bytes 589832 | tf_op jit(solution)/shard_map/ppermute | solution.py:313
  31.5 3.2 %collective-permute-start.14 = (bf16[3,256,128]{2,1,0:T(8,128)(2,1)S(1)}, bf16[3,256,128]{2,1,0:T(8,128)(2,1)S(1)}, u32[]{:S(2)}, u32[]{:S(2)}) collective-permute-start(bf16[3,256,128]{2,1,0:T(8,128)(2,1)S(1)} %get-tuple-element.36), channel_id=1, source_target_pairs={{1,2},{2,1},{3,4},{4,3},{5,6},{6,5},{9,10},{10,9},{11,12},{12,11},... | collective-permute-start | bytes 589832 | tf_op jit(solution)/shard_map/ppermute | solution.py:313
  34.7 5.3 %collective-permute-done.8.refs_1_ = bf16[3,256,128]{2,1,0:T(8,128)(2,1)S(1)} collective-permute-done((bf16[3,256,128]{2,1,0:T(8,128)(2,1)S(1)}, bf16[3,256,128]{2,1,0:T(8,128)(2,1)S(1)}, u32[]{:S(2)}, u32[]{:S(2)}) %collective-permute-start.8) | collective-permute-done | bytes 196640 | tf_op jit(solution)/shard_map/ppermute | solution.py:313
  40.0 5.7 %collective-permute-done.13.refs_4_ = bf16[3,256,128]{2,1,0:T(8,128)(2,1)S(1)} collective-permute-done((bf16[3,256,128]{2,1,0:T(8,128)(2,1)S(1)}, bf16[3,256,128]{2,1,0:T(8,128)(2,1)S(1)}, u32[]{:S(2)}, u32[]{:S(2)}) %collective-permute-start.13) | collective-permute-done | bytes 196640 | tf_op jit(solution)/shard_map/ppermute | solution.py:313
  45.8 0.0 collective-permute-done.14.refs_5_
  45.8 0.9 %summed.1 = bf16[3,256,256]{2,1,0:T(8,128)(2,1)} custom-call(f32[3,256,128]{2,1,0:T(8,128)S(1)} %get-tuple-element.28.refs_0_, bf16[3,256,128]{2,1,0:T(8,128)(2,1)S(1)} %collective-permute-done.8.refs_1_, bf16[3,256,128]{2,1,0:T(8,128)(2,1)S(1)} %collective-permute-done.9.refs_2_, f32[3,256,128]{2,1,0:T(8,128)S(1)} %get-tuple-element.34.refs_3_, ...), custom_call_target="tpu_custom_call" | custom-call | tf_op jit(solution)/shard_map/summed/pallas_call | solution.py:265
  (12 shorter events, 0.1 us)
Async XLA Ops:
  0.0 8.6 %collective-permute-start.4 = (bf16[1,3,128,128]{3,2,1,0:T(8,128)(2,1)}, bf16[1,3,128,128]{3,2,1,0:T(8,128)(2,1)S(1)}, u32[]{:S(2)}, u32[]{:S(2)}) collective-permute-start(bf16[1,3,128,128]{3,2,1,0:T(8,128)(2,1)} %bitcast.6), channel_id=1, source_target_pairs={{4,16},{5,17},{6,18},{7,19},{12,24},{13,25},{14,26},{15,27},{16,4}... | collective-permute-start | bytes 294920 | tf_op jit(solution)/shard_map/ppermute | solution.py:58
  2.9 5.8 %collective-permute-start.3 = (bf16[1,3,128,128]{3,2,1,0:T(8,128)(2,1)}, bf16[1,3,128,128]{3,2,1,0:T(8,128)(2,1)S(1)}, u32[]{:S(2)}, u32[]{:S(2)}) collective-permute-start(bf16[1,3,128,128]{3,2,1,0:T(8,128)(2,1)} %bitcast.7), channel_id=1, source_target_pairs={{0,4},{1,5},{2,6},{3,7},{4,20},{5,21},{6,22},{7,23},{8,12},{9,13},... | collective-permute-start | bytes 294920 | tf_op jit(solution)/shard_map/ppermute | solution.py:58
  4.0 13.2 %collective-permute-start = (bf16[3,272,256]{2,1,0:T(8,128)(2,1)S(1)}, bf16[3,272,256]{2,1,0:T(8,128)(2,1)S(1)}, u32[]{:S(2)}, u32[]{:S(2)}) collective-permute-start(bf16[3,272,256]{2,1,0:T(8,128)(2,1)S(1)} %get-tuple-element.21.refs_0_), channel_id=1, source_target_pairs={{0,16},{8,24},{16,0},{24,8},{1,17},{9,25},{17,1},{25,9},{2,18},{10... | collective-permute-start | bytes 1253384 | tf_op jit(solution)/shard_map/ppermute | solution.py:35
  8.7 9.4 %collective-permute-start.6 = (bf16[2,3,128,128]{3,2,1,0:T(8,128)(2,1)S(1)}, bf16[2,3,128,128]{3,2,1,0:T(8,128)(2,1)S(1)}, u32[]{:S(2)}, u32[]{:S(2)}) collective-permute-start(bf16[2,3,128,128]{3,2,1,0:T(8,128)(2,1)S(1)} %pad_maximum_fusion.own), channel_id=1, source_target_pairs={{0,1},{1,0},{2,3},{3,2},{4,5},{5,4},{6,7},{7,6},{8,9},{9,8},{10,11... | collective-permute-start | bytes 589832 | tf_op jit(solution)/shard_map/ppermute | solution.py:39
  10.0 8.1 %collective-permute-start.5 = (bf16[2,3,128,128]{3,2,1,0:T(8,128)(2,1)S(1)}, bf16[2,3,128,128]{3,2,1,0:T(8,128)(2,1)S(1)}, u32[]{:S(2)}, u32[]{:S(2)}) collective-permute-start(bf16[2,3,128,128]{3,2,1,0:T(8,128)(2,1)S(1)} %pad_maximum_fusion.own), channel_id=1, source_target_pairs={{0,2},{1,3},{2,0},{3,1},{4,6},{5,7},{6,4},{7,5},{8,10},{9,11},{10,... | collective-permute-start | bytes 589832 | tf_op jit(solution)/shard_map/ppermute | solution.py:39
  13.3 8.7 %collective-permute-start.1 = (bf16[3,272,256]{2,1,0:T(8,128)(2,1)S(1)}, bf16[3,272,256]{2,1,0:T(8,128)(2,1)S(1)}, u32[]{:S(2)}, u32[]{:S(2)}) collective-permute-start(bf16[3,272,256]{2,1,0:T(8,128)(2,1)S(1)} %get-tuple-element.21.refs_0_), channel_id=1, source_target_pairs={{0,8},{8,0},{16,24},{24,16},{1,9},{9,1},{17,25},{25,17},{2,10},{10... | collective-permute-start | bytes 1253384 | tf_op jit(solution)/shard_map/ppermute | solution.py:35
  17.2 4.7 %collective-permute-start.2 = (bf16[3,272,256]{2,1,0:T(8,128)(2,1)S(1)}, bf16[3,272,256]{2,1,0:T(8,128)(2,1)S(1)}, u32[]{:S(2)}, u32[]{:S(2)}) collective-permute-start(bf16[3,272,256]{2,1,0:T(8,128)(2,1)S(1)} %collective-permute-done.refs_1_), channel_id=1, source_target_pairs={{0,8},{8,0},{16,24},{24,16},{1,9},{9,1},{17,25},{25,17},{2,10},{10... | collective-permute-start | bytes 1253384 | tf_op jit(solution)/shard_map/ppermute | solution.py:35
  18.2 5.4 %collective-permute-start.7 = (bf16[2,3,128,128]{3,2,1,0:T(8,128)(2,1)S(1)}, bf16[2,3,128,128]{3,2,1,0:T(8,128)(2,1)S(1)}, u32[]{:S(2)}, u32[]{:S(2)}) collective-permute-start(bf16[2,3,128,128]{3,2,1,0:T(8,128)(2,1)S(1)} %broadcast_select_fusion.1), channel_id=1, source_target_pairs={{0,8},{8,0},{16,24},{24,16},{1,9},{9,1},{17,25},{25,17},{2,10},{10... | collective-permute-start | bytes 589832 | tf_op jit(solution)/shard_map/ppermute | solution.py:35
  19.2 5.4 %collective-permute-start.10 = (bf16[1,3,128,128]{3,2,1,0:T(8,128)(2,1)S(1)}, bf16[1,3,128,128]{3,2,1,0:T(8,128)(2,1)S(1)}, u32[]{:S(2)}, u32[]{:S(2)}) collective-permute-start(bf16[1,3,128,128]{3,2,1,0:T(8,128)(2,1)S(1)} %slice.6), channel_id=1, source_target_pairs={{0,2},{1,3},{2,0},{3,1},{4,6},{5,7},{6,4},{7,5},{8,10},{9,11},{10,... | collective-permute-start | bytes 294920 | tf_op jit(solution)/shard_map/ppermute | solution.py:39
  20.8 3.9 %collective-permute-start.11 = (bf16[1,3,128,128]{3,2,1,0:T(8,128)(2,1)S(1)}, bf16[1,3,128,128]{3,2,1,0:T(8,128)(2,1)S(1)}, u32[]{:S(2)}, u32[]{:S(2)}) collective-permute-start(bf16[1,3,128,128]{3,2,1,0:T(8,128)(2,1)S(1)} %slice.7), channel_id=1, source_target_pairs={{0,1},{1,0},{2,3},{3,2},{4,5},{5,4},{6,7},{7,6},{8,9},{9,8},{10,11... | collective-permute-start | bytes 294920 | tf_op jit(solution)/shard_map/ppermute | solution.py:39
  24.7 4.7 %collective-permute-start.12 = (bf16[2,3,128,128]{3,2,1,0:T(8,128)(2,1)S(1)}, bf16[2,3,128,128]{3,2,1,0:T(8,128)(2,1)S(1)}, u32[]{:S(2)}, u32[]{:S(2)}) collective-permute-start(bf16[2,3,128,128]{3,2,1,0:T(8,128)(2,1)S(1)} %broadcast_select_fusion), channel_id=1, source_target_pairs={{0,8},{8,0},{16,24},{24,16},{1,9},{9,1},{17,25},{25,17},{2,10},{10... | collective-permute-start | bytes 589832 | tf_op jit(solution)/shard_map/ppermute | solution.py:35
  26.2 13.8 %collective-permute-start.8 = (bf16[3,256,128]{2,1,0:T(8,128)(2,1)S(1)}, bf16[3,256,128]{2,1,0:T(8,128)(2,1)S(1)}, u32[]{:S(2)}, u32[]{:S(2)}) collective-permute-start(bf16[3,256,128]{2,1,0:T(8,128)(2,1)S(1)} %get-tuple-element.29), channel_id=1, source_target_pairs={{0,1},{1,0},{2,3},{3,2},{4,5},{5,4},{6,7},{7,6},{8,9},{9,8},{10,11... | collective-permute-start | bytes 589832 | tf_op jit(solution)/shard_map/ppermute | solution.py:313
  27.5 12.6 %collective-permute-start.9 = (bf16[3,256,128]{2,1,0:T(8,128)(2,1)S(1)}, bf16[3,256,128]{2,1,0:T(8,128)(2,1)S(1)}, u32[]{:S(2)}, u32[]{:S(2)}) collective-permute-start(bf16[3,256,128]{2,1,0:T(8,128)(2,1)S(1)} %get-tuple-element.30), channel_id=1, source_target_pairs={{1,2},{2,1},{3,4},{4,3},{5,6},{6,5},{9,10},{10,9},{11,12},{12,11},... | collective-permute-start | bytes 589832 | tf_op jit(solution)/shard_map/ppermute | solution.py:313
  30.4 15.4 %collective-permute-start.13 = (bf16[3,256,128]{2,1,0:T(8,128)(2,1)S(1)}, bf16[3,256,128]{2,1,0:T(8,128)(2,1)S(1)}, u32[]{:S(2)}, u32[]{:S(2)}) collective-permute-start(bf16[3,256,128]{2,1,0:T(8,128)(2,1)S(1)} %get-tuple-element.35), channel_id=1, source_target_pairs={{0,1},{1,0},{2,3},{3,2},{4,5},{5,4},{6,7},{7,6},{8,9},{9,8},{10,11... | collective-permute-start | bytes 589832 | tf_op jit(solution)/shard_map/ppermute | solution.py:313
  31.5 14.3 %collective-permute-start.14 = (bf16[3,256,128]{2,1,0:T(8,128)(2,1)S(1)}, bf16[3,256,128]{2,1,0:T(8,128)(2,1)S(1)}, u32[]{:S(2)}, u32[]{:S(2)}) collective-permute-start(bf16[3,256,128]{2,1,0:T(8,128)(2,1)S(1)} %get-tuple-element.36), channel_id=1, source_target_pairs={{1,2},{2,1},{3,4},{4,3},{5,6},{6,5},{9,10},{10,9},{11,12},{12,11},... | collective-permute-start | bytes 589832 | tf_op jit(solution)/shard_map/ppermute | solution.py:313

commit v5 on v4

--- a/solution.py
+++ b/solution.py
@@ -94,21 +94,25 @@
 
 
 def shift_of(left, inner):
-    return jnp.max(left[inner, ML:, :MR].astype(jnp.float32)).astype(jnp.int32)
+    row = left.shape[0] - TILE + inner
+    return jnp.max(left[row : row + 1, :MR].astype(jnp.float32)).astype(jnp.int32)
 
 
 def pack_kernel(shift, left, right, packed, kept, shift_ref, sems):
+    rows = left.shape[0]
     copies = [
         pltpu.make_async_copy(shift, shift_ref, sems.at[0]),
-        pltpu.make_async_copy(left, packed.at[:, pl.ds(0, ML)], sems.at[1]),
+        pltpu.make_async_copy(left, packed.at[pl.ds(0, rows)], sems.at[1]),
         pltpu.make_async_copy(right, kept, sems.at[2]),
     ]
     for copy in copies:
         copy.start()
     copies[0].wait()
-    for inner in range(left.shape[0]):
-        tag = jnp.full((TILE, ML), shift_ref[inner].astype(jnp.float32)).astype(jnp.bfloat16)
-        packed[inner, ML:] = tag
+    row = lax.broadcasted_iota(jnp.int32, (TILE, ML), 0)
+    tags = jnp.zeros((TILE, ML), jnp.float32)
+    for inner in range(rows // ML):
+        tags = jnp.where(row == inner, shift_ref[inner].astype(jnp.float32), tags)
+    packed[rows:] = tags.astype(jnp.bfloat16)
     for copy in copies[1:]:
         copy.wait()
 
@@ -116,7 +120,7 @@
 def pack(shift, left, right):
     return pl.pallas_call(
         pack_kernel,
-        out_shape=[in_vmem((left.shape[0], ML + TILE, ML)), in_vmem(right.shape)],
+        out_shape=[in_vmem((left.shape[0] + TILE, ML)), in_vmem(right.shape)],
         in_specs=[HBM] * 3,
         out_specs=[VMEM] * 2,
         scratch_shapes=[pltpu.SMEM(shift.shape, jnp.int32), pltpu.SemaphoreType.DMA((3,))],
@@ -171,21 +175,21 @@
     *lefts, window, z_ref = refs
     per = z_ref.shape[0]
     width = per * MR
-    terms = lefts[0].shape[0]
+    terms = lefts[0].shape[0] // ML
     for piece, left in enumerate(lefts):
         for inner in range(terms):
             term = piece * terms + inner
             offset = pl.multiple_of((1 + shift_of(left, inner)) * MR, MR)
             for v in range(VECS):
                 z = jnp.dot(
-                    left[inner, :ML], window[v, :, pl.ds(offset, width)], preferred_element_type=jnp.float32
+                    left[inner * ML : (inner + 1) * ML], window[v, :, pl.ds(offset, width)], preferred_element_type=jnp.float32
                 ).astype(jnp.bfloat16)
                 for column in range(per):
                     z_ref[column, v, :, term * MR : (term + 1) * MR] = z[:, column * MR : (column + 1) * MR]
 
 
 def left_products(lefts, window):
-    terms = len(lefts) * lefts[0].shape[0]
+    terms = len(lefts) * (lefts[0].shape[0] // ML)
     width = window.shape[2] - 2 * MR
     return pl.pallas_call(
         left_kernel,
@@ -240,33 +244,39 @@
 
 
 def sum_kernel(per, *refs):
-    *parts, out_ref = refs
+    *parts, out_hbm, out_ref, sems = refs
     zeros, lows, highs = parts[::3], parts[1::3], parts[2::3]
     sec = lax.axis_index("sec")
     beyond = (sec ^ ((((sec + 1) ^ 1) + per - 1) % per)) % per
+    copies = [pltpu.make_async_copy(out_ref.at[v], out_hbm.at[v], sems.at[v]) for v in range(VECS)]
 
     def add(high):
         @pl.when(beyond == high)
         def _():
-            for cls in range(per):
-                column = pl.multiple_of(((sec % per) ^ cls) * MR, MR)
-                for v in range(VECS):
-                    total = zeros[cls][v] + lows[cls ^ 1][v].astype(jnp.float32)
+            for v in range(VECS):
+                for cls in range(per):
+                    column = pl.multiple_of(((sec % per) ^ cls) * MR, MR)
+                    total = zeros[cls][v].astype(jnp.float32) + lows[cls ^ 1][v].astype(jnp.float32)
                     total = total + highs[cls ^ high][v].astype(jnp.float32)
                     out_ref[v, :, pl.ds(column, MR)] = total.astype(jnp.bfloat16)
+                copies[v].start()
 
     carry = 1
     while carry < per:
         add(carry)
         carry = 2 * carry + 1
+    for copy in copies:
+        copy.wait()
 
 
 def summed(per, parts):
+    shape = (VECS, ML, per * MR)
     return pl.pallas_call(
         functools.partial(sum_kernel, per),
-        out_shape=jax.ShapeDtypeStruct((VECS, ML, per * MR), jnp.bfloat16),
+        out_shape=jax.ShapeDtypeStruct(shape, jnp.bfloat16),
         in_specs=[VMEM] * len(parts),
-        out_specs=VMEM,
+        out_specs=HBM,
+        scratch_shapes=[in_vmem(shape), pltpu.SemaphoreType.DMA((VECS,))],
         compiler_params=grant(8),
         name="summed",
     )(*parts)
@@ -277,7 +287,7 @@
     tie = lax.optimization_barrier
     matching = lax.axis_index("op") ^ (lax.axis_index("sec") // per)
     held = right_ops.reshape((1,) + right_ops.shape[:1] + right_ops.shape[2:])
-    packed, kept = pack(term_shift, left_ops.transpose(1, 0, 2), held)
+    packed, kept = pack(term_shift, left_ops.transpose(1, 0, 2).reshape(-1, ML), held)
     window = window_of(wavefunction.transpose(1, 0, 2), n_op)
     lefts = [packed]
     bit = n_op // 2
@@ -312,7 +322,7 @@
         zero, to_low, to_high = right_products(cls, per, z, own, other, received, lefts)
         parts += [zero, lax.ppermute(to_low, "sec", low), lax.ppermute(to_high, "sec", high)]
         if later is not None:
-            later, _ = tie((later, zero))
+            later, parts[-3] = tie((later, zero.astype(jnp.bfloat16)))
             other = jnp.concatenate(later)
             others.append(other)
     return summed(per, parts).transpose(1, 0, 2)

time: 46.9 us -> 46.2 us (0.985); the launches traced: 46.7 us -> 45.4 us
  starting transfers between devices: 25 us -> 24.3 us
    ppermute x2, starting transfers between devices: 5.1 us -> 4.09 us  [on_device(): lax.ppermute(to_high, 'sec', high)]
    ppermute x2, starting transfers between devices: 2.4 us -> 3.07 us  [on_device(): lax.ppermute(to_low, 'sec', low)]
  transfers between devices with their start and end apart: 15 -> 15, of which waited for: 3 -> 3; matrix products, arithmetic and copies ran while one was open for 0% -> 0% of each run, Pallas kernels for 14% -> 15%
where the time goes in v5:
time: 46.2 us; the launch traced here: 45.4 us
  starting transfers between devices  24.3 us (53%)
  waiting for transfers between devices  13.4 us (29%)
  Pallas kernels  7.41 us (16%)
    ppermute x2, waiting for transfers between devices, on_device(): lax.ppermute(to_low, 'sec', low)  11 us
    ppermute x5, starting transfers between devices, over_op(): return lax.ppermute(x, 'op', [(o, o ^ bit) for o in range(n_op)])  7.25 us
    ppermute x4, starting transfers between devices, over_sec(): return lax.ppermute(x, 'sec', [(d, d ^ bit) for d in range(n_sec)])  6.94 us
    ppermute x2, starting transfers between devices, on_device(): lax.ppermute(to_high, 'sec', high)  4.09 us
    ppermute x2, starting transfers between devices, on_device(): lax.ppermute(to_low, 'sec', low)  3.07 us
    ppermute x1, starting transfers between devices, towards_owner(): lax.ppermute(held, ('op', 'sec'), second)  2.88 us
    ppermute x5, waiting for transfers between devices, over_op(): return lax.ppermute(x, 'op', [(o, o ^ bit) for o in range(n_op)])  2.42 us
    pallas_call x1, Pallas kernels, window_of(): pl.pallas_call(functools.partial(window_kernel, n_op), out_shape=in_vmem(...  2 us
  transfers between devices with their start and end apart: 15, of which 3 were waited for; matrix products, arithmetic and copies ran while one was open for 0% of the time, Pallas kernels for 15%

profile of v5, /device:TPU:17, one launch (start us, length us, event | category | flops | bytes accessed | tf_op | source)
XLA Modules:
  0.0 45.4 jit_solution(1428231674326179582)
XLA Ops:
  0.0 2.9 %collective-permute-start.1 = (bf16[1,3,128,128]{3,2,1,0:T(8,128)(2,1)}, bf16[1,3,128,128]{3,2,1,0:T(8,128)(2,1)S(1)}, u32[]{:S(2)}, u32[]{:S(2)}) collective-permute-start(bf16[1,3,128,128]{3,2,1,0:T(8,128)(2,1)} %bitcast.8), channel_id=1, source_target_pairs={{4,16},{5,17},{6,18},{7,19},{12,24},{13,25},{14,26},{15,27},{16,4}... | collective-permute-start | bytes 294920 | tf_op jit(solution)/shard_map/ppermute | solution.py:58
  2.9 0.1 collective-permute-start
  3.0 1.0 %pack.1 = (bf16[784,256]{1,0:T(8,128)(2,1)S(1)}, bf16[1,3,128,128]{3,2,1,0:T(8,128)(2,1)S(1)}) custom-call(s32[3]{0:T(128)} %shift.1, bf16[768,256]{1,0:T(8,128)(2,1)} %bitcast.7, bf16[1,3,128,128]{3,2,1,0:T(8,128)(2,1)} %bitcast.10), custom_call_target="tpu_custom_call" | custom-call | bytes 33554432 | tf_op jit(solution)/shard_map/pack/pallas_call | solution.py:121
  4.0 2.6 %collective-permute-start.6 = (bf16[784,256]{1,0:T(8,128)(2,1)S(1)}, bf16[784,256]{1,0:T(8,128)(2,1)S(1)}, u32[]{:S(2)}, u32[]{:S(2)}) collective-permute-start(bf16[784,256]{1,0:T(8,128)(2,1)S(1)} %get-tuple-element.27.refs_0_), channel_id=1, source_target_pairs={{0,16},{8,24},{16,0},{24,8},{1,17},{9,25},{17,1},{25,9},{2,18},{10... | collective-permute-start | bytes 1204232 | tf_op jit(solution)/shard_map/ppermute | solution.py:35
  6.6 2.0 %window.1.refs_4_ = bf16[3,256,512]{2,1,0:T(8,128)(2,1)S(1)} custom-call(bf16[3,256,1024]{2,1,0:T(8,128)(2,1)} %bitcast.6), custom_call_target="tpu_custom_call" | custom-call | bytes 2097152 | tf_op jit(solution)/shard_map/window/pallas_call | solution.py:162
  8.6 0.0 collective-permute-done.1
  8.6 0.0 collective-permute-done
  8.7 1.3 %collective-permute-start.3 = (bf16[2,3,128,128]{3,2,1,0:T(8,128)(2,1)S(1)}, bf16[2,3,128,128]{3,2,1,0:T(8,128)(2,1)S(1)}, u32[]{:S(2)}, u32[]{:S(2)}) collective-permute-start(bf16[2,3,128,128]{3,2,1,0:T(8,128)(2,1)S(1)} %pad_maximum_fusion.own), channel_id=1, source_target_pairs={{0,1},{1,0},{2,3},{3,2},{4,5},{5,4},{6,7},{7,6},{8,9},{9,8},{10,11... | collective-permute-start | bytes 589832 | tf_op jit(solution)/shard_map/ppermute | solution.py:39
  10.0 3.2 %collective-permute-start.2 = (bf16[2,3,128,128]{3,2,1,0:T(8,128)(2,1)S(1)}, bf16[2,3,128,128]{3,2,1,0:T(8,128)(2,1)S(1)}, u32[]{:S(2)}, u32[]{:S(2)}) collective-permute-start(bf16[2,3,128,128]{3,2,1,0:T(8,128)(2,1)S(1)} %pad_maximum_fusion.own), channel_id=1, source_target_pairs={{0,2},{1,3},{2,0},{3,1},{4,6},{5,7},{6,4},{7,5},{8,10},{9,11},{10,... | collective-permute-start | bytes 589832 | tf_op jit(solution)/shard_map/ppermute | solution.py:39
  13.3 1.2 %collective-permute-start.7 = (bf16[784,256]{1,0:T(8,128)(2,1)S(1)}, bf16[784,256]{1,0:T(8,128)(2,1)S(1)}, u32[]{:S(2)}, u32[]{:S(2)}) collective-permute-start(bf16[784,256]{1,0:T(8,128)(2,1)S(1)} %get-tuple-element.27.refs_0_), channel_id=1, source_target_pairs={{0,8},{8,0},{16,24},{24,16},{1,9},{9,1},{17,25},{25,17},{2,10},{10... | collective-permute-start | bytes 1204232 | tf_op jit(solution)/shard_map/ppermute | solution.py:35
  14.5 2.4 %collective-permute-done.6.refs_1_ = bf16[784,256]{1,0:T(8,128)(2,1)S(1)} collective-permute-done((bf16[784,256]{1,0:T(8,128)(2,1)S(1)}, bf16[784,256]{1,0:T(8,128)(2,1)S(1)}, u32[]{:S(2)}, u32[]{:S(2)}) %collective-permute-start.6) | collective-permute-done | bytes 401440 | tf_op jit(solution)/shard_map/ppermute | solution.py:35
  16.9 0.9 %collective-permute-start.8 = (bf16[784,256]{1,0:T(8,128)(2,1)S(1)}, bf16[784,256]{1,0:T(8,128)(2,1)S(1)}, u32[]{:S(2)}, u32[]{:S(2)}) collective-permute-start(bf16[784,256]{1,0:T(8,128)(2,1)S(1)} %collective-permute-done.6.refs_1_), channel_id=1, source_target_pairs={{0,8},{8,0},{16,24},{24,16},{1,9},{9,1},{17,25},{25,17},{2,10},{10... | collective-permute-start | bytes 1204232 | tf_op jit(solution)/shard_map/ppermute | solution.py:35
  17.8 0.0 collective-permute-done.3.own
  17.8 1.4 %collective-permute-start.9 = (bf16[2,3,128,128]{3,2,1,0:T(8,128)(2,1)S(1)}, bf16[2,3,128,128]{3,2,1,0:T(8,128)(2,1)S(1)}, u32[]{:S(2)}, u32[]{:S(2)}) collective-permute-start(bf16[2,3,128,128]{3,2,1,0:T(8,128)(2,1)S(1)} %broadcast_select_fusion.1), channel_id=1, source_target_pairs={{0,8},{8,0},{16,24},{24,16},{1,9},{9,1},{17,25},{25,17},{2,10},{10... | collective-permute-start | bytes 589832 | tf_op jit(solution)/shard_map/ppermute | solution.py:35
  19.2 0.3 collective-permute-start.5
  19.5 2.1 %collective-permute-start.4 = (bf16[1,3,128,128]{3,2,1,0:T(8,128)(2,1)S(1)}, bf16[1,3,128,128]{3,2,1,0:T(8,128)(2,1)S(1)}, u32[]{:S(2)}, u32[]{:S(2)}) collective-permute-start(bf16[1,3,128,128]{3,2,1,0:T(8,128)(2,1)S(1)} %slice.6), channel_id=1, source_target_pairs={{0,2},{1,3},{2,0},{3,1},{4,6},{5,7},{6,4},{7,5},{8,10},{9,11},{10,... | collective-permute-start | bytes 294920 | tf_op jit(solution)/shard_map/ppermute | solution.py:39
  21.6 0.0 collective-permute-done.7.refs_2_
  21.6 0.0 collective-permute-done.8.refs_3_
  21.6 1.6 %left_products.1.z_ref = bf16[2,3,256,1536]{3,2,1,0:T(8,128)(2,1)S(1)} custom-call(bf16[784,256]{1,0:T(8,128)(2,1)S(1)} %get-tuple-element.27.refs_0_, bf16[784,256]{1,0:T(8,128)(2,1)S(1)} %collective-permute-done.6.refs_1_, bf16[784,256]{1,0:T(8,128)(2,1)S(1)} %collective-permute-done.7.refs_2_, bf16[784,256]{1,0:T(8,128)(2,1)S(1)} %collective-permute-done.8.refs_3_, ...), custom_call_target="tpu_custom_call" | custom-call | flops 1207959552 | bytes 1048576 | tf_op jit(solution)/shard_map/left_products/pallas_call | solution.py:194
  23.3 1.0 %right_products.2 = (f32[3,256,128]{2,1,0:T(8,128)S(1)}, bf16[3,256,128]{2,1,0:T(8,128)(2,1)S(1)}, bf16[3,256,128]{2,1,0:T(8,128)(2,1)S(1)}) custom-call(bf16[2,3,256,1536]{3,2,1,0:T(8,128)(2,1)S(1)} %left_products.1.z_ref, bf16[2,3,128,128]{3,2,1,0:T(8,128)(2,1)S(1)} %pad_maximum_fusion.own, bf16[2,3,128,128]{3,2,1,0:T(8,128)(2,1)S(1)} %collective-permute-done.2.other, ...), custom_call_target="tpu_custom_call" | custom-call | tf_op jit(solution)/shard_map/right_products/pallas_call | solution.py:234
  24.3 0.0 collective-permute-done.4
  24.4 1.1 %collective-permute-start.12 = (bf16[2,3,128,128]{3,2,1,0:T(8,128)(2,1)S(1)}, bf16[2,3,128,128]{3,2,1,0:T(8,128)(2,1)S(1)}, u32[]{:S(2)}, u32[]{:S(2)}) collective-permute-start(bf16[2,3,128,128]{3,2,1,0:T(8,128)(2,1)S(1)} %broadcast_select_fusion), channel_id=1, source_target_pairs={{0,8},{8,0},{16,24},{24,16},{1,9},{9,1},{17,25},{25,17},{2,10},{10... | collective-permute-start | bytes 589832 | tf_op jit(solution)/shard_map/ppermute | solution.py:35
  25.5 0.6 %collective-permute-start.10 = (bf16[3,256,128]{2,1,0:T(8,128)(2,1)S(1)}, bf16[3,256,128]{2,1,0:T(8,128)(2,1)S(1)}, u32[]{:S(2)}, u32[]{:S(2)}) collective-permute-start(bf16[3,256,128]{2,1,0:T(8,128)(2,1)S(1)} %get-tuple-element.32), channel_id=1, source_target_pairs={{0,1},{1,0},{2,3},{3,2},{4,5},{5,4},{6,7},{7,6},{8,9},{9,8},{10,11... | collective-permute-start | bytes 589832 | tf_op jit(solution)/shard_map/ppermute | solution.py:323
  26.1 2.2 %collective-permute-start.11 = (bf16[3,256,128]{2,1,0:T(8,128)(2,1)S(1)}, bf16[3,256,128]{2,1,0:T(8,128)(2,1)S(1)}, u32[]{:S(2)}, u32[]{:S(2)}) collective-permute-start(bf16[3,256,128]{2,1,0:T(8,128)(2,1)S(1)} %get-tuple-element.33), channel_id=1, source_target_pairs={{1,2},{2,1},{3,4},{4,3},{5,6},{6,5},{9,10},{10,9},{11,12},{12,11},... | collective-permute-start | bytes 589832 | tf_op jit(solution)/shard_map/ppermute | solution.py:323
  28.3 0.0 collective-permute-done.12.received
  28.3 1.0 %right_products.3 = (f32[3,256,128]{2,1,0:T(8,128)S(1)}, bf16[3,256,128]{2,1,0:T(8,128)(2,1)S(1)}, bf16[3,256,128]{2,1,0:T(8,128)(2,1)S(1)}) custom-call(bf16[2,3,256,1536]{3,2,1,0:T(8,128)(2,1)S(1)} %left_products.1.z_ref, bf16[2,3,128,128]{3,2,1,0:T(8,128)(2,1)S(1)} %collective-permute-done.3.own, ...), custom_call_target="tpu_custom_call" | custom-call | tf_op jit(solution)/shard_map/right_products/pallas_call | solution.py:234
  29.3 2.4 %collective-permute-start.13 = (bf16[3,256,128]{2,1,0:T(8,128)(2,1)S(1)}, bf16[3,256,128]{2,1,0:T(8,128)(2,1)S(1)}, u32[]{:S(2)}, u32[]{:S(2)}) collective-permute-start(bf16[3,256,128]{2,1,0:T(8,128)(2,1)S(1)} %get-tuple-element.37), channel_id=1, source_target_pairs={{0,1},{1,0},{2,3},{3,2},{4,5},{5,4},{6,7},{7,6},{8,9},{9,8},{10,11... | collective-permute-start | bytes 589832 | tf_op jit(solution)/shard_map/ppermute | solution.py:323
  31.7 1.9 %collective-permute-start.14 = (bf16[3,256,128]{2,1,0:T(8,128)(2,1)S(1)}, bf16[3,256,128]{2,1,0:T(8,128)(2,1)S(1)}, u32[]{:S(2)}, u32[]{:S(2)}) collective-permute-start(bf16[3,256,128]{2,1,0:T(8,128)(2,1)S(1)} %get-tuple-element.38), channel_id=1, source_target_pairs={{1,2},{2,1},{3,4},{4,3},{5,6},{6,5},{9,10},{10,9},{11,12},{12,11},... | collective-permute-start | bytes 589832 | tf_op jit(solution)/shard_map/ppermute | solution.py:323
  33.6 2.5 %collective-permute-done.10.refs_1_ = bf16[3,256,128]{2,1,0:T(8,128)(2,1)S(1)} collective-permute-done((bf16[3,256,128]{2,1,0:T(8,128)(2,1)S(1)}, bf16[3,256,128]{2,1,0:T(8,128)(2,1)S(1)}, u32[]{:S(2)}, u32[]{:S(2)}) %collective-permute-start.10) | collective-permute-done | bytes 196640 | tf_op jit(solution)/shard_map/ppermute | solution.py:323
  36.2 0.0 collective-permute-done.11.refs_2_
  36.2 8.4 %collective-permute-done.13.refs_4_ = bf16[3,256,128]{2,1,0:T(8,128)(2,1)S(1)} collective-permute-done((bf16[3,256,128]{2,1,0:T(8,128)(2,1)S(1)}, bf16[3,256,128]{2,1,0:T(8,128)(2,1)S(1)}, u32[]{:S(2)}, u32[]{:S(2)}) %collective-permute-start.13) | collective-permute-done | bytes 196640 | tf_op jit(solution)/shard_map/ppermute | solution.py:323
  44.6 0.8 %summed.1 = bf16[3,256,256]{2,1,0:T(8,128)(2,1)} custom-call(bf16[3,256,128]{2,1,0:T(8,128)(2,1)S(1)} %convert_element_type.3.refs_0_, bf16[3,256,128]{2,1,0:T(8,128)(2,1)S(1)} %collective-permute-done.10.refs_1_, bf16[3,256,128]{2,1,0:T(8,128)(2,1)S(1)} %collective-permute-done.11.refs_2_, f32[3,256,128]{2,1,0:T(8,128)S(1)} %get-tuple-element.36.refs_3_, ...), custom_call_target="tpu_custom_call" | custom-call | tf_op jit(solution)/shard_map/summed/pallas_call | solution.py:274
  (13 shorter events, 0.2 us)
Async XLA Ops:
  0.0 8.6 %collective-permute-start.1 = (bf16[1,3,128,128]{3,2,1,0:T(8,128)(2,1)}, bf16[1,3,128,128]{3,2,1,0:T(8,128)(2,1)S(1)}, u32[]{:S(2)}, u32[]{:S(2)}) collective-permute-start(bf16[1,3,128,128]{3,2,1,0:T(8,128)(2,1)} %bitcast.8), channel_id=1, source_target_pairs={{4,16},{5,17},{6,18},{7,19},{12,24},{13,25},{14,26},{15,27},{16,4}... | collective-permute-start | bytes 294920 | tf_op jit(solution)/shard_map/ppermute | solution.py:58
  2.9 5.8 %collective-permute-start = (bf16[1,3,128,128]{3,2,1,0:T(8,128)(2,1)}, bf16[1,3,128,128]{3,2,1,0:T(8,128)(2,1)S(1)}, u32[]{:S(2)}, u32[]{:S(2)}) collective-permute-start(bf16[1,3,128,128]{3,2,1,0:T(8,128)(2,1)} %bitcast.9), channel_id=1, source_target_pairs={{0,4},{1,5},{2,6},{3,7},{4,20},{5,21},{6,22},{7,23},{8,12},{9,13},... | collective-permute-start | bytes 294920 | tf_op jit(solution)/shard_map/ppermute | solution.py:58
  4.0 12.9 %collective-permute-start.6 = (bf16[784,256]{1,0:T(8,128)(2,1)S(1)}, bf16[784,256]{1,0:T(8,128)(2,1)S(1)}, u32[]{:S(2)}, u32[]{:S(2)}) collective-permute-start(bf16[784,256]{1,0:T(8,128)(2,1)S(1)} %get-tuple-element.27.refs_0_), channel_id=1, source_target_pairs={{0,16},{8,24},{16,0},{24,8},{1,17},{9,25},{17,1},{25,9},{2,18},{10... | collective-permute-start | bytes 1204232 | tf_op jit(solution)/shard_map/ppermute | solution.py:35
  8.7 9.1 %collective-permute-start.3 = (bf16[2,3,128,128]{3,2,1,0:T(8,128)(2,1)S(1)}, bf16[2,3,128,128]{3,2,1,0:T(8,128)(2,1)S(1)}, u32[]{:S(2)}, u32[]{:S(2)}) collective-permute-start(bf16[2,3,128,128]{3,2,1,0:T(8,128)(2,1)S(1)} %pad_maximum_fusion.own), channel_id=1, source_target_pairs={{0,1},{1,0},{2,3},{3,2},{4,5},{5,4},{6,7},{7,6},{8,9},{9,8},{10,11... | collective-permute-start | bytes 589832 | tf_op jit(solution)/shard_map/ppermute | solution.py:39
  10.0 7.8 %collective-permute-start.2 = (bf16[2,3,128,128]{3,2,1,0:T(8,128)(2,1)S(1)}, bf16[2,3,128,128]{3,2,1,0:T(8,128)(2,1)S(1)}, u32[]{:S(2)}, u32[]{:S(2)}) collective-permute-start(bf16[2,3,128,128]{3,2,1,0:T(8,128)(2,1)S(1)} %pad_maximum_fusion.own), channel_id=1, source_target_pairs={{0,2},{1,3},{2,0},{3,1},{4,6},{5,7},{6,4},{7,5},{8,10},{9,11},{10,... | collective-permute-start | bytes 589832 | tf_op jit(solution)/shard_map/ppermute | solution.py:39
  13.3 8.4 %collective-permute-start.7 = (bf16[784,256]{1,0:T(8,128)(2,1)S(1)}, bf16[784,256]{1,0:T(8,128)(2,1)S(1)}, u32[]{:S(2)}, u32[]{:S(2)}) collective-permute-start(bf16[784,256]{1,0:T(8,128)(2,1)S(1)} %get-tuple-element.27.refs_0_), channel_id=1, source_target_pairs={{0,8},{8,0},{16,24},{24,16},{1,9},{9,1},{17,25},{25,17},{2,10},{10... | collective-permute-start | bytes 1204232 | tf_op jit(solution)/shard_map/ppermute | solution.py:35
  16.9 4.7 %collective-permute-start.8 = (bf16[784,256]{1,0:T(8,128)(2,1)S(1)}, bf16[784,256]{1,0:T(8,128)(2,1)S(1)}, u32[]{:S(2)}, u32[]{:S(2)}) collective-permute-start(bf16[784,256]{1,0:T(8,128)(2,1)S(1)} %collective-permute-done.6.refs_1_), channel_id=1, source_target_pairs={{0,8},{8,0},{16,24},{24,16},{1,9},{9,1},{17,25},{25,17},{2,10},{10... | collective-permute-start | bytes 1204232 | tf_op jit(solution)/shard_map/ppermute | solution.py:35
  17.8 5.4 %collective-permute-start.9 = (bf16[2,3,128,128]{3,2,1,0:T(8,128)(2,1)S(1)}, bf16[2,3,128,128]{3,2,1,0:T(8,128)(2,1)S(1)}, u32[]{:S(2)}, u32[]{:S(2)}) collective-permute-start(bf16[2,3,128,128]{3,2,1,0:T(8,128)(2,1)S(1)} %broadcast_select_fusion.1), channel_id=1, source_target_pairs={{0,8},{8,0},{16,24},{24,16},{1,9},{9,1},{17,25},{25,17},{2,10},{10... | collective-permute-start | bytes 589832 | tf_op jit(solution)/shard_map/ppermute | solution.py:35
  19.2 5.0 %collective-permute-start.5 = (bf16[1,3,128,128]{3,2,1,0:T(8,128)(2,1)S(1)}, bf16[1,3,128,128]{3,2,1,0:T(8,128)(2,1)S(1)}, u32[]{:S(2)}, u32[]{:S(2)}) collective-permute-start(bf16[1,3,128,128]{3,2,1,0:T(8,128)(2,1)S(1)} %slice.7), channel_id=1, source_target_pairs={{0,1},{1,0},{2,3},{3,2},{4,5},{5,4},{6,7},{7,6},{8,9},{9,8},{10,11... | collective-permute-start | bytes 294920 | tf_op jit(solution)/shard_map/ppermute | solution.py:39
  19.5 4.8 %collective-permute-start.4 = (bf16[1,3,128,128]{3,2,1,0:T(8,128)(2,1)S(1)}, bf16[1,3,128,128]{3,2,1,0:T(8,128)(2,1)S(1)}, u32[]{:S(2)}, u32[]{:S(2)}) collective-permute-start(bf16[1,3,128,128]{3,2,1,0:T(8,128)(2,1)S(1)} %slice.6), channel_id=1, source_target_pairs={{0,2},{1,3},{2,0},{3,1},{4,6},{5,7},{6,4},{7,5},{8,10},{9,11},{10,... | collective-permute-start | bytes 294920 | tf_op jit(solution)/shard_map/ppermute | solution.py:39
  24.4 4.0 %collective-permute-start.12 = (bf16[2,3,128,128]{3,2,1,0:T(8,128)(2,1)S(1)}, bf16[2,3,128,128]{3,2,1,0:T(8,128)(2,1)S(1)}, u32[]{:S(2)}, u32[]{:S(2)}) collective-permute-start(bf16[2,3,128,128]{3,2,1,0:T(8,128)(2,1)S(1)} %broadcast_select_fusion), channel_id=1, source_target_pairs={{0,8},{8,0},{16,24},{24,16},{1,9},{9,1},{17,25},{25,17},{2,10},{10... | collective-permute-start | bytes 589832 | tf_op jit(solution)/shard_map/ppermute | solution.py:35
  25.5 10.7 %collective-permute-start.10 = (bf16[3,256,128]{2,1,0:T(8,128)(2,1)S(1)}, bf16[3,256,128]{2,1,0:T(8,128)(2,1)S(1)}, u32[]{:S(2)}, u32[]{:S(2)}) collective-permute-start(bf16[3,256,128]{2,1,0:T(8,128)(2,1)S(1)} %get-tuple-element.32), channel_id=1, source_target_pairs={{0,1},{1,0},{2,3},{3,2},{4,5},{5,4},{6,7},{7,6},{8,9},{9,8},{10,11... | collective-permute-start | bytes 589832 | tf_op jit(solution)/shard_map/ppermute | solution.py:323
  26.1 10.1 %collective-permute-start.11 = (bf16[3,256,128]{2,1,0:T(8,128)(2,1)S(1)}, bf16[3,256,128]{2,1,0:T(8,128)(2,1)S(1)}, u32[]{:S(2)}, u32[]{:S(2)}) collective-permute-start(bf16[3,256,128]{2,1,0:T(8,128)(2,1)S(1)} %get-tuple-element.33), channel_id=1, source_target_pairs={{1,2},{2,1},{3,4},{4,3},{5,6},{6,5},{9,10},{10,9},{11,12},{12,11},... | collective-permute-start | bytes 589832 | tf_op jit(solution)/shard_map/ppermute | solution.py:323
  29.3 15.3 %collective-permute-start.13 = (bf16[3,256,128]{2,1,0:T(8,128)(2,1)S(1)}, bf16[3,256,128]{2,1,0:T(8,128)(2,1)S(1)}, u32[]{:S(2)}, u32[]{:S(2)}) collective-permute-start(bf16[3,256,128]{2,1,0:T(8,128)(2,1)S(1)} %get-tuple-element.37), channel_id=1, source_target_pairs={{0,1},{1,0},{2,3},{3,2},{4,5},{5,4},{6,7},{7,6},{8,9},{9,8},{10,11... | collective-permute-start | bytes 589832 | tf_op jit(solution)/shard_map/ppermute | solution.py:323
  31.7 12.9 %collective-permute-start.14 = (bf16[3,256,128]{2,1,0:T(8,128)(2,1)S(1)}, bf16[3,256,128]{2,1,0:T(8,128)(2,1)S(1)}, u32[]{:S(2)}, u32[]{:S(2)}) collective-permute-start(bf16[3,256,128]{2,1,0:T(8,128)(2,1)S(1)} %get-tuple-element.38), channel_id=1, source_target_pairs={{1,2},{2,1},{3,4},{4,3},{5,6},{6,5},{9,10},{10,9},{11,12},{12,11},... | collective-permute-start | bytes 589832 | tf_op jit(solution)/shard_map/ppermute | solution.py:323

commit v6 on v5

--- a/solution.py
+++ b/solution.py
@@ -223,17 +223,18 @@
                     z_ref[column, v, :, term * MR : (term + 1) * MR], block, preferred_element_type=jnp.float32
                 )
     for v in range(VECS):
-        down, up = total[0, v].astype(jnp.bfloat16), total[2, v].astype(jnp.bfloat16)
+        down, up = total[0, v], total[2, v]
         zero_ref[v] = total[1, v]
-        low_ref[v] = jnp.where(even, up, down)
-        high_ref[v] = jnp.where(even, down, up)
-
-
-def right_products(cls, per, z, own, other, received, lefts):
+        low_ref[v] = jnp.where(even, up, down).astype(low_ref.dtype)
+        high_ref[v] = jnp.where(even, down, up).astype(high_ref.dtype)
+
+
+def right_products(cls, per, through, z, own, other, received, lefts):
     block = (VECS, ML, MR)
+    low_type = jnp.float32 if through else jnp.bfloat16
     return pl.pallas_call(
         functools.partial(right_kernel, cls, per),
-        out_shape=[jax.ShapeDtypeStruct(block, dtype) for dtype in (jnp.float32, jnp.bfloat16, jnp.bfloat16)],
+        out_shape=[jax.ShapeDtypeStruct(block, dtype) for dtype in (jnp.float32, low_type, jnp.bfloat16)],
         in_specs=[VMEM] * (4 + len(lefts)),
         out_specs=[VMEM] * 3,
         scratch_shapes=[in_vmem((3,) + block, jnp.float32)],
@@ -243,9 +244,25 @@
     )(z, own, other, received, *lefts)
 
 
-def sum_kernel(per, *refs):
+def joined_kernel(low, passing, out_ref):
+    out_ref[...] = (low[...] + passing[...].astype(jnp.float32)).astype(jnp.bfloat16)
+
+
+def joined(low, passing):
+    return pl.pallas_call(
+        joined_kernel,
+        out_shape=jax.ShapeDtypeStruct(low.shape, jnp.bfloat16),
+        in_specs=[VMEM] * 2,
+        out_specs=VMEM,
+        compiler_params=grant(8),
+        cost_estimate=cost(0, 0),
+        name="joined",
+    )(low, passing)
+
+
+def sum_kernel(per, direct, *refs):
     *parts, out_hbm, out_ref, sems = refs
-    zeros, lows, highs = parts[::3], parts[1::3], parts[2::3]
+    zeros, lows, highs = parts[:per], parts[per : 2 * per], dict(zip(direct, parts[2 * per :]))
     sec = lax.axis_index("sec")
     beyond = (sec ^ ((((sec + 1) ^ 1) + per - 1) % per)) % per
     copies = [pltpu.make_async_copy(out_ref.at[v], out_hbm.at[v], sems.at[v]) for v in range(VECS)]
@@ -257,7 +274,8 @@
                 for cls in range(per):
                     column = pl.multiple_of(((sec % per) ^ cls) * MR, MR)
                     total = zeros[cls][v].astype(jnp.float32) + lows[cls ^ 1][v].astype(jnp.float32)
-                    total = total + highs[cls ^ high][v].astype(jnp.float32)
+                    if cls ^ high in highs:
+                        total = total + highs[cls ^ high][v].astype(jnp.float32)
                     out_ref[v, :, pl.ds(column, MR)] = total.astype(jnp.bfloat16)
                 copies[v].start()
 
@@ -269,10 +287,10 @@
         copy.wait()
 
 
-def summed(per, parts):
+def summed(per, direct, parts):
     shape = (VECS, ML, per * MR)
     return pl.pallas_call(
-        functools.partial(sum_kernel, per),
+        functools.partial(sum_kernel, per, direct),
         out_shape=jax.ShapeDtypeStruct(shape, jnp.bfloat16),
         in_specs=[VMEM] * len(parts),
         out_specs=HBM,
@@ -307,6 +325,8 @@
     z = left_products(lefts, window)
     low = [(d, d ^ 1) for d in range(n_sec)]
     high = [(d, ((d + 1) ^ 1) - 1) for d in range(1, n_sec - 1)]
+    through = (0,)
+    along = [(d, d + 2 if d % 2 else d - 2) for d in range(1, n_sec - 1)]
     settled = (matching & 1) == 0
     parts, others = [], [other]
     for cls, own in enumerate(owns):
@@ -319,13 +339,20 @@
                 over_sec(owns[cls + 1][:half], n_sec, per),
                 over_sec(others[(cls + 1) ^ step][half:], n_sec, step),
             ]
-        zero, to_low, to_high = right_products(cls, per, z, own, other, received, lefts)
-        parts += [zero, lax.ppermute(to_low, "sec", low), lax.ppermute(to_high, "sec", high)]
+        zero, to_low, to_high = right_products(cls, per, cls in through, z, own, other, received, lefts)
+        if cls in through:
+            passing = lax.ppermute(to_high, "sec", along)
+            parts += [zero, to_low, passing]
+        else:
+            parts += [zero, lax.ppermute(to_low, "sec", low), lax.ppermute(to_high, "sec", high)]
         if later is not None:
             later, parts[-3] = tie((later, zero.astype(jnp.bfloat16)))
             other = jnp.concatenate(later)
             others.append(other)
-    return summed(per, parts).transpose(1, 0, 2)
+    parts[1] = lax.ppermute(joined(tie((parts[1], parts[3]))[0], parts[2]), "sec", low)
+    direct = [cls for cls in range(per) if cls not in through]
+    parts = parts[::3] + parts[1::3] + [parts[3 * cls + 2] for cls in direct]
+    return summed(per, direct, parts).transpose(1, 0, 2)
 
 
 def solution(mesh):

time: 46.2 us -> 45.4 us (0.983); the launches traced: 45.4 us -> 45.2 us
  starting transfers between devices: 24.3 us -> 23.8 us
    ppermute x2 -> x1, waiting for transfers between devices: 11 us -> 3.97 us  [on_device(): lax.ppermute(to_low, 'sec', low)]
    ppermute x0 -> x2, waiting for transfers between devices: none -> 6.56 us  [the longest x1 5.12 us: on_device(): lax.ppermute(joined(tie((parts[1], parts[3]))[0], parts[2]), 'sec', low)]
    ppermute x0 -> x2, starting transfers between devices: none -> 2.6 us  [the longest x1 1.91 us: on_device(): passing = lax.ppermute(to_high, 'sec', along)]
    ppermute x2 -> x1, starting transfers between devices: 4.09 us -> 1.91 us  [on_device(): lax.ppermute(to_high, 'sec', high)]
    ppermute x2 -> x1, starting transfers between devices: 3.07 us -> 2.15 us  [on_device(): lax.ppermute(to_low, 'sec', low)]
    ppermute x2 -> x1, waiting for transfers between devices: 0.01 us -> 0.63 us  [on_device(): lax.ppermute(to_high, 'sec', high)]
  transfers between devices with their start and end apart: 15 -> 15, of which waited for: 3 -> 5; matrix products, arithmetic and copies ran while one was open for 0% -> 0% of each run, Pallas kernels for 15% -> 15%
where the time goes in v6:
time: 45.4 us; the launch traced here: 45.2 us
  starting transfers between devices  23.8 us (52%)
  waiting for transfers between devices  13.6 us (30%)
  Pallas kernels  7.45 us (16%)
    ppermute x5, starting transfers between devices, over_op(): return lax.ppermute(x, 'op', [(o, o ^ bit) for o in range(n_op)])  7.22 us
    ppermute x4, starting transfers between devices, over_sec(): return lax.ppermute(x, 'sec', [(d, d ^ bit) for d in range(n_sec)])  6.94 us
    ppermute x1, waiting for transfers between devices, on_device(): lax.ppermute(joined(tie((parts[1], parts[3]))[0], parts[2]), 'sec', low)  5.12 us
    ppermute x1, waiting for transfers between devices, on_device(): lax.ppermute(to_low, 'sec', low)  3.97 us
    ppermute x1, starting transfers between devices, towards_owner(): lax.ppermute(held, ('op', 'sec'), second)  2.88 us
    ppermute x5, waiting for transfers between devices, over_op(): return lax.ppermute(x, 'op', [(o, o ^ bit) for o in range(n_op)])  2.42 us
    ppermute x1, starting transfers between devices, on_device(): lax.ppermute(to_low, 'sec', low)  2.15 us
    pallas_call x1, Pallas kernels, window_of(): pl.pallas_call(functools.partial(window_kernel, n_op), out_shape=in_vmem(...  2 us
  transfers between devices with their start and end apart: 15, of which 5 were waited for; matrix products, arithmetic and copies ran while one was open for 0% of the time, Pallas kernels for 15%

profile of v6, /device:TPU:17, one launch (start us, length us, event | category | flops | bytes accessed | tf_op | source)
XLA Modules:
  0.0 45.2 jit_solution(14568993453756000938)
XLA Ops:
  0.0 2.9 %collective-permute-start.1 = (bf16[1,3,128,128]{3,2,1,0:T(8,128)(2,1)}, bf16[1,3,128,128]{3,2,1,0:T(8,128)(2,1)S(1)}, u32[]{:S(2)}, u32[]{:S(2)}) collective-permute-start(bf16[1,3,128,128]{3,2,1,0:T(8,128)(2,1)} %bitcast.8), channel_id=1, source_target_pairs={{4,16},{5,17},{6,18},{7,19},{12,24},{13,25},{14,26},{15,27},{16,4}... | collective-permute-start | bytes 294920 | tf_op jit(solution)/shard_map/ppermute | solution.py:58
  2.9 0.1 collective-permute-start
  3.0 1.0 %pack.1 = (bf16[784,256]{1,0:T(8,128)(2,1)S(1)}, bf16[1,3,128,128]{3,2,1,0:T(8,128)(2,1)S(1)}) custom-call(s32[3]{0:T(128)} %shift.1, bf16[768,256]{1,0:T(8,128)(2,1)} %bitcast.7, bf16[1,3,128,128]{3,2,1,0:T(8,128)(2,1)} %bitcast.10), custom_call_target="tpu_custom_call" | custom-call | bytes 33554432 | tf_op jit(solution)/shard_map/pack/pallas_call | solution.py:121
  4.0 2.6 %collective-permute-start.6 = (bf16[784,256]{1,0:T(8,128)(2,1)S(1)}, bf16[784,256]{1,0:T(8,128)(2,1)S(1)}, u32[]{:S(2)}, u32[]{:S(2)}) collective-permute-start(bf16[784,256]{1,0:T(8,128)(2,1)S(1)} %get-tuple-element.28.refs_0_), channel_id=1, source_target_pairs={{0,16},{8,24},{16,0},{24,8},{1,17},{9,25},{17,1},{25,9},{2,18},{10... | collective-permute-start | bytes 1204232 | tf_op jit(solution)/shard_map/ppermute | solution.py:35
  6.6 2.0 %window.1.refs_4_ = bf16[3,256,512]{2,1,0:T(8,128)(2,1)S(1)} custom-call(bf16[3,256,1024]{2,1,0:T(8,128)(2,1)} %bitcast.6), custom_call_target="tpu_custom_call" | custom-call | bytes 2097152 | tf_op jit(solution)/shard_map/window/pallas_call | solution.py:162
  8.6 0.0 collective-permute-done.1
  8.6 0.0 collective-permute-done
  8.7 1.3 %collective-permute-start.3 = (bf16[2,3,128,128]{3,2,1,0:T(8,128)(2,1)S(1)}, bf16[2,3,128,128]{3,2,1,0:T(8,128)(2,1)S(1)}, u32[]{:S(2)}, u32[]{:S(2)}) collective-permute-start(bf16[2,3,128,128]{3,2,1,0:T(8,128)(2,1)S(1)} %pad_maximum_fusion.own), channel_id=1, source_target_pairs={{0,1},{1,0},{2,3},{3,2},{4,5},{5,4},{6,7},{7,6},{8,9},{9,8},{10,11... | collective-permute-start | bytes 589832 | tf_op jit(solution)/shard_map/ppermute | solution.py:39
  10.0 3.2 %collective-permute-start.2 = (bf16[2,3,128,128]{3,2,1,0:T(8,128)(2,1)S(1)}, bf16[2,3,128,128]{3,2,1,0:T(8,128)(2,1)S(1)}, u32[]{:S(2)}, u32[]{:S(2)}) collective-permute-start(bf16[2,3,128,128]{3,2,1,0:T(8,128)(2,1)S(1)} %pad_maximum_fusion.own), channel_id=1, source_target_pairs={{0,2},{1,3},{2,0},{3,1},{4,6},{5,7},{6,4},{7,5},{8,10},{9,11},{10,... | collective-permute-start | bytes 589832 | tf_op jit(solution)/shard_map/ppermute | solution.py:39
  13.3 1.2 %collective-permute-start.7 = (bf16[784,256]{1,0:T(8,128)(2,1)S(1)}, bf16[784,256]{1,0:T(8,128)(2,1)S(1)}, u32[]{:S(2)}, u32[]{:S(2)}) collective-permute-start(bf16[784,256]{1,0:T(8,128)(2,1)S(1)} %get-tuple-element.28.refs_0_), channel_id=1, source_target_pairs={{0,8},{8,0},{16,24},{24,16},{1,9},{9,1},{17,25},{25,17},{2,10},{10... | collective-permute-start | bytes 1204232 | tf_op jit(solution)/shard_map/ppermute | solution.py:35
  14.5 2.4 %collective-permute-done.6.refs_1_ = bf16[784,256]{1,0:T(8,128)(2,1)S(1)} collective-permute-done((bf16[784,256]{1,0:T(8,128)(2,1)S(1)}, bf16[784,256]{1,0:T(8,128)(2,1)S(1)}, u32[]{:S(2)}, u32[]{:S(2)}) %collective-permute-start.6) | collective-permute-done | bytes 401440 | tf_op jit(solution)/shard_map/ppermute | solution.py:35
  16.9 0.9 %collective-permute-start.8 = (bf16[784,256]{1,0:T(8,128)(2,1)S(1)}, bf16[784,256]{1,0:T(8,128)(2,1)S(1)}, u32[]{:S(2)}, u32[]{:S(2)}) collective-permute-start(bf16[784,256]{1,0:T(8,128)(2,1)S(1)} %collective-permute-done.6.refs_1_), channel_id=1, source_target_pairs={{0,8},{8,0},{16,24},{24,16},{1,9},{9,1},{17,25},{25,17},{2,10},{10... | collective-permute-start | bytes 1204232 | tf_op jit(solution)/shard_map/ppermute | solution.py:35
  17.8 1.4 %collective-permute-start.9 = (bf16[2,3,128,128]{3,2,1,0:T(8,128)(2,1)S(1)}, bf16[2,3,128,128]{3,2,1,0:T(8,128)(2,1)S(1)}, u32[]{:S(2)}, u32[]{:S(2)}) collective-permute-start(bf16[2,3,128,128]{3,2,1,0:T(8,128)(2,1)S(1)} %broadcast_select_fusion.1), channel_id=1, source_target_pairs={{0,8},{8,0},{16,24},{24,16},{1,9},{9,1},{17,25},{25,17},{2,10},{10... | collective-permute-start | bytes 589832 | tf_op jit(solution)/shard_map/ppermute | solution.py:35
  19.2 0.3 collective-permute-start.5
  19.5 2.1 %collective-permute-start.4 = (bf16[1,3,128,128]{3,2,1,0:T(8,128)(2,1)S(1)}, bf16[1,3,128,128]{3,2,1,0:T(8,128)(2,1)S(1)}, u32[]{:S(2)}, u32[]{:S(2)}) collective-permute-start(bf16[1,3,128,128]{3,2,1,0:T(8,128)(2,1)S(1)} %slice.6), channel_id=1, source_target_pairs={{0,2},{1,3},{2,0},{3,1},{4,6},{5,7},{6,4},{7,5},{8,10},{9,11},{10,... | collective-permute-start | bytes 294920 | tf_op jit(solution)/shard_map/ppermute | solution.py:39
  21.6 0.0 collective-permute-done.7.refs_2_
  21.6 0.0 collective-permute-done.8.refs_3_
  21.6 1.7 %left_products.1.z_ref = bf16[2,3,256,1536]{3,2,1,0:T(8,128)(2,1)S(1)} custom-call(bf16[784,256]{1,0:T(8,128)(2,1)S(1)} %get-tuple-element.28.refs_0_, bf16[784,256]{1,0:T(8,128)(2,1)S(1)} %collective-permute-done.6.refs_1_, bf16[784,256]{1,0:T(8,128)(2,1)S(1)} %collective-permute-done.7.refs_2_, bf16[784,256]{1,0:T(8,128)(2,1)S(1)} %collective-permute-done.8.refs_3_, ...), custom_call_target="tpu_custom_call" | custom-call | flops 1207959552 | bytes 1048576 | tf_op jit(solution)/shard_map/left_products/pallas_call | solution.py:194
  23.3 0.0 collective-permute-done.9.received
  23.3 1.0 %right_products.2 = (f32[3,256,128]{2,1,0:T(8,128)S(1)}, f32[3,256,128]{2,1,0:T(8,128)S(1)}, bf16[3,256,128]{2,1,0:T(8,128)(2,1)S(1)}) custom-call(bf16[2,3,256,1536]{3,2,1,0:T(8,128)(2,1)S(1)} %left_products.1.z_ref, bf16[2,3,128,128]{3,2,1,0:T(8,128)(2,1)S(1)} %pad_maximum_fusion.own, bf16[2,3,128,128]{3,2,1,0:T(8,128)(2,1)S(1)} %collective-permute-done.2.other, ...), custom_call_target="tpu_custom_call" | custom-call | tf_op jit(solution)/shard_map/right_products/pallas_call | solution.py:235
  24.3 0.0 collective-permute-done.5
  24.4 1.1 %collective-permute-start.10 = (bf16[2,3,128,128]{3,2,1,0:T(8,128)(2,1)S(1)}, bf16[2,3,128,128]{3,2,1,0:T(8,128)(2,1)S(1)}, u32[]{:S(2)}, u32[]{:S(2)}) collective-permute-start(bf16[2,3,128,128]{3,2,1,0:T(8,128)(2,1)S(1)} %broadcast_select_fusion), channel_id=1, source_target_pairs={{0,8},{8,0},{16,24},{24,16},{1,9},{9,1},{17,25},{25,17},{2,10},{10... | collective-permute-start | bytes 589832 | tf_op jit(solution)/shard_map/ppermute | solution.py:35
  25.5 1.9 %collective-permute-start.11 = (bf16[3,256,128]{2,1,0:T(8,128)(2,1)S(1)}, bf16[3,256,128]{2,1,0:T(8,128)(2,1)S(1)}, u32[]{:S(2)}, u32[]{:S(2)}) collective-permute-start(bf16[3,256,128]{2,1,0:T(8,128)(2,1)S(1)} %get-tuple-element.38), channel_id=1, source_target_pairs={{1,3},{2,0},{3,5},{4,2},{5,7},{6,4},{9,11},{10,8},{11,13},{12,10},... | collective-permute-start | bytes 589832 | tf_op jit(solution)/shard_map/ppermute | solution.py:344
  27.4 1.0 %right_products.3 = (f32[3,256,128]{2,1,0:T(8,128)S(1)}, bf16[3,256,128]{2,1,0:T(8,128)(2,1)S(1)}, bf16[3,256,128]{2,1,0:T(8,128)(2,1)S(1)}) custom-call(bf16[2,3,256,1536]{3,2,1,0:T(8,128)(2,1)S(1)} %left_products.1.z_ref, bf16[2,3,128,128]{3,2,1,0:T(8,128)(2,1)S(1)} %collective-permute-done.3.own, ...), custom_call_target="tpu_custom_call" | custom-call | tf_op jit(solution)/shard_map/right_products/pallas_call | solution.py:235
  28.4 2.1 %collective-permute-start.13 = (bf16[3,256,128]{2,1,0:T(8,128)(2,1)S(1)}, bf16[3,256,128]{2,1,0:T(8,128)(2,1)S(1)}, u32[]{:S(2)}, u32[]{:S(2)}) collective-permute-start(bf16[3,256,128]{2,1,0:T(8,128)(2,1)S(1)} %get-tuple-element.39), channel_id=1, source_target_pairs={{0,1},{1,0},{2,3},{3,2},{4,5},{5,4},{6,7},{7,6},{8,9},{9,8},{10,11... | collective-permute-start | bytes 589832 | tf_op jit(solution)/shard_map/ppermute | solution.py:347
  30.5 1.9 %collective-permute-start.14 = (bf16[3,256,128]{2,1,0:T(8,128)(2,1)S(1)}, bf16[3,256,128]{2,1,0:T(8,128)(2,1)S(1)}, u32[]{:S(2)}, u32[]{:S(2)}) collective-permute-start(bf16[3,256,128]{2,1,0:T(8,128)(2,1)S(1)} %get-tuple-element.40), channel_id=1, source_target_pairs={{1,2},{2,1},{3,4},{4,3},{5,6},{6,5},{9,10},{10,9},{11,12},{12,11},... | collective-permute-start | bytes 589832 | tf_op jit(solution)/shard_map/ppermute | solution.py:347
  32.4 1.4 %collective-permute-done.11.passing = bf16[3,256,128]{2,1,0:T(8,128)(2,1)S(1)} collective-permute-done((bf16[3,256,128]{2,1,0:T(8,128)(2,1)S(1)}, bf16[3,256,128]{2,1,0:T(8,128)(2,1)S(1)}, u32[]{:S(2)}, u32[]{:S(2)}) %collective-permute-start.11) | collective-permute-done | bytes 196640 | tf_op jit(solution)/shard_map/ppermute | solution.py:344
  33.9 0.7 %collective-permute-start.12 = (bf16[3,256,128]{2,1,0:T(8,128)(2,1)S(1)}, bf16[3,256,128]{2,1,0:T(8,128)(2,1)S(1)}, u32[]{:S(2)}, u32[]{:S(2)}) collective-permute-start(bf16[3,256,128]{2,1,0:T(8,128)(2,1)S(1)} %joined.1), channel_id=1, source_target_pairs={{0,1},{1,0},{2,3},{3,2},{4,5},{5,4},{6,7},{7,6},{8,9},{9,8},{10,11... | collective-permute-start | bytes 589832 | tf_op jit(solution)/shard_map/ppermute | solution.py:352
  34.6 4.0 %collective-permute-done.13.refs_3_ = bf16[3,256,128]{2,1,0:T(8,128)(2,1)S(1)} collective-permute-done((bf16[3,256,128]{2,1,0:T(8,128)(2,1)S(1)}, bf16[3,256,128]{2,1,0:T(8,128)(2,1)S(1)}, u32[]{:S(2)}, u32[]{:S(2)}) %collective-permute-start.13) | collective-permute-done | bytes 196640 | tf_op jit(solution)/shard_map/ppermute | solution.py:347
  38.6 0.6 %collective-permute-done.14.refs_4_ = bf16[3,256,128]{2,1,0:T(8,128)(2,1)S(1)} collective-permute-done((bf16[3,256,128]{2,1,0:T(8,128)(2,1)S(1)}, bf16[3,256,128]{2,1,0:T(8,128)(2,1)S(1)}, u32[]{:S(2)}, u32[]{:S(2)}) %collective-permute-start.14) | collective-permute-done | bytes 196640 | tf_op jit(solution)/shard_map/ppermute | solution.py:347
  39.2 5.1 %collective-permute-done.12.refs_2_ = bf16[3,256,128]{2,1,0:T(8,128)(2,1)S(1)} collective-permute-done((bf16[3,256,128]{2,1,0:T(8,128)(2,1)S(1)}, bf16[3,256,128]{2,1,0:T(8,128)(2,1)S(1)}, u32[]{:S(2)}, u32[]{:S(2)}) %collective-permute-start.12) | collective-permute-done | bytes 196640 | tf_op jit(solution)/shard_map/ppermute | solution.py:352
  44.4 0.8 %summed.1 = bf16[3,256,256]{2,1,0:T(8,128)(2,1)} custom-call(bf16[3,256,128]{2,1,0:T(8,128)(2,1)S(1)} %convert_element_type.3.refs_0_, f32[3,256,128]{2,1,0:T(8,128)S(1)} %get-tuple-element.35.refs_1_, bf16[3,256,128]{2,1,0:T(8,128)(2,1)S(1)} %collective-permute-done.12.refs_2_, bf16[3,256,128]{2,1,0:T(8,128)(2,1)S(1)} %collective-permute-done.13.refs_3_, ...), custom_call_target="tpu_custom_call" | custom-call | tf_op jit(solution)/shard_map/summed/pallas_call | solution.py:292
  (14 shorter events, 0.2 us)
Async XLA Ops:
  0.0 8.6 %collective-permute-start.1 = (bf16[1,3,128,128]{3,2,1,0:T(8,128)(2,1)}, bf16[1,3,128,128]{3,2,1,0:T(8,128)(2,1)S(1)}, u32[]{:S(2)}, u32[]{:S(2)}) collective-permute-start(bf16[1,3,128,128]{3,2,1,0:T(8,128)(2,1)} %bitcast.8), channel_id=1, source_target_pairs={{4,16},{5,17},{6,18},{7,19},{12,24},{13,25},{14,26},{15,27},{16,4}... | collective-permute-start | bytes 294920 | tf_op jit(solution)/shard_map/ppermute | solution.py:58
  2.9 5.8 %collective-permute-start = (bf16[1,3,128,128]{3,2,1,0:T(8,128)(2,1)}, bf16[1,3,128,128]{3,2,1,0:T(8,128)(2,1)S(1)}, u32[]{:S(2)}, u32[]{:S(2)}) collective-permute-start(bf16[1,3,128,128]{3,2,1,0:T(8,128)(2,1)} %bitcast.9), channel_id=1, source_target_pairs={{0,4},{1,5},{2,6},{3,7},{4,20},{5,21},{6,22},{7,23},{8,12},{9,13},... | collective-permute-start | bytes 294920 | tf_op jit(solution)/shard_map/ppermute | solution.py:58
  4.0 12.9 %collective-permute-start.6 = (bf16[784,256]{1,0:T(8,128)(2,1)S(1)}, bf16[784,256]{1,0:T(8,128)(2,1)S(1)}, u32[]{:S(2)}, u32[]{:S(2)}) collective-permute-start(bf16[784,256]{1,0:T(8,128)(2,1)S(1)} %get-tuple-element.28.refs_0_), channel_id=1, source_target_pairs={{0,16},{8,24},{16,0},{24,8},{1,17},{9,25},{17,1},{25,9},{2,18},{10... | collective-permute-start | bytes 1204232 | tf_op jit(solution)/shard_map/ppermute | solution.py:35
  8.7 9.1 %collective-permute-start.3 = (bf16[2,3,128,128]{3,2,1,0:T(8,128)(2,1)S(1)}, bf16[2,3,128,128]{3,2,1,0:T(8,128)(2,1)S(1)}, u32[]{:S(2)}, u32[]{:S(2)}) collective-permute-start(bf16[2,3,128,128]{3,2,1,0:T(8,128)(2,1)S(1)} %pad_maximum_fusion.own), channel_id=1, source_target_pairs={{0,1},{1,0},{2,3},{3,2},{4,5},{5,4},{6,7},{7,6},{8,9},{9,8},{10,11... | collective-permute-start | bytes 589832 | tf_op jit(solution)/shard_map/ppermute | solution.py:39
  10.0 7.8 %collective-permute-start.2 = (bf16[2,3,128,128]{3,2,1,0:T(8,128)(2,1)S(1)}, bf16[2,3,128,128]{3,2,1,0:T(8,128)(2,1)S(1)}, u32[]{:S(2)}, u32[]{:S(2)}) collective-permute-start(bf16[2,3,128,128]{3,2,1,0:T(8,128)(2,1)S(1)} %pad_maximum_fusion.own), channel_id=1, source_target_pairs={{0,2},{1,3},{2,0},{3,1},{4,6},{5,7},{6,4},{7,5},{8,10},{9,11},{10,... | collective-permute-start | bytes 589832 | tf_op jit(solution)/shard_map/ppermute | solution.py:39
  13.3 8.4 %collective-permute-start.7 = (bf16[784,256]{1,0:T(8,128)(2,1)S(1)}, bf16[784,256]{1,0:T(8,128)(2,1)S(1)}, u32[]{:S(2)}, u32[]{:S(2)}) collective-permute-start(bf16[784,256]{1,0:T(8,128)(2,1)S(1)} %get-tuple-element.28.refs_0_), channel_id=1, source_target_pairs={{0,8},{8,0},{16,24},{24,16},{1,9},{9,1},{17,25},{25,17},{2,10},{10... | collective-permute-start | bytes 1204232 | tf_op jit(solution)/shard_map/ppermute | solution.py:35
  16.9 4.7 %collective-permute-start.8 = (bf16[784,256]{1,0:T(8,128)(2,1)S(1)}, bf16[784,256]{1,0:T(8,128)(2,1)S(1)}, u32[]{:S(2)}, u32[]{:S(2)}) collective-permute-start(bf16[784,256]{1,0:T(8,128)(2,1)S(1)} %collective-permute-done.6.refs_1_), channel_id=1, source_target_pairs={{0,8},{8,0},{16,24},{24,16},{1,9},{9,1},{17,25},{25,17},{2,10},{10... | collective-permute-start | bytes 1204232 | tf_op jit(solution)/shard_map/ppermute | solution.py:35
  17.8 5.4 %collective-permute-start.9 = (bf16[2,3,128,128]{3,2,1,0:T(8,128)(2,1)S(1)}, bf16[2,3,128,128]{3,2,1,0:T(8,128)(2,1)S(1)}, u32[]{:S(2)}, u32[]{:S(2)}) collective-permute-start(bf16[2,3,128,128]{3,2,1,0:T(8,128)(2,1)S(1)} %broadcast_select_fusion.1), channel_id=1, source_target_pairs={{0,8},{8,0},{16,24},{24,16},{1,9},{9,1},{17,25},{25,17},{2,10},{10... | collective-permute-start | bytes 589832 | tf_op jit(solution)/shard_map/ppermute | solution.py:35
  19.2 5.1 %collective-permute-start.5 = (bf16[1,3,128,128]{3,2,1,0:T(8,128)(2,1)S(1)}, bf16[1,3,128,128]{3,2,1,0:T(8,128)(2,1)S(1)}, u32[]{:S(2)}, u32[]{:S(2)}) collective-permute-start(bf16[1,3,128,128]{3,2,1,0:T(8,128)(2,1)S(1)} %slice.7), channel_id=1, source_target_pairs={{0,1},{1,0},{2,3},{3,2},{4,5},{5,4},{6,7},{7,6},{8,9},{9,8},{10,11... | collective-permute-start | bytes 294920 | tf_op jit(solution)/shard_map/ppermute | solution.py:39
  19.5 4.8 %collective-permute-start.4 = (bf16[1,3,128,128]{3,2,1,0:T(8,128)(2,1)S(1)}, bf16[1,3,128,128]{3,2,1,0:T(8,128)(2,1)S(1)}, u32[]{:S(2)}, u32[]{:S(2)}) collective-permute-start(bf16[1,3,128,128]{3,2,1,0:T(8,128)(2,1)S(1)} %slice.6), channel_id=1, source_target_pairs={{0,2},{1,3},{2,0},{3,1},{4,6},{5,7},{6,4},{7,5},{8,10},{9,11},{10,... | collective-permute-start | bytes 294920 | tf_op jit(solution)/shard_map/ppermute | solution.py:39
  24.4 3.0 %collective-permute-start.10 = (bf16[2,3,128,128]{3,2,1,0:T(8,128)(2,1)S(1)}, bf16[2,3,128,128]{3,2,1,0:T(8,128)(2,1)S(1)}, u32[]{:S(2)}, u32[]{:S(2)}) collective-permute-start(bf16[2,3,128,128]{3,2,1,0:T(8,128)(2,1)S(1)} %broadcast_select_fusion), channel_id=1, source_target_pairs={{0,8},{8,0},{16,24},{24,16},{1,9},{9,1},{17,25},{25,17},{2,10},{10... | collective-permute-start | bytes 589832 | tf_op jit(solution)/shard_map/ppermute | solution.py:35
  25.5 8.4 %collective-permute-start.11 = (bf16[3,256,128]{2,1,0:T(8,128)(2,1)S(1)}, bf16[3,256,128]{2,1,0:T(8,128)(2,1)S(1)}, u32[]{:S(2)}, u32[]{:S(2)}) collective-permute-start(bf16[3,256,128]{2,1,0:T(8,128)(2,1)S(1)} %get-tuple-element.38), channel_id=1, source_target_pairs={{1,3},{2,0},{3,5},{4,2},{5,7},{6,4},{9,11},{10,8},{11,13},{12,10},... | collective-permute-start | bytes 589832 | tf_op jit(solution)/shard_map/ppermute | solution.py:344
  28.4 10.2 %collective-permute-start.13 = (bf16[3,256,128]{2,1,0:T(8,128)(2,1)S(1)}, bf16[3,256,128]{2,1,0:T(8,128)(2,1)S(1)}, u32[]{:S(2)}, u32[]{:S(2)}) collective-permute-start(bf16[3,256,128]{2,1,0:T(8,128)(2,1)S(1)} %get-tuple-element.39), channel_id=1, source_target_pairs={{0,1},{1,0},{2,3},{3,2},{4,5},{5,4},{6,7},{7,6},{8,9},{9,8},{10,11... | collective-permute-start | bytes 589832 | tf_op jit(solution)/shard_map/ppermute | solution.py:347
  30.5 8.7 %collective-permute-start.14 = (bf16[3,256,128]{2,1,0:T(8,128)(2,1)S(1)}, bf16[3,256,128]{2,1,0:T(8,128)(2,1)S(1)}, u32[]{:S(2)}, u32[]{:S(2)}) collective-permute-start(bf16[3,256,128]{2,1,0:T(8,128)(2,1)S(1)} %get-tuple-element.40), channel_id=1, source_target_pairs={{1,2},{2,1},{3,4},{4,3},{5,6},{6,5},{9,10},{10,9},{11,12},{12,11},... | collective-permute-start | bytes 589832 | tf_op jit(solution)/shard_map/ppermute | solution.py:347
  33.9 10.4 %collective-permute-start.12 = (bf16[3,256,128]{2,1,0:T(8,128)(2,1)S(1)}, bf16[3,256,128]{2,1,0:T(8,128)(2,1)S(1)}, u32[]{:S(2)}, u32[]{:S(2)}) collective-permute-start(bf16[3,256,128]{2,1,0:T(8,128)(2,1)S(1)} %joined.1), channel_id=1, source_target_pairs={{0,1},{1,0},{2,3},{3,2},{4,5},{5,4},{6,7},{7,6},{8,9},{9,8},{10,11... | collective-permute-start | bytes 589832 | tf_op jit(solution)/shard_map/ppermute | solution.py:352

commit v7 on v6

--- a/solution.py
+++ b/solution.py
@@ -94,8 +94,9 @@
 
 
 def shift_of(left, inner):
-    row = left.shape[0] - TILE + inner
-    return jnp.max(left[row : row + 1, :MR].astype(jnp.float32)).astype(jnp.int32)
+    tags = left[left.shape[0] - TILE :, :MR].astype(jnp.float32)
+    row = lax.broadcasted_iota(jnp.int32, tags.shape, 0)
+    return jnp.max(jnp.where(row == inner, tags, -1.0)).astype(jnp.int32)
 
 
 def pack_kernel(shift, left, right, packed, kept, shift_ref, sems):
@@ -278,13 +279,13 @@
                         total = total + highs[cls ^ high][v].astype(jnp.float32)
                     out_ref[v, :, pl.ds(column, MR)] = total.astype(jnp.bfloat16)
                 copies[v].start()
+            for copy in copies:
+                copy.wait()
 
     carry = 1
     while carry < per:
         add(carry)
         carry = 2 * carry + 1
-    for copy in copies:
-        copy.wait()
 
 
 def summed(per, direct, parts):
@@ -325,7 +326,9 @@
     z = left_products(lefts, window)
     low = [(d, d ^ 1) for d in range(n_sec)]
     high = [(d, ((d + 1) ^ 1) - 1) for d in range(1, n_sec - 1)]
-    through = (0,)
+    turn = 2 % per
+    through = sorted({0, turn}) if per <= 4 else []
+    lows = []
     along = [(d, d + 2 if d % 2 else d - 2) for d in range(1, n_sec - 1)]
     settled = (matching & 1) == 0
     parts, others = [], [other]
@@ -349,7 +352,11 @@
             later, parts[-3] = tie((later, zero.astype(jnp.bfloat16)))
             other = jnp.concatenate(later)
             others.append(other)
-    parts[1] = lax.ppermute(joined(tie((parts[1], parts[3]))[0], parts[2]), "sec", low)
+    for cls in through:
+        own_low = tie((parts[3 * cls + 1], parts[3]))[0]
+        lows.append(lax.ppermute(joined(own_low, parts[3 * (cls ^ turn) + 2]), "sec", low))
+    for cls, part in zip(through, lows):
+        parts[3 * cls + 1] = part
     direct = [cls for cls in range(per) if cls not in through]
     parts = parts[::3] + parts[1::3] + [parts[3 * cls + 2] for cls in direct]
     return summed(per, direct, parts).transpose(1, 0, 2)

time: 45.4 us -> 45.4 us (level)
  no operation moved by 1% of the time
where the time goes in v7:
time: 45.4 us; the launch traced here: 45.2 us
  starting transfers between devices  23.7 us (52%)
  waiting for transfers between devices  13.6 us (30%)
  Pallas kernels  7.5 us (17%)
    ppermute x5, starting transfers between devices, over_op(): return lax.ppermute(x, 'op', [(o, o ^ bit) for o in range(n_op)])  7.23 us
    ppermute x4, starting transfers between devices, over_sec(): return lax.ppermute(x, 'sec', [(d, d ^ bit) for d in range(n_sec)])  6.94 us
    ppermute x1, waiting for transfers between devices, on_device(): lax.ppermute(joined(own_low, parts[3 * (cls ^ turn) + 2]), 'sec', low)  5.13 us
    ppermute x1, waiting for transfers between devices, on_device(): lax.ppermute(to_low, 'sec', low)  3.97 us
    ppermute x1, starting transfers between devices, towards_owner(): lax.ppermute(held, ('op', 'sec'), second)  2.88 us
    ppermute x5, waiting for transfers between devices, over_op(): return lax.ppermute(x, 'op', [(o, o ^ bit) for o in range(n_op)])  2.42 us
    ppermute x1, starting transfers between devices, on_device(): lax.ppermute(to_low, 'sec', low)  2.1 us
    pallas_call x1, Pallas kernels, window_of(): pl.pallas_call(functools.partial(window_kernel, n_op), out_shape=in_vmem(...  2 us
  transfers between devices with their start and end apart: 15, of which 5 were waited for; matrix products, arithmetic and copies ran while one was open for 0% of the time, Pallas kernels for 15%

profile of v7, /device:TPU:17, one launch (start us, length us, event | category | flops | bytes accessed | tf_op | source)
XLA Modules:
  0.0 45.2 jit_solution(11044468566440219499)
XLA Ops:
  0.0 2.9 %collective-permute-start.1 = (bf16[1,3,128,128]{3,2,1,0:T(8,128)(2,1)}, bf16[1,3,128,128]{3,2,1,0:T(8,128)(2,1)S(1)}, u32[]{:S(2)}, u32[]{:S(2)}) collective-permute-start(bf16[1,3,128,128]{3,2,1,0:T(8,128)(2,1)} %bitcast.8), channel_id=1, source_target_pairs={{4,16},{5,17},{6,18},{7,19},{12,24},{13,25},{14,26},{15,27},{16,4}... | collective-permute-start | bytes 294920 | tf_op jit(solution)/shard_map/ppermute | solution.py:58
  2.9 0.1 collective-permute-start
  3.0 1.0 %pack.1 = (bf16[784,256]{1,0:T(8,128)(2,1)S(1)}, bf16[1,3,128,128]{3,2,1,0:T(8,128)(2,1)S(1)}) custom-call(s32[3]{0:T(128)} %shift.1, bf16[768,256]{1,0:T(8,128)(2,1)} %bitcast.7, bf16[1,3,128,128]{3,2,1,0:T(8,128)(2,1)} %bitcast.10), custom_call_target="tpu_custom_call" | custom-call | bytes 33554432 | tf_op jit(solution)/shard_map/pack/pallas_call | solution.py:122
  4.0 2.6 %collective-permute-start.6 = (bf16[784,256]{1,0:T(8,128)(2,1)S(1)}, bf16[784,256]{1,0:T(8,128)(2,1)S(1)}, u32[]{:S(2)}, u32[]{:S(2)}) collective-permute-start(bf16[784,256]{1,0:T(8,128)(2,1)S(1)} %get-tuple-element.28.refs_0_), channel_id=1, source_target_pairs={{0,16},{8,24},{16,0},{24,8},{1,17},{9,25},{17,1},{25,9},{2,18},{10... | collective-permute-start | bytes 1204232 | tf_op jit(solution)/shard_map/ppermute | solution.py:35
  6.6 2.0 %window.1.refs_4_ = bf16[3,256,512]{2,1,0:T(8,128)(2,1)S(1)} custom-call(bf16[3,256,1024]{2,1,0:T(8,128)(2,1)} %bitcast.6), custom_call_target="tpu_custom_call" | custom-call | bytes 2097152 | tf_op jit(solution)/shard_map/window/pallas_call | solution.py:163
  8.6 0.0 collective-permute-done.1
  8.7 1.3 %collective-permute-start.3 = (bf16[2,3,128,128]{3,2,1,0:T(8,128)(2,1)S(1)}, bf16[2,3,128,128]{3,2,1,0:T(8,128)(2,1)S(1)}, u32[]{:S(2)}, u32[]{:S(2)}) collective-permute-start(bf16[2,3,128,128]{3,2,1,0:T(8,128)(2,1)S(1)} %pad_maximum_fusion.own), channel_id=1, source_target_pairs={{0,1},{1,0},{2,3},{3,2},{4,5},{5,4},{6,7},{7,6},{8,9},{9,8},{10,11... | collective-permute-start | bytes 589832 | tf_op jit(solution)/shard_map/ppermute | solution.py:39
  10.0 3.2 %collective-permute-start.2 = (bf16[2,3,128,128]{3,2,1,0:T(8,128)(2,1)S(1)}, bf16[2,3,128,128]{3,2,1,0:T(8,128)(2,1)S(1)}, u32[]{:S(2)}, u32[]{:S(2)}) collective-permute-start(bf16[2,3,128,128]{3,2,1,0:T(8,128)(2,1)S(1)} %pad_maximum_fusion.own), channel_id=1, source_target_pairs={{0,2},{1,3},{2,0},{3,1},{4,6},{5,7},{6,4},{7,5},{8,10},{9,11},{10,... | collective-permute-start | bytes 589832 | tf_op jit(solution)/shard_map/ppermute | solution.py:39
  13.3 1.2 %collective-permute-start.7 = (bf16[784,256]{1,0:T(8,128)(2,1)S(1)}, bf16[784,256]{1,0:T(8,128)(2,1)S(1)}, u32[]{:S(2)}, u32[]{:S(2)}) collective-permute-start(bf16[784,256]{1,0:T(8,128)(2,1)S(1)} %get-tuple-element.28.refs_0_), channel_id=1, source_target_pairs={{0,8},{8,0},{16,24},{24,16},{1,9},{9,1},{17,25},{25,17},{2,10},{10... | collective-permute-start | bytes 1204232 | tf_op jit(solution)/shard_map/ppermute | solution.py:35
  14.5 2.4 %collective-permute-done.6.refs_1_ = bf16[784,256]{1,0:T(8,128)(2,1)S(1)} collective-permute-done((bf16[784,256]{1,0:T(8,128)(2,1)S(1)}, bf16[784,256]{1,0:T(8,128)(2,1)S(1)}, u32[]{:S(2)}, u32[]{:S(2)}) %collective-permute-start.6) | collective-permute-done | bytes 401440 | tf_op jit(solution)/shard_map/ppermute | solution.py:35
  16.9 0.9 %collective-permute-start.8 = (bf16[784,256]{1,0:T(8,128)(2,1)S(1)}, bf16[784,256]{1,0:T(8,128)(2,1)S(1)}, u32[]{:S(2)}, u32[]{:S(2)}) collective-permute-start(bf16[784,256]{1,0:T(8,128)(2,1)S(1)} %collective-permute-done.6.refs_1_), channel_id=1, source_target_pairs={{0,8},{8,0},{16,24},{24,16},{1,9},{9,1},{17,25},{25,17},{2,10},{10... | collective-permute-start | bytes 1204232 | tf_op jit(solution)/shard_map/ppermute | solution.py:35
  17.8 1.4 %collective-permute-start.9 = (bf16[2,3,128,128]{3,2,1,0:T(8,128)(2,1)S(1)}, bf16[2,3,128,128]{3,2,1,0:T(8,128)(2,1)S(1)}, u32[]{:S(2)}, u32[]{:S(2)}) collective-permute-start(bf16[2,3,128,128]{3,2,1,0:T(8,128)(2,1)S(1)} %broadcast_select_fusion.1), channel_id=1, source_target_pairs={{0,8},{8,0},{16,24},{24,16},{1,9},{9,1},{17,25},{25,17},{2,10},{10... | collective-permute-start | bytes 589832 | tf_op jit(solution)/shard_map/ppermute | solution.py:35
  19.2 0.3 collective-permute-start.5
  19.5 2.1 %collective-permute-start.4 = (bf16[1,3,128,128]{3,2,1,0:T(8,128)(2,1)S(1)}, bf16[1,3,128,128]{3,2,1,0:T(8,128)(2,1)S(1)}, u32[]{:S(2)}, u32[]{:S(2)}) collective-permute-start(bf16[1,3,128,128]{3,2,1,0:T(8,128)(2,1)S(1)} %slice.6), channel_id=1, source_target_pairs={{0,2},{1,3},{2,0},{3,1},{4,6},{5,7},{6,4},{7,5},{8,10},{9,11},{10,... | collective-permute-start | bytes 294920 | tf_op jit(solution)/shard_map/ppermute | solution.py:39
  21.6 0.0 collective-permute-done.7.refs_2_
  21.6 0.0 collective-permute-done.8.refs_3_
  21.6 1.7 %left_products.1.z_ref = bf16[2,3,256,1536]{3,2,1,0:T(8,128)(2,1)S(1)} custom-call(bf16[784,256]{1,0:T(8,128)(2,1)S(1)} %get-tuple-element.28.refs_0_, bf16[784,256]{1,0:T(8,128)(2,1)S(1)} %collective-permute-done.6.refs_1_, bf16[784,256]{1,0:T(8,128)(2,1)S(1)} %collective-permute-done.7.refs_2_, bf16[784,256]{1,0:T(8,128)(2,1)S(1)} %collective-permute-done.8.refs_3_, ...), custom_call_target="tpu_custom_call" | custom-call | flops 1207959552 | bytes 1048576 | tf_op jit(solution)/shard_map/left_products/pallas_call | solution.py:195
  23.3 0.0 collective-permute-done.9.received
  23.3 1.0 %right_products.2 = (f32[3,256,128]{2,1,0:T(8,128)S(1)}, f32[3,256,128]{2,1,0:T(8,128)S(1)}, bf16[3,256,128]{2,1,0:T(8,128)(2,1)S(1)}) custom-call(bf16[2,3,256,1536]{3,2,1,0:T(8,128)(2,1)S(1)} %left_products.1.z_ref, bf16[2,3,128,128]{3,2,1,0:T(8,128)(2,1)S(1)} %pad_maximum_fusion.own, bf16[2,3,128,128]{3,2,1,0:T(8,128)(2,1)S(1)} %collective-permute-done.2.other, ...), custom_call_target="tpu_custom_call" | custom-call | tf_op jit(solution)/shard_map/right_products/pallas_call | solution.py:236
  24.3 0.0 collective-permute-done.5
  24.4 1.1 %collective-permute-start.10 = (bf16[2,3,128,128]{3,2,1,0:T(8,128)(2,1)S(1)}, bf16[2,3,128,128]{3,2,1,0:T(8,128)(2,1)S(1)}, u32[]{:S(2)}, u32[]{:S(2)}) collective-permute-start(bf16[2,3,128,128]{3,2,1,0:T(8,128)(2,1)S(1)} %broadcast_select_fusion), channel_id=1, source_target_pairs={{0,8},{8,0},{16,24},{24,16},{1,9},{9,1},{17,25},{25,17},{2,10},{10... | collective-permute-start | bytes 589832 | tf_op jit(solution)/shard_map/ppermute | solution.py:35
  25.5 1.9 %collective-permute-start.11 = (bf16[3,256,128]{2,1,0:T(8,128)(2,1)S(1)}, bf16[3,256,128]{2,1,0:T(8,128)(2,1)S(1)}, u32[]{:S(2)}, u32[]{:S(2)}) collective-permute-start(bf16[3,256,128]{2,1,0:T(8,128)(2,1)S(1)} %get-tuple-element.38), channel_id=1, source_target_pairs={{1,3},{2,0},{3,5},{4,2},{5,7},{6,4},{9,11},{10,8},{11,13},{12,10},... | collective-permute-start | bytes 589832 | tf_op jit(solution)/shard_map/ppermute | solution.py:347
  27.5 0.0 collective-permute-done.10.received
  27.5 1.0 %right_products.3 = (f32[3,256,128]{2,1,0:T(8,128)S(1)}, bf16[3,256,128]{2,1,0:T(8,128)(2,1)S(1)}, bf16[3,256,128]{2,1,0:T(8,128)(2,1)S(1)}) custom-call(bf16[2,3,256,1536]{3,2,1,0:T(8,128)(2,1)S(1)} %left_products.1.z_ref, bf16[2,3,128,128]{3,2,1,0:T(8,128)(2,1)S(1)} %collective-permute-done.3.own, ...), custom_call_target="tpu_custom_call" | custom-call | tf_op jit(solution)/shard_map/right_products/pallas_call | solution.py:236
  28.4 2.1 %collective-permute-start.13 = (bf16[3,256,128]{2,1,0:T(8,128)(2,1)S(1)}, bf16[3,256,128]{2,1,0:T(8,128)(2,1)S(1)}, u32[]{:S(2)}, u32[]{:S(2)}) collective-permute-start(bf16[3,256,128]{2,1,0:T(8,128)(2,1)S(1)} %get-tuple-element.39), channel_id=1, source_target_pairs={{0,1},{1,0},{2,3},{3,2},{4,5},{5,4},{6,7},{7,6},{8,9},{9,8},{10,11... | collective-permute-start | bytes 589832 | tf_op jit(solution)/shard_map/ppermute | solution.py:350
  30.5 1.9 %collective-permute-start.14 = (bf16[3,256,128]{2,1,0:T(8,128)(2,1)S(1)}, bf16[3,256,128]{2,1,0:T(8,128)(2,1)S(1)}, u32[]{:S(2)}, u32[]{:S(2)}) collective-permute-start(bf16[3,256,128]{2,1,0:T(8,128)(2,1)S(1)} %get-tuple-element.40), channel_id=1, source_target_pairs={{1,2},{2,1},{3,4},{4,3},{5,6},{6,5},{9,10},{10,9},{11,12},{12,11},... | collective-permute-start | bytes 589832 | tf_op jit(solution)/shard_map/ppermute | solution.py:350
  32.5 1.5 %collective-permute-done.11.passing = bf16[3,256,128]{2,1,0:T(8,128)(2,1)S(1)} collective-permute-done((bf16[3,256,128]{2,1,0:T(8,128)(2,1)S(1)}, bf16[3,256,128]{2,1,0:T(8,128)(2,1)S(1)}, u32[]{:S(2)}, u32[]{:S(2)}) %collective-permute-start.11) | collective-permute-done | bytes 196640 | tf_op jit(solution)/shard_map/ppermute | solution.py:347
  34.0 0.6 %collective-permute-start.12 = (bf16[3,256,128]{2,1,0:T(8,128)(2,1)S(1)}, bf16[3,256,128]{2,1,0:T(8,128)(2,1)S(1)}, u32[]{:S(2)}, u32[]{:S(2)}) collective-permute-start(bf16[3,256,128]{2,1,0:T(8,128)(2,1)S(1)} %joined.1), channel_id=1, source_target_pairs={{0,1},{1,0},{2,3},{3,2},{4,5},{5,4},{6,7},{7,6},{8,9},{9,8},{10,11... | collective-permute-start | bytes 589832 | tf_op jit(solution)/shard_map/ppermute | solution.py:357
  34.6 4.0 %collective-permute-done.13.refs_3_ = bf16[3,256,128]{2,1,0:T(8,128)(2,1)S(1)} collective-permute-done((bf16[3,256,128]{2,1,0:T(8,128)(2,1)S(1)}, bf16[3,256,128]{2,1,0:T(8,128)(2,1)S(1)}, u32[]{:S(2)}, u32[]{:S(2)}) %collective-permute-start.13) | collective-permute-done | bytes 196640 | tf_op jit(solution)/shard_map/ppermute | solution.py:350
  38.6 0.6 %collective-permute-done.14.refs_4_ = bf16[3,256,128]{2,1,0:T(8,128)(2,1)S(1)} collective-permute-done((bf16[3,256,128]{2,1,0:T(8,128)(2,1)S(1)}, bf16[3,256,128]{2,1,0:T(8,128)(2,1)S(1)}, u32[]{:S(2)}, u32[]{:S(2)}) %collective-permute-start.14) | collective-permute-done | bytes 196640 | tf_op jit(solution)/shard_map/ppermute | solution.py:350
  39.2 5.1 %collective-permute-done.12.refs_2_ = bf16[3,256,128]{2,1,0:T(8,128)(2,1)S(1)} collective-permute-done((bf16[3,256,128]{2,1,0:T(8,128)(2,1)S(1)}, bf16[3,256,128]{2,1,0:T(8,128)(2,1)S(1)}, u32[]{:S(2)}, u32[]{:S(2)}) %collective-permute-start.12) | collective-permute-done | bytes 196640 | tf_op jit(solution)/shard_map/ppermute | solution.py:357
  44.4 0.8 %summed.1 = bf16[3,256,256]{2,1,0:T(8,128)(2,1)} custom-call(bf16[3,256,128]{2,1,0:T(8,128)(2,1)S(1)} %convert_element_type.3.refs_0_, f32[3,256,128]{2,1,0:T(8,128)S(1)} %get-tuple-element.35.refs_1_, bf16[3,256,128]{2,1,0:T(8,128)(2,1)S(1)} %collective-permute-done.12.refs_2_, bf16[3,256,128]{2,1,0:T(8,128)(2,1)S(1)} %collective-permute-done.13.refs_3_, ...), custom_call_target="tpu_custom_call" | custom-call | tf_op jit(solution)/shard_map/summed/pallas_call | solution.py:293
  (14 shorter events, 0.2 us)
Async XLA Ops:
  0.0 8.6 %collective-permute-start.1 = (bf16[1,3,128,128]{3,2,1,0:T(8,128)(2,1)}, bf16[1,3,128,128]{3,2,1,0:T(8,128)(2,1)S(1)}, u32[]{:S(2)}, u32[]{:S(2)}) collective-permute-start(bf16[1,3,128,128]{3,2,1,0:T(8,128)(2,1)} %bitcast.8), channel_id=1, source_target_pairs={{4,16},{5,17},{6,18},{7,19},{12,24},{13,25},{14,26},{15,27},{16,4}... | collective-permute-start | bytes 294920 | tf_op jit(solution)/shard_map/ppermute | solution.py:58
  2.9 5.8 %collective-permute-start = (bf16[1,3,128,128]{3,2,1,0:T(8,128)(2,1)}, bf16[1,3,128,128]{3,2,1,0:T(8,128)(2,1)S(1)}, u32[]{:S(2)}, u32[]{:S(2)}) collective-permute-start(bf16[1,3,128,128]{3,2,1,0:T(8,128)(2,1)} %bitcast.9), channel_id=1, source_target_pairs={{0,4},{1,5},{2,6},{3,7},{4,20},{5,21},{6,22},{7,23},{8,12},{9,13},... | collective-permute-start | bytes 294920 | tf_op jit(solution)/shard_map/ppermute | solution.py:58
  4.0 12.9 %collective-permute-start.6 = (bf16[784,256]{1,0:T(8,128)(2,1)S(1)}, bf16[784,256]{1,0:T(8,128)(2,1)S(1)}, u32[]{:S(2)}, u32[]{:S(2)}) collective-permute-start(bf16[784,256]{1,0:T(8,128)(2,1)S(1)} %get-tuple-element.28.refs_0_), channel_id=1, source_target_pairs={{0,16},{8,24},{16,0},{24,8},{1,17},{9,25},{17,1},{25,9},{2,18},{10... | collective-permute-start | bytes 1204232 | tf_op jit(solution)/shard_map/ppermute | solution.py:35
  8.7 9.1 %collective-permute-start.3 = (bf16[2,3,128,128]{3,2,1,0:T(8,128)(2,1)S(1)}, bf16[2,3,128,128]{3,2,1,0:T(8,128)(2,1)S(1)}, u32[]{:S(2)}, u32[]{:S(2)}) collective-permute-start(bf16[2,3,128,128]{3,2,1,0:T(8,128)(2,1)S(1)} %pad_maximum_fusion.own), channel_id=1, source_target_pairs={{0,1},{1,0},{2,3},{3,2},{4,5},{5,4},{6,7},{7,6},{8,9},{9,8},{10,11... | collective-permute-start | bytes 589832 | tf_op jit(solution)/shard_map/ppermute | solution.py:39
  10.0 7.8 %collective-permute-start.2 = (bf16[2,3,128,128]{3,2,1,0:T(8,128)(2,1)S(1)}, bf16[2,3,128,128]{3,2,1,0:T(8,128)(2,1)S(1)}, u32[]{:S(2)}, u32[]{:S(2)}) collective-permute-start(bf16[2,3,128,128]{3,2,1,0:T(8,128)(2,1)S(1)} %pad_maximum_fusion.own), channel_id=1, source_target_pairs={{0,2},{1,3},{2,0},{3,1},{4,6},{5,7},{6,4},{7,5},{8,10},{9,11},{10,... | collective-permute-start | bytes 589832 | tf_op jit(solution)/shard_map/ppermute | solution.py:39
  13.3 8.4 %collective-permute-start.7 = (bf16[784,256]{1,0:T(8,128)(2,1)S(1)}, bf16[784,256]{1,0:T(8,128)(2,1)S(1)}, u32[]{:S(2)}, u32[]{:S(2)}) collective-permute-start(bf16[784,256]{1,0:T(8,128)(2,1)S(1)} %get-tuple-element.28.refs_0_), channel_id=1, source_target_pairs={{0,8},{8,0},{16,24},{24,16},{1,9},{9,1},{17,25},{25,17},{2,10},{10... | collective-permute-start | bytes 1204232 | tf_op jit(solution)/shard_map/ppermute | solution.py:35
  16.9 4.7 %collective-permute-start.8 = (bf16[784,256]{1,0:T(8,128)(2,1)S(1)}, bf16[784,256]{1,0:T(8,128)(2,1)S(1)}, u32[]{:S(2)}, u32[]{:S(2)}) collective-permute-start(bf16[784,256]{1,0:T(8,128)(2,1)S(1)} %collective-permute-done.6.refs_1_), channel_id=1, source_target_pairs={{0,8},{8,0},{16,24},{24,16},{1,9},{9,1},{17,25},{25,17},{2,10},{10... | collective-permute-start | bytes 1204232 | tf_op jit(solution)/shard_map/ppermute | solution.py:35
  17.8 5.5 %collective-permute-start.9 = (bf16[2,3,128,128]{3,2,1,0:T(8,128)(2,1)S(1)}, bf16[2,3,128,128]{3,2,1,0:T(8,128)(2,1)S(1)}, u32[]{:S(2)}, u32[]{:S(2)}) collective-permute-start(bf16[2,3,128,128]{3,2,1,0:T(8,128)(2,1)S(1)} %broadcast_select_fusion.1), channel_id=1, source_target_pairs={{0,8},{8,0},{16,24},{24,16},{1,9},{9,1},{17,25},{25,17},{2,10},{10... | collective-permute-start | bytes 589832 | tf_op jit(solution)/shard_map/ppermute | solution.py:35
  19.2 5.1 %collective-permute-start.5 = (bf16[1,3,128,128]{3,2,1,0:T(8,128)(2,1)S(1)}, bf16[1,3,128,128]{3,2,1,0:T(8,128)(2,1)S(1)}, u32[]{:S(2)}, u32[]{:S(2)}) collective-permute-start(bf16[1,3,128,128]{3,2,1,0:T(8,128)(2,1)S(1)} %slice.7), channel_id=1, source_target_pairs={{0,1},{1,0},{2,3},{3,2},{4,5},{5,4},{6,7},{7,6},{8,9},{9,8},{10,11... | collective-permute-start | bytes 294920 | tf_op jit(solution)/shard_map/ppermute | solution.py:39
  19.5 4.8 %collective-permute-start.4 = (bf16[1,3,128,128]{3,2,1,0:T(8,128)(2,1)S(1)}, bf16[1,3,128,128]{3,2,1,0:T(8,128)(2,1)S(1)}, u32[]{:S(2)}, u32[]{:S(2)}) collective-permute-start(bf16[1,3,128,128]{3,2,1,0:T(8,128)(2,1)S(1)} %slice.6), channel_id=1, source_target_pairs={{0,2},{1,3},{2,0},{3,1},{4,6},{5,7},{6,4},{7,5},{8,10},{9,11},{10,... | collective-permute-start | bytes 294920 | tf_op jit(solution)/shard_map/ppermute | solution.py:39
  24.4 3.0 %collective-permute-start.10 = (bf16[2,3,128,128]{3,2,1,0:T(8,128)(2,1)S(1)}, bf16[2,3,128,128]{3,2,1,0:T(8,128)(2,1)S(1)}, u32[]{:S(2)}, u32[]{:S(2)}) collective-permute-start(bf16[2,3,128,128]{3,2,1,0:T(8,128)(2,1)S(1)} %broadcast_select_fusion), channel_id=1, source_target_pairs={{0,8},{8,0},{16,24},{24,16},{1,9},{9,1},{17,25},{25,17},{2,10},{10... | collective-permute-start | bytes 589832 | tf_op jit(solution)/shard_map/ppermute | solution.py:35
  25.5 8.4 %collective-permute-start.11 = (bf16[3,256,128]{2,1,0:T(8,128)(2,1)S(1)}, bf16[3,256,128]{2,1,0:T(8,128)(2,1)S(1)}, u32[]{:S(2)}, u32[]{:S(2)}) collective-permute-start(bf16[3,256,128]{2,1,0:T(8,128)(2,1)S(1)} %get-tuple-element.38), channel_id=1, source_target_pairs={{1,3},{2,0},{3,5},{4,2},{5,7},{6,4},{9,11},{10,8},{11,13},{12,10},... | collective-permute-start | bytes 589832 | tf_op jit(solution)/shard_map/ppermute | solution.py:347
  28.4 10.1 %collective-permute-start.13 = (bf16[3,256,128]{2,1,0:T(8,128)(2,1)S(1)}, bf16[3,256,128]{2,1,0:T(8,128)(2,1)S(1)}, u32[]{:S(2)}, u32[]{:S(2)}) collective-permute-start(bf16[3,256,128]{2,1,0:T(8,128)(2,1)S(1)} %get-tuple-element.39), channel_id=1, source_target_pairs={{0,1},{1,0},{2,3},{3,2},{4,5},{5,4},{6,7},{7,6},{8,9},{9,8},{10,11... | collective-permute-start | bytes 589832 | tf_op jit(solution)/shard_map/ppermute | solution.py:350
  30.5 8.7 %collective-permute-start.14 = (bf16[3,256,128]{2,1,0:T(8,128)(2,1)S(1)}, bf16[3,256,128]{2,1,0:T(8,128)(2,1)S(1)}, u32[]{:S(2)}, u32[]{:S(2)}) collective-permute-start(bf16[3,256,128]{2,1,0:T(8,128)(2,1)S(1)} %get-tuple-element.40), channel_id=1, source_target_pairs={{1,2},{2,1},{3,4},{4,3},{5,6},{6,5},{9,10},{10,9},{11,12},{12,11},... | collective-permute-start | bytes 589832 | tf_op jit(solution)/shard_map/ppermute | solution.py:350
  34.0 10.4 %collective-permute-start.12 = (bf16[3,256,128]{2,1,0:T(8,128)(2,1)S(1)}, bf16[3,256,128]{2,1,0:T(8,128)(2,1)S(1)}, u32[]{:S(2)}, u32[]{:S(2)}) collective-permute-start(bf16[3,256,128]{2,1,0:T(8,128)(2,1)S(1)} %joined.1), channel_id=1, source_target_pairs={{0,1},{1,0},{2,3},{3,2},{4,5},{5,4},{6,7},{7,6},{8,9},{9,8},{10,11... | collective-permute-start | bytes 589832 | tf_op jit(solution)/shard_map/ppermute | solution.py:357

commit v8 on v7

--- a/solution.py
+++ b/solution.py
@@ -261,26 +261,24 @@
     )(low, passing)
 
 
-def sum_kernel(per, direct, *refs):
-    *parts, out_hbm, out_ref, sems = refs
-    zeros, lows, highs = parts[:per], parts[per : 2 * per], dict(zip(direct, parts[2 * per :]))
+def early_kernel(per, through, *refs):
+    parts, outs = refs[: len(refs) - per], refs[len(refs) - per :]
+    direct = [cls for cls in range(per) if cls not in through]
+    zeros, lows, highs = parts[:per], dict(zip(direct, parts[per:])), dict(zip(direct, parts[per + len(direct) :]))
     sec = lax.axis_index("sec")
     beyond = (sec ^ ((((sec + 1) ^ 1) + per - 1) % per)) % per
-    copies = [pltpu.make_async_copy(out_ref.at[v], out_hbm.at[v], sems.at[v]) for v in range(VECS)]
 
     def add(high):
         @pl.when(beyond == high)
         def _():
-            for v in range(VECS):
-                for cls in range(per):
-                    column = pl.multiple_of(((sec % per) ^ cls) * MR, MR)
-                    total = zeros[cls][v].astype(jnp.float32) + lows[cls ^ 1][v].astype(jnp.float32)
+            for cls in range(per):
+                for v in range(VECS):
+                    total = zeros[cls][v].astype(jnp.float32)
+                    if cls ^ 1 in lows:
+                        total = total + lows[cls ^ 1][v].astype(jnp.float32)
                     if cls ^ high in highs:
                         total = total + highs[cls ^ high][v].astype(jnp.float32)
-                    out_ref[v, :, pl.ds(column, MR)] = total.astype(jnp.bfloat16)
-                copies[v].start()
-            for copy in copies:
-                copy.wait()
+                    outs[cls][v] = total.astype(outs[cls].dtype)
 
     carry = 1
     while carry < per:
@@ -288,17 +286,46 @@
         carry = 2 * carry + 1
 
 
-def summed(per, direct, parts):
-    shape = (VECS, ML, per * MR)
-    return pl.pallas_call(
-        functools.partial(sum_kernel, per, direct),
-        out_shape=jax.ShapeDtypeStruct(shape, jnp.bfloat16),
+def early_sums(per, through, parts):
+    block = (VECS, ML, MR)
+    return pl.pallas_call(
+        functools.partial(early_kernel, per, through),
+        out_shape=[in_vmem(block, jnp.float32 if cls ^ 1 in through else jnp.bfloat16) for cls in range(per)],
         in_specs=[VMEM] * len(parts),
+        out_specs=[VMEM] * per,
+        compiler_params=grant(8),
+        cost_estimate=cost(0, 0),
+        name="early_sums",
+    )(*parts)
+
+
+def sum_kernel(per, through, *refs):
+    sums, lows = refs[:per], dict(zip(through, refs[per:]))
+    out_hbm, late, sems = refs[per + len(through) :]
+    sec = lax.axis_index("sec")
+    copies = []
+    for cls in sorted(range(per), key=lambda c: c ^ 1 in lows):
+        column = pl.multiple_of(((sec % per) ^ cls) * MR, MR)
+        source = sums[cls]
+        if cls ^ 1 in lows:
+            source = late.at[cls]
+            late[cls] = (sums[cls][...] + lows[cls ^ 1][...].astype(jnp.float32)).astype(jnp.bfloat16)
+        copies.append(pltpu.make_async_copy(source, out_hbm.at[:, :, pl.ds(column, MR)], sems.at[cls]))
+        copies[-1].start()
+    for copy in copies:
+        copy.wait()
+
+
+def summed(per, through, sums, lows):
+    return pl.pallas_call(
+        functools.partial(sum_kernel, per, through),
+        out_shape=jax.ShapeDtypeStruct((VECS, ML, per * MR), jnp.bfloat16),
+        in_specs=[VMEM] * (len(sums) + len(lows)),
         out_specs=HBM,
-        scratch_shapes=[in_vmem(shape), pltpu.SemaphoreType.DMA((VECS,))],
+        scratch_shapes=[in_vmem((per, VECS, ML, MR)), pltpu.SemaphoreType.DMA((per,))],
         compiler_params=grant(8),
         name="summed",
-    )(*parts)
+    )(*sums, *lows)
 
 
 def on_device(n_op, n_sec, wavefunction, left_ops, right_ops, term_shift):
@@ -322,7 +349,7 @@
     while bit < per:
         owns = owns + [over_sec(c, n_sec, bit) for c in owns]
         bit *= 2
-    other, owns = tie((over_sec(owns[0], n_sec, per), owns))
+    other, owns[1:] = tie((over_sec(owns[0], n_sec, per), owns[1:]))
     z = left_products(lefts, window)
     low = [(d, d ^ 1) for d in range(n_sec)]
     high = [(d, ((d + 1) ^ 1) - 1) for d in range(1, n_sec - 1)]
@@ -355,11 +382,10 @@
     for cls in through:
         own_low = tie((parts[3 * cls + 1], parts[3]))[0]
         lows.append(lax.ppermute(joined(own_low, parts[3 * (cls ^ turn) + 2]), "sec", low))
-    for cls, part in zip(through, lows):
-        parts[3 * cls + 1] = part
     direct = [cls for cls in range(per) if cls not in through]
-    parts = parts[::3] + parts[1::3] + [parts[3 * cls + 2] for cls in direct]
-    return summed(per, direct, parts).transpose(1, 0, 2)
+    parts = parts[::3] + [parts[3 * cls + 1] for cls in direct] + [parts[3 * cls + 2] for cls in direct]
+    sums = early_sums(per, through, parts)
+    return summed(per, through, sums, lows).transpose(1, 0, 2)
 
 
 def solution(mesh):

time: 45.4 us -> 45.4 us (level)
  no operation moved by 1% of the time
where the time goes in v8:
time: 45.4 us; the launch traced here: 45.1 us
  starting transfers between devices  23.8 us (52%)
  waiting for transfers between devices  13.5 us (30%)
  Pallas kernels  7.49 us (16%)
    ppermute x5, starting transfers between devices, over_op(): return lax.ppermute(x, 'op', [(o, o ^ bit) for o in range(n_op)])  7.25 us
    ppermute x4, starting transfers between devices, over_sec(): return lax.ppermute(x, 'sec', [(d, d ^ bit) for d in range(n_sec)])  6.94 us
    ppermute x1, waiting for transfers between devices, on_device(): lax.ppermute(joined(own_low, parts[3 * (cls ^ turn) + 2]), 'sec', low)  5.04 us
    ppermute x1, waiting for transfers between devices, on_device(): lax.ppermute(to_low, 'sec', low)  3.97 us
    ppermute x1, starting transfers between devices, towards_owner(): lax.ppermute(held, ('op', 'sec'), second)  2.88 us
    ppermute x5, waiting for transfers between devices, over_op(): return lax.ppermute(x, 'op', [(o, o ^ bit) for o in range(n_op)])  2.42 us
    ppermute x1, starting transfers between devices, on_device(): lax.ppermute(to_low, 'sec', low)  2.14 us
    pallas_call x1, Pallas kernels, window_of(): pl.pallas_call(functools.partial(window_kernel, n_op), out_shape=in_vmem(...  2 us
  transfers between devices with their start and end apart: 15, of which 5 were waited for; matrix products, arithmetic and copies ran while one was open for 0% of the time, Pallas kernels for 15%

profile of v8, /device:TPU:17, one launch (start us, length us, event | category | flops | bytes accessed | tf_op | source)
XLA Modules:
  0.0 45.1 jit_solution(15407857559812510338)
XLA Ops:
  0.0 2.9 %collective-permute-start.1 = (bf16[1,3,128,128]{3,2,1,0:T(8,128)(2,1)}, bf16[1,3,128,128]{3,2,1,0:T(8,128)(2,1)S(1)}, u32[]{:S(2)}, u32[]{:S(2)}) collective-permute-start(bf16[1,3,128,128]{3,2,1,0:T(8,128)(2,1)} %bitcast.8), channel_id=1, source_target_pairs={{4,16},{5,17},{6,18},{7,19},{12,24},{13,25},{14,26},{15,27},{16,4}... | collective-permute-start | bytes 294920 | tf_op jit(solution)/shard_map/ppermute | solution.py:58
  2.9 0.1 collective-permute-start
  3.0 1.0 %pack.1 = (bf16[784,256]{1,0:T(8,128)(2,1)S(1)}, bf16[1,3,128,128]{3,2,1,0:T(8,128)(2,1)S(1)}) custom-call(s32[3]{0:T(128)} %shift.1, bf16[768,256]{1,0:T(8,128)(2,1)} %bitcast.7, bf16[1,3,128,128]{3,2,1,0:T(8,128)(2,1)} %bitcast.10), custom_call_target="tpu_custom_call" | custom-call | bytes 33554432 | tf_op jit(solution)/shard_map/pack/pallas_call | solution.py:122
  4.0 2.6 %collective-permute-start.6 = (bf16[784,256]{1,0:T(8,128)(2,1)S(1)}, bf16[784,256]{1,0:T(8,128)(2,1)S(1)}, u32[]{:S(2)}, u32[]{:S(2)}) collective-permute-start(bf16[784,256]{1,0:T(8,128)(2,1)S(1)} %get-tuple-element.29.refs_0_), channel_id=1, source_target_pairs={{0,16},{8,24},{16,0},{24,8},{1,17},{9,25},{17,1},{25,9},{2,18},{10... | collective-permute-start | bytes 1204232 | tf_op jit(solution)/shard_map/ppermute | solution.py:35
  6.6 2.0 %window.1.refs_4_ = bf16[3,256,512]{2,1,0:T(8,128)(2,1)S(1)} custom-call(bf16[3,256,1024]{2,1,0:T(8,128)(2,1)} %bitcast.6), custom_call_target="tpu_custom_call" | custom-call | bytes 2097152 | tf_op jit(solution)/shard_map/window/pallas_call | solution.py:163
  8.6 0.0 collective-permute-done.1
  8.7 1.3 %collective-permute-start.3 = (bf16[2,3,128,128]{3,2,1,0:T(8,128)(2,1)S(1)}, bf16[2,3,128,128]{3,2,1,0:T(8,128)(2,1)S(1)}, u32[]{:S(2)}, u32[]{:S(2)}) collective-permute-start(bf16[2,3,128,128]{3,2,1,0:T(8,128)(2,1)S(1)} %pad_maximum_fusion.own), channel_id=1, source_target_pairs={{0,1},{1,0},{2,3},{3,2},{4,5},{5,4},{6,7},{7,6},{8,9},{9,8},{10,11... | collective-permute-start | bytes 589832 | tf_op jit(solution)/shard_map/ppermute | solution.py:39
  10.0 3.2 %collective-permute-start.2 = (bf16[2,3,128,128]{3,2,1,0:T(8,128)(2,1)S(1)}, bf16[2,3,128,128]{3,2,1,0:T(8,128)(2,1)S(1)}, u32[]{:S(2)}, u32[]{:S(2)}) collective-permute-start(bf16[2,3,128,128]{3,2,1,0:T(8,128)(2,1)S(1)} %pad_maximum_fusion.own), channel_id=1, source_target_pairs={{0,2},{1,3},{2,0},{3,1},{4,6},{5,7},{6,4},{7,5},{8,10},{9,11},{10,... | collective-permute-start | bytes 589832 | tf_op jit(solution)/shard_map/ppermute | solution.py:39
  13.3 1.2 %collective-permute-start.7 = (bf16[784,256]{1,0:T(8,128)(2,1)S(1)}, bf16[784,256]{1,0:T(8,128)(2,1)S(1)}, u32[]{:S(2)}, u32[]{:S(2)}) collective-permute-start(bf16[784,256]{1,0:T(8,128)(2,1)S(1)} %get-tuple-element.29.refs_0_), channel_id=1, source_target_pairs={{0,8},{8,0},{16,24},{24,16},{1,9},{9,1},{17,25},{25,17},{2,10},{10... | collective-permute-start | bytes 1204232 | tf_op jit(solution)/shard_map/ppermute | solution.py:35
  14.5 2.4 %collective-permute-done.6.refs_1_ = bf16[784,256]{1,0:T(8,128)(2,1)S(1)} collective-permute-done((bf16[784,256]{1,0:T(8,128)(2,1)S(1)}, bf16[784,256]{1,0:T(8,128)(2,1)S(1)}, u32[]{:S(2)}, u32[]{:S(2)}) %collective-permute-start.6) | collective-permute-done | bytes 401440 | tf_op jit(solution)/shard_map/ppermute | solution.py:35
  16.9 0.9 %collective-permute-start.8 = (bf16[784,256]{1,0:T(8,128)(2,1)S(1)}, bf16[784,256]{1,0:T(8,128)(2,1)S(1)}, u32[]{:S(2)}, u32[]{:S(2)}) collective-permute-start(bf16[784,256]{1,0:T(8,128)(2,1)S(1)} %collective-permute-done.6.refs_1_), channel_id=1, source_target_pairs={{0,8},{8,0},{16,24},{24,16},{1,9},{9,1},{17,25},{25,17},{2,10},{10... | collective-permute-start | bytes 1204232 | tf_op jit(solution)/shard_map/ppermute | solution.py:35
  17.8 1.4 %collective-permute-start.9 = (bf16[2,3,128,128]{3,2,1,0:T(8,128)(2,1)S(1)}, bf16[2,3,128,128]{3,2,1,0:T(8,128)(2,1)S(1)}, u32[]{:S(2)}, u32[]{:S(2)}) collective-permute-start(bf16[2,3,128,128]{3,2,1,0:T(8,128)(2,1)S(1)} %broadcast_select_fusion.1), channel_id=1, source_target_pairs={{0,8},{8,0},{16,24},{24,16},{1,9},{9,1},{17,25},{25,17},{2,10},{10... | collective-permute-start | bytes 589832 | tf_op jit(solution)/shard_map/ppermute | solution.py:35
  19.2 0.3 collective-permute-start.5
  19.5 2.1 %collective-permute-start.4 = (bf16[1,3,128,128]{3,2,1,0:T(8,128)(2,1)S(1)}, bf16[1,3,128,128]{3,2,1,0:T(8,128)(2,1)S(1)}, u32[]{:S(2)}, u32[]{:S(2)}) collective-permute-start(bf16[1,3,128,128]{3,2,1,0:T(8,128)(2,1)S(1)} %slice.6), channel_id=1, source_target_pairs={{0,2},{1,3},{2,0},{3,1},{4,6},{5,7},{6,4},{7,5},{8,10},{9,11},{10,... | collective-permute-start | bytes 294920 | tf_op jit(solution)/shard_map/ppermute | solution.py:39
  21.6 0.0 collective-permute-done.7.refs_2_
  21.6 0.0 collective-permute-done.8.refs_3_
  21.6 1.6 %left_products.1.z_ref = bf16[2,3,256,1536]{3,2,1,0:T(8,128)(2,1)S(1)} custom-call(bf16[784,256]{1,0:T(8,128)(2,1)S(1)} %get-tuple-element.29.refs_0_, bf16[784,256]{1,0:T(8,128)(2,1)S(1)} %collective-permute-done.6.refs_1_, bf16[784,256]{1,0:T(8,128)(2,1)S(1)} %collective-permute-done.7.refs_2_, bf16[784,256]{1,0:T(8,128)(2,1)S(1)} %collective-permute-done.8.refs_3_, ...), custom_call_target="tpu_custom_call" | custom-call | flops 1207959552 | bytes 1048576 | tf_op jit(solution)/shard_map/left_products/pallas_call | solution.py:195
  23.3 1.0 %right_products.2 = (f32[3,256,128]{2,1,0:T(8,128)S(1)}, f32[3,256,128]{2,1,0:T(8,128)S(1)}, bf16[3,256,128]{2,1,0:T(8,128)(2,1)S(1)}) custom-call(bf16[2,3,256,1536]{3,2,1,0:T(8,128)(2,1)S(1)} %left_products.1.z_ref, bf16[2,3,128,128]{3,2,1,0:T(8,128)(2,1)S(1)} %pad_maximum_fusion.own, bf16[2,3,128,128]{3,2,1,0:T(8,128)(2,1)S(1)} %collective-permute-done.2.other, ...), custom_call_target="tpu_custom_call" | custom-call | tf_op jit(solution)/shard_map/right_products/pallas_call | solution.py:236
  24.3 0.0 collective-permute-done.5
  24.3 0.0 collective-permute-done.4
  24.4 1.1 %collective-permute-start.10 = (bf16[2,3,128,128]{3,2,1,0:T(8,128)(2,1)S(1)}, bf16[2,3,128,128]{3,2,1,0:T(8,128)(2,1)S(1)}, u32[]{:S(2)}, u32[]{:S(2)}) collective-permute-start(bf16[2,3,128,128]{3,2,1,0:T(8,128)(2,1)S(1)} %broadcast_select_fusion), channel_id=1, source_target_pairs={{0,8},{8,0},{16,24},{24,16},{1,9},{9,1},{17,25},{25,17},{2,10},{10... | collective-permute-start | bytes 589832 | tf_op jit(solution)/shard_map/ppermute | solution.py:35
  25.5 1.9 %collective-permute-start.13 = (bf16[3,256,128]{2,1,0:T(8,128)(2,1)S(1)}, bf16[3,256,128]{2,1,0:T(8,128)(2,1)S(1)}, u32[]{:S(2)}, u32[]{:S(2)}) collective-permute-start(bf16[3,256,128]{2,1,0:T(8,128)(2,1)S(1)} %get-tuple-element.42), channel_id=1, source_target_pairs={{1,3},{2,0},{3,5},{4,2},{5,7},{6,4},{9,11},{10,8},{11,13},{12,10},... | collective-permute-start | bytes 589832 | tf_op jit(solution)/shard_map/ppermute | solution.py:374
  27.4 1.0 %right_products.3 = (f32[3,256,128]{2,1,0:T(8,128)S(1)}, bf16[3,256,128]{2,1,0:T(8,128)(2,1)S(1)}, bf16[3,256,128]{2,1,0:T(8,128)(2,1)S(1)}) custom-call(bf16[2,3,256,1536]{3,2,1,0:T(8,128)(2,1)S(1)} %left_products.1.z_ref, bf16[2,3,128,128]{3,2,1,0:T(8,128)(2,1)S(1)} %collective-permute-done.3.own, ...), custom_call_target="tpu_custom_call" | custom-call | tf_op jit(solution)/shard_map/right_products/pallas_call | solution.py:236
  28.4 2.1 %collective-permute-start.11 = (bf16[3,256,128]{2,1,0:T(8,128)(2,1)S(1)}, bf16[3,256,128]{2,1,0:T(8,128)(2,1)S(1)}, u32[]{:S(2)}, u32[]{:S(2)}) collective-permute-start(bf16[3,256,128]{2,1,0:T(8,128)(2,1)S(1)} %get-tuple-element.36), channel_id=1, source_target_pairs={{0,1},{1,0},{2,3},{3,2},{4,5},{5,4},{6,7},{7,6},{8,9},{9,8},{10,11... | collective-permute-start | bytes 589832 | tf_op jit(solution)/shard_map/ppermute | solution.py:377
  30.5 1.9 %collective-permute-start.12 = (bf16[3,256,128]{2,1,0:T(8,128)(2,1)S(1)}, bf16[3,256,128]{2,1,0:T(8,128)(2,1)S(1)}, u32[]{:S(2)}, u32[]{:S(2)}) collective-permute-start(bf16[3,256,128]{2,1,0:T(8,128)(2,1)S(1)} %get-tuple-element.37), channel_id=1, source_target_pairs={{1,2},{2,1},{3,4},{4,3},{5,6},{6,5},{9,10},{10,9},{11,12},{12,11},... | collective-permute-start | bytes 589832 | tf_op jit(solution)/shard_map/ppermute | solution.py:377
  32.5 1.4 %collective-permute-done.13.passing = bf16[3,256,128]{2,1,0:T(8,128)(2,1)S(1)} collective-permute-done((bf16[3,256,128]{2,1,0:T(8,128)(2,1)S(1)}, bf16[3,256,128]{2,1,0:T(8,128)(2,1)S(1)}, u32[]{:S(2)}, u32[]{:S(2)}) %collective-permute-start.13) | collective-permute-done | bytes 196640 | tf_op jit(solution)/shard_map/ppermute | solution.py:374
  33.9 0.7 %collective-permute-start.14 = (bf16[3,256,128]{2,1,0:T(8,128)(2,1)S(1)}, bf16[3,256,128]{2,1,0:T(8,128)(2,1)S(1)}, u32[]{:S(2)}, u32[]{:S(2)}) collective-permute-start(bf16[3,256,128]{2,1,0:T(8,128)(2,1)S(1)} %joined.1), channel_id=1, source_target_pairs={{0,1},{1,0},{2,3},{3,2},{4,5},{5,4},{6,7},{7,6},{8,9},{9,8},{10,11... | collective-permute-start | bytes 589832 | tf_op jit(solution)/shard_map/ppermute | solution.py:384
  34.6 4.0 %collective-permute-done.11.refs_2_ = bf16[3,256,128]{2,1,0:T(8,128)(2,1)S(1)} collective-permute-done((bf16[3,256,128]{2,1,0:T(8,128)(2,1)S(1)}, bf16[3,256,128]{2,1,0:T(8,128)(2,1)S(1)}, u32[]{:S(2)}, u32[]{:S(2)}) %collective-permute-start.11) | collective-permute-done | bytes 196640 | tf_op jit(solution)/shard_map/ppermute | solution.py:377
  38.6 0.6 %collective-permute-done.12.refs_3_ = bf16[3,256,128]{2,1,0:T(8,128)(2,1)S(1)} collective-permute-done((bf16[3,256,128]{2,1,0:T(8,128)(2,1)S(1)}, bf16[3,256,128]{2,1,0:T(8,128)(2,1)S(1)}, u32[]{:S(2)}, u32[]{:S(2)}) %collective-permute-start.12) | collective-permute-done | bytes 196640 | tf_op jit(solution)/shard_map/ppermute | solution.py:377
  39.2 0.1 early_sums.1
  39.3 5.0 %collective-permute-done.14.refs_2_ = bf16[3,256,128]{2,1,0:T(8,128)(2,1)S(1)} collective-permute-done((bf16[3,256,128]{2,1,0:T(8,128)(2,1)S(1)}, bf16[3,256,128]{2,1,0:T(8,128)(2,1)S(1)}, u32[]{:S(2)}, u32[]{:S(2)}) %collective-permute-start.14) | collective-permute-done | bytes 196640 | tf_op jit(solution)/shard_map/ppermute | solution.py:384
  44.4 0.8 %summed.1 = bf16[3,256,256]{2,1,0:T(8,128)(2,1)} custom-call(bf16[3,256,128]{2,1,0:T(8,128)(2,1)S(1)} %get-tuple-element.38.refs_0_, f32[3,256,128]{2,1,0:T(8,128)S(1)} %get-tuple-element.39.refs_1_, bf16[3,256,128]{2,1,0:T(8,128)(2,1)S(1)} %collective-permute-done.14.refs_2_), custom_call_target="tpu_custom_call" | custom-call | tf_op jit(solution)/shard_map/summed/pallas_call | solution.py:320
  (15 shorter events, 0.2 us)
Async XLA Ops:
  0.0 8.6 %collective-permute-start.1 = (bf16[1,3,128,128]{3,2,1,0:T(8,128)(2,1)}, bf16[1,3,128,128]{3,2,1,0:T(8,128)(2,1)S(1)}, u32[]{:S(2)}, u32[]{:S(2)}) collective-permute-start(bf16[1,3,128,128]{3,2,1,0:T(8,128)(2,1)} %bitcast.8), channel_id=1, source_target_pairs={{4,16},{5,17},{6,18},{7,19},{12,24},{13,25},{14,26},{15,27},{16,4}... | collective-permute-start | bytes 294920 | tf_op jit(solution)/shard_map/ppermute | solution.py:58
  2.9 5.8 %collective-permute-start = (bf16[1,3,128,128]{3,2,1,0:T(8,128)(2,1)}, bf16[1,3,128,128]{3,2,1,0:T(8,128)(2,1)S(1)}, u32[]{:S(2)}, u32[]{:S(2)}) collective-permute-start(bf16[1,3,128,128]{3,2,1,0:T(8,128)(2,1)} %bitcast.9), channel_id=1, source_target_pairs={{0,4},{1,5},{2,6},{3,7},{4,20},{5,21},{6,22},{7,23},{8,12},{9,13},... | collective-permute-start | bytes 294920 | tf_op jit(solution)/shard_map/ppermute | solution.py:58
  4.0 12.9 %collective-permute-start.6 = (bf16[784,256]{1,0:T(8,128)(2,1)S(1)}, bf16[784,256]{1,0:T(8,128)(2,1)S(1)}, u32[]{:S(2)}, u32[]{:S(2)}) collective-permute-start(bf16[784,256]{1,0:T(8,128)(2,1)S(1)} %get-tuple-element.29.refs_0_), channel_id=1, source_target_pairs={{0,16},{8,24},{16,0},{24,8},{1,17},{9,25},{17,1},{25,9},{2,18},{10... | collective-permute-start | bytes 1204232 | tf_op jit(solution)/shard_map/ppermute | solution.py:35
  8.7 9.1 %collective-permute-start.3 = (bf16[2,3,128,128]{3,2,1,0:T(8,128)(2,1)S(1)}, bf16[2,3,128,128]{3,2,1,0:T(8,128)(2,1)S(1)}, u32[]{:S(2)}, u32[]{:S(2)}) collective-permute-start(bf16[2,3,128,128]{3,2,1,0:T(8,128)(2,1)S(1)} %pad_maximum_fusion.own), channel_id=1, source_target_pairs={{0,1},{1,0},{2,3},{3,2},{4,5},{5,4},{6,7},{7,6},{8,9},{9,8},{10,11... | collective-permute-start | bytes 589832 | tf_op jit(solution)/shard_map/ppermute | solution.py:39
  10.0 7.8 %collective-permute-start.2 = (bf16[2,3,128,128]{3,2,1,0:T(8,128)(2,1)S(1)}, bf16[2,3,128,128]{3,2,1,0:T(8,128)(2,1)S(1)}, u32[]{:S(2)}, u32[]{:S(2)}) collective-permute-start(bf16[2,3,128,128]{3,2,1,0:T(8,128)(2,1)S(1)} %pad_maximum_fusion.own), channel_id=1, source_target_pairs={{0,2},{1,3},{2,0},{3,1},{4,6},{5,7},{6,4},{7,5},{8,10},{9,11},{10,... | collective-permute-start | bytes 589832 | tf_op jit(solution)/shard_map/ppermute | solution.py:39
  13.3 8.4 %collective-permute-start.7 = (bf16[784,256]{1,0:T(8,128)(2,1)S(1)}, bf16[784,256]{1,0:T(8,128)(2,1)S(1)}, u32[]{:S(2)}, u32[]{:S(2)}) collective-permute-start(bf16[784,256]{1,0:T(8,128)(2,1)S(1)} %get-tuple-element.29.refs_0_), channel_id=1, source_target_pairs={{0,8},{8,0},{16,24},{24,16},{1,9},{9,1},{17,25},{25,17},{2,10},{10... | collective-permute-start | bytes 1204232 | tf_op jit(solution)/shard_map/ppermute | solution.py:35
  16.9 4.8 %collective-permute-start.8 = (bf16[784,256]{1,0:T(8,128)(2,1)S(1)}, bf16[784,256]{1,0:T(8,128)(2,1)S(1)}, u32[]{:S(2)}, u32[]{:S(2)}) collective-permute-start(bf16[784,256]{1,0:T(8,128)(2,1)S(1)} %collective-permute-done.6.refs_1_), channel_id=1, source_target_pairs={{0,8},{8,0},{16,24},{24,16},{1,9},{9,1},{17,25},{25,17},{2,10},{10... | collective-permute-start | bytes 1204232 | tf_op jit(solution)/shard_map/ppermute | solution.py:35
  17.8 5.4 %collective-permute-start.9 = (bf16[2,3,128,128]{3,2,1,0:T(8,128)(2,1)S(1)}, bf16[2,3,128,128]{3,2,1,0:T(8,128)(2,1)S(1)}, u32[]{:S(2)}, u32[]{:S(2)}) collective-permute-start(bf16[2,3,128,128]{3,2,1,0:T(8,128)(2,1)S(1)} %broadcast_select_fusion.1), channel_id=1, source_target_pairs={{0,8},{8,0},{16,24},{24,16},{1,9},{9,1},{17,25},{25,17},{2,10},{10... | collective-permute-start | bytes 589832 | tf_op jit(solution)/shard_map/ppermute | solution.py:35
  19.2 5.1 %collective-permute-start.5 = (bf16[1,3,128,128]{3,2,1,0:T(8,128)(2,1)S(1)}, bf16[1,3,128,128]{3,2,1,0:T(8,128)(2,1)S(1)}, u32[]{:S(2)}, u32[]{:S(2)}) collective-permute-start(bf16[1,3,128,128]{3,2,1,0:T(8,128)(2,1)S(1)} %slice.7), channel_id=1, source_target_pairs={{0,1},{1,0},{2,3},{3,2},{4,5},{5,4},{6,7},{7,6},{8,9},{9,8},{10,11... | collective-permute-start | bytes 294920 | tf_op jit(solution)/shard_map/ppermute | solution.py:39
  19.5 4.8 %collective-permute-start.4 = (bf16[1,3,128,128]{3,2,1,0:T(8,128)(2,1)S(1)}, bf16[1,3,128,128]{3,2,1,0:T(8,128)(2,1)S(1)}, u32[]{:S(2)}, u32[]{:S(2)}) collective-permute-start(bf16[1,3,128,128]{3,2,1,0:T(8,128)(2,1)S(1)} %slice.6), channel_id=1, source_target_pairs={{0,2},{1,3},{2,0},{3,1},{4,6},{5,7},{6,4},{7,5},{8,10},{9,11},{10,... | collective-permute-start | bytes 294920 | tf_op jit(solution)/shard_map/ppermute | solution.py:39
  24.4 3.1 %collective-permute-start.10 = (bf16[2,3,128,128]{3,2,1,0:T(8,128)(2,1)S(1)}, bf16[2,3,128,128]{3,2,1,0:T(8,128)(2,1)S(1)}, u32[]{:S(2)}, u32[]{:S(2)}) collective-permute-start(bf16[2,3,128,128]{3,2,1,0:T(8,128)(2,1)S(1)} %broadcast_select_fusion), channel_id=1, source_target_pairs={{0,8},{8,0},{16,24},{24,16},{1,9},{9,1},{17,25},{25,17},{2,10},{10... | collective-permute-start | bytes 589832 | tf_op jit(solution)/shard_map/ppermute | solution.py:35
  25.5 8.4 %collective-permute-start.13 = (bf16[3,256,128]{2,1,0:T(8,128)(2,1)S(1)}, bf16[3,256,128]{2,1,0:T(8,128)(2,1)S(1)}, u32[]{:S(2)}, u32[]{:S(2)}) collective-permute-start(bf16[3,256,128]{2,1,0:T(8,128)(2,1)S(1)} %get-tuple-element.42), channel_id=1, source_target_pairs={{1,3},{2,0},{3,5},{4,2},{5,7},{6,4},{9,11},{10,8},{11,13},{12,10},... | collective-permute-start | bytes 589832 | tf_op jit(solution)/shard_map/ppermute | solution.py:374
  28.4 10.2 %collective-permute-start.11 = (bf16[3,256,128]{2,1,0:T(8,128)(2,1)S(1)}, bf16[3,256,128]{2,1,0:T(8,128)(2,1)S(1)}, u32[]{:S(2)}, u32[]{:S(2)}) collective-permute-start(bf16[3,256,128]{2,1,0:T(8,128)(2,1)S(1)} %get-tuple-element.36), channel_id=1, source_target_pairs={{0,1},{1,0},{2,3},{3,2},{4,5},{5,4},{6,7},{7,6},{8,9},{9,8},{10,11... | collective-permute-start | bytes 589832 | tf_op jit(solution)/shard_map/ppermute | solution.py:377
  30.5 8.7 %collective-permute-start.12 = (bf16[3,256,128]{2,1,0:T(8,128)(2,1)S(1)}, bf16[3,256,128]{2,1,0:T(8,128)(2,1)S(1)}, u32[]{:S(2)}, u32[]{:S(2)}) collective-permute-start(bf16[3,256,128]{2,1,0:T(8,128)(2,1)S(1)} %get-tuple-element.37), channel_id=1, source_target_pairs={{1,2},{2,1},{3,4},{4,3},{5,6},{6,5},{9,10},{10,9},{11,12},{12,11},... | collective-permute-start | bytes 589832 | tf_op jit(solution)/shard_map/ppermute | solution.py:377
  33.9 10.4 %collective-permute-start.14 = (bf16[3,256,128]{2,1,0:T(8,128)(2,1)S(1)}, bf16[3,256,128]{2,1,0:T(8,128)(2,1)S(1)}, u32[]{:S(2)}, u32[]{:S(2)}) collective-permute-start(bf16[3,256,128]{2,1,0:T(8,128)(2,1)S(1)} %joined.1), channel_id=1, source_target_pairs={{0,1},{1,0},{2,3},{3,2},{4,5},{5,4},{6,7},{7,6},{8,9},{9,8},{10,11... | collective-permute-start | bytes 589832 | tf_op jit(solution)/shard_map/ppermute | solution.py:384

commit v9 on v7

--- a/solution.py
+++ b/solution.py
@@ -322,7 +322,7 @@
     while bit < per:
         owns = owns + [over_sec(c, n_sec, bit) for c in owns]
         bit *= 2
-    other, owns = tie((over_sec(owns[0], n_sec, per), owns))
+    other, owns[1:] = tie((over_sec(owns[0], n_sec, per), owns[1:]))
     z = left_products(lefts, window)
     low = [(d, d ^ 1) for d in range(n_sec)]
     high = [(d, ((d + 1) ^ 1) - 1) for d in range(1, n_sec - 1)]

time: 45.4 us -> 45.4 us (level)
  no operation moved by 1% of the time
where the time goes in v9:
time: 45.4 us; the launch traced here: 45.2 us
  starting transfers between devices  23.7 us (52%)
  waiting for transfers between devices  13.6 us (30%)
  Pallas kernels  7.47 us (16%)
    ppermute x5, starting transfers between devices, over_op(): return lax.ppermute(x, 'op', [(o, o ^ bit) for o in range(n_op)])  7.22 us
    ppermute x4, starting transfers between devices, over_sec(): return lax.ppermute(x, 'sec', [(d, d ^ bit) for d in range(n_sec)])  6.94 us
    ppermute x1, waiting for transfers between devices, on_device(): lax.ppermute(joined(own_low, parts[3 * (cls ^ turn) + 2]), 'sec', low)  5.12 us
    ppermute x1, waiting for transfers between devices, on_device(): lax.ppermute(to_low, 'sec', low)  3.97 us
    ppermute x1, starting transfers between devices, towards_owner(): lax.ppermute(held, ('op', 'sec'), second)  2.88 us
    ppermute x5, waiting for transfers between devices, over_op(): return lax.ppermute(x, 'op', [(o, o ^ bit) for o in range(n_op)])  2.42 us
    ppermute x1, starting transfers between devices, on_device(): lax.ppermute(to_low, 'sec', low)  2.14 us
    pallas_call x1, Pallas kernels, window_of(): pl.pallas_call(functools.partial(window_kernel, n_op), out_shape=in_vmem(...  2 us
  transfers between devices with their start and end apart: 15, of which 5 were waited for; matrix products, arithmetic and copies ran while one was open for 0% of the time, Pallas kernels for 15%

profile of v9, /device:TPU:17, one launch (start us, length us, event | category | flops | bytes accessed | tf_op | source)
XLA Modules:
  0.0 45.2 jit_solution(18406691237665588497)
XLA Ops:
  0.0 2.9 %collective-permute-start.1 = (bf16[1,3,128,128]{3,2,1,0:T(8,128)(2,1)}, bf16[1,3,128,128]{3,2,1,0:T(8,128)(2,1)S(1)}, u32[]{:S(2)}, u32[]{:S(2)}) collective-permute-start(bf16[1,3,128,128]{3,2,1,0:T(8,128)(2,1)} %bitcast.8), channel_id=1, source_target_pairs={{4,16},{5,17},{6,18},{7,19},{12,24},{13,25},{14,26},{15,27},{16,4}... | collective-permute-start | bytes 294920 | tf_op jit(solution)/shard_map/ppermute | solution.py:58
  2.9 0.1 collective-permute-start
  3.0 1.0 %pack.1 = (bf16[784,256]{1,0:T(8,128)(2,1)S(1)}, bf16[1,3,128,128]{3,2,1,0:T(8,128)(2,1)S(1)}) custom-call(s32[3]{0:T(128)} %shift.1, bf16[768,256]{1,0:T(8,128)(2,1)} %bitcast.7, bf16[1,3,128,128]{3,2,1,0:T(8,128)(2,1)} %bitcast.10), custom_call_target="tpu_custom_call" | custom-call | bytes 33554432 | tf_op jit(solution)/shard_map/pack/pallas_call | solution.py:122
  4.0 2.6 %collective-permute-start.6 = (bf16[784,256]{1,0:T(8,128)(2,1)S(1)}, bf16[784,256]{1,0:T(8,128)(2,1)S(1)}, u32[]{:S(2)}, u32[]{:S(2)}) collective-permute-start(bf16[784,256]{1,0:T(8,128)(2,1)S(1)} %get-tuple-element.27.refs_0_), channel_id=1, source_target_pairs={{0,16},{8,24},{16,0},{24,8},{1,17},{9,25},{17,1},{25,9},{2,18},{10... | collective-permute-start | bytes 1204232 | tf_op jit(solution)/shard_map/ppermute | solution.py:35
  6.6 2.0 %window.1.refs_4_ = bf16[3,256,512]{2,1,0:T(8,128)(2,1)S(1)} custom-call(bf16[3,256,1024]{2,1,0:T(8,128)(2,1)} %bitcast.6), custom_call_target="tpu_custom_call" | custom-call | bytes 2097152 | tf_op jit(solution)/shard_map/window/pallas_call | solution.py:163
  8.6 0.0 collective-permute-done.1
  8.6 0.0 collective-permute-done
  8.7 1.3 %collective-permute-start.3 = (bf16[2,3,128,128]{3,2,1,0:T(8,128)(2,1)S(1)}, bf16[2,3,128,128]{3,2,1,0:T(8,128)(2,1)S(1)}, u32[]{:S(2)}, u32[]{:S(2)}) collective-permute-start(bf16[2,3,128,128]{3,2,1,0:T(8,128)(2,1)S(1)} %pad_maximum_fusion.own), channel_id=1, source_target_pairs={{0,1},{1,0},{2,3},{3,2},{4,5},{5,4},{6,7},{7,6},{8,9},{9,8},{10,11... | collective-permute-start | bytes 589832 | tf_op jit(solution)/shard_map/ppermute | solution.py:39
  10.0 3.2 %collective-permute-start.2 = (bf16[2,3,128,128]{3,2,1,0:T(8,128)(2,1)S(1)}, bf16[2,3,128,128]{3,2,1,0:T(8,128)(2,1)S(1)}, u32[]{:S(2)}, u32[]{:S(2)}) collective-permute-start(bf16[2,3,128,128]{3,2,1,0:T(8,128)(2,1)S(1)} %pad_maximum_fusion.own), channel_id=1, source_target_pairs={{0,2},{1,3},{2,0},{3,1},{4,6},{5,7},{6,4},{7,5},{8,10},{9,11},{10,... | collective-permute-start | bytes 589832 | tf_op jit(solution)/shard_map/ppermute | solution.py:39
  13.3 1.2 %collective-permute-start.7 = (bf16[784,256]{1,0:T(8,128)(2,1)S(1)}, bf16[784,256]{1,0:T(8,128)(2,1)S(1)}, u32[]{:S(2)}, u32[]{:S(2)}) collective-permute-start(bf16[784,256]{1,0:T(8,128)(2,1)S(1)} %get-tuple-element.27.refs_0_), channel_id=1, source_target_pairs={{0,8},{8,0},{16,24},{24,16},{1,9},{9,1},{17,25},{25,17},{2,10},{10... | collective-permute-start | bytes 1204232 | tf_op jit(solution)/shard_map/ppermute | solution.py:35
  14.5 2.4 %collective-permute-done.6.refs_1_ = bf16[784,256]{1,0:T(8,128)(2,1)S(1)} collective-permute-done((bf16[784,256]{1,0:T(8,128)(2,1)S(1)}, bf16[784,256]{1,0:T(8,128)(2,1)S(1)}, u32[]{:S(2)}, u32[]{:S(2)}) %collective-permute-start.6) | collective-permute-done | bytes 401440 | tf_op jit(solution)/shard_map/ppermute | solution.py:35
  16.9 0.9 %collective-permute-start.8 = (bf16[784,256]{1,0:T(8,128)(2,1)S(1)}, bf16[784,256]{1,0:T(8,128)(2,1)S(1)}, u32[]{:S(2)}, u32[]{:S(2)}) collective-permute-start(bf16[784,256]{1,0:T(8,128)(2,1)S(1)} %collective-permute-done.6.refs_1_), channel_id=1, source_target_pairs={{0,8},{8,0},{16,24},{24,16},{1,9},{9,1},{17,25},{25,17},{2,10},{10... | collective-permute-start | bytes 1204232 | tf_op jit(solution)/shard_map/ppermute | solution.py:35
  17.8 1.4 %collective-permute-start.9 = (bf16[2,3,128,128]{3,2,1,0:T(8,128)(2,1)S(1)}, bf16[2,3,128,128]{3,2,1,0:T(8,128)(2,1)S(1)}, u32[]{:S(2)}, u32[]{:S(2)}) collective-permute-start(bf16[2,3,128,128]{3,2,1,0:T(8,128)(2,1)S(1)} %broadcast_select_fusion.1), channel_id=1, source_target_pairs={{0,8},{8,0},{16,24},{24,16},{1,9},{9,1},{17,25},{25,17},{2,10},{10... | collective-permute-start | bytes 589832 | tf_op jit(solution)/shard_map/ppermute | solution.py:35
  19.2 0.3 collective-permute-start.5
  19.5 2.1 %collective-permute-start.4 = (bf16[1,3,128,128]{3,2,1,0:T(8,128)(2,1)S(1)}, bf16[1,3,128,128]{3,2,1,0:T(8,128)(2,1)S(1)}, u32[]{:S(2)}, u32[]{:S(2)}) collective-permute-start(bf16[1,3,128,128]{3,2,1,0:T(8,128)(2,1)S(1)} %slice.6), channel_id=1, source_target_pairs={{0,2},{1,3},{2,0},{3,1},{4,6},{5,7},{6,4},{7,5},{8,10},{9,11},{10,... | collective-permute-start | bytes 294920 | tf_op jit(solution)/shard_map/ppermute | solution.py:39
  21.6 0.0 collective-permute-done.7.refs_2_
  21.6 0.0 collective-permute-done.8.refs_3_
  21.6 1.6 %left_products.1.z_ref = bf16[2,3,256,1536]{3,2,1,0:T(8,128)(2,1)S(1)} custom-call(bf16[784,256]{1,0:T(8,128)(2,1)S(1)} %get-tuple-element.27.refs_0_, bf16[784,256]{1,0:T(8,128)(2,1)S(1)} %collective-permute-done.6.refs_1_, bf16[784,256]{1,0:T(8,128)(2,1)S(1)} %collective-permute-done.7.refs_2_, bf16[784,256]{1,0:T(8,128)(2,1)S(1)} %collective-permute-done.8.refs_3_, ...), custom_call_target="tpu_custom_call" | custom-call | flops 1207959552 | bytes 1048576 | tf_op jit(solution)/shard_map/left_products/pallas_call | solution.py:195
  23.3 0.0 collective-permute-done.9.received
  23.3 1.0 %right_products.2 = (f32[3,256,128]{2,1,0:T(8,128)S(1)}, f32[3,256,128]{2,1,0:T(8,128)S(1)}, bf16[3,256,128]{2,1,0:T(8,128)(2,1)S(1)}) custom-call(bf16[2,3,256,1536]{3,2,1,0:T(8,128)(2,1)S(1)} %left_products.1.z_ref, bf16[2,3,128,128]{3,2,1,0:T(8,128)(2,1)S(1)} %pad_maximum_fusion.own, bf16[2,3,128,128]{3,2,1,0:T(8,128)(2,1)S(1)} %collective-permute-done.2.other, ...), custom_call_target="tpu_custom_call" | custom-call | tf_op jit(solution)/shard_map/right_products/pallas_call | solution.py:236
  24.3 0.0 collective-permute-done.5
  24.4 1.1 %collective-permute-start.10 = (bf16[2,3,128,128]{3,2,1,0:T(8,128)(2,1)S(1)}, bf16[2,3,128,128]{3,2,1,0:T(8,128)(2,1)S(1)}, u32[]{:S(2)}, u32[]{:S(2)}) collective-permute-start(bf16[2,3,128,128]{3,2,1,0:T(8,128)(2,1)S(1)} %broadcast_select_fusion), channel_id=1, source_target_pairs={{0,8},{8,0},{16,24},{24,16},{1,9},{9,1},{17,25},{25,17},{2,10},{10... | collective-permute-start | bytes 589832 | tf_op jit(solution)/shard_map/ppermute | solution.py:35
  25.5 1.9 %collective-permute-start.11 = (bf16[3,256,128]{2,1,0:T(8,128)(2,1)S(1)}, bf16[3,256,128]{2,1,0:T(8,128)(2,1)S(1)}, u32[]{:S(2)}, u32[]{:S(2)}) collective-permute-start(bf16[3,256,128]{2,1,0:T(8,128)(2,1)S(1)} %get-tuple-element.36), channel_id=1, source_target_pairs={{1,3},{2,0},{3,5},{4,2},{5,7},{6,4},{9,11},{10,8},{11,13},{12,10},... | collective-permute-start | bytes 589832 | tf_op jit(solution)/shard_map/ppermute | solution.py:347
  27.4 1.0 %right_products.3 = (f32[3,256,128]{2,1,0:T(8,128)S(1)}, bf16[3,256,128]{2,1,0:T(8,128)(2,1)S(1)}, bf16[3,256,128]{2,1,0:T(8,128)(2,1)S(1)}) custom-call(bf16[2,3,256,1536]{3,2,1,0:T(8,128)(2,1)S(1)} %left_products.1.z_ref, bf16[2,3,128,128]{3,2,1,0:T(8,128)(2,1)S(1)} %collective-permute-done.3.own, ...), custom_call_target="tpu_custom_call" | custom-call | tf_op jit(solution)/shard_map/right_products/pallas_call | solution.py:236
  28.4 2.1 %collective-permute-start.13 = (bf16[3,256,128]{2,1,0:T(8,128)(2,1)S(1)}, bf16[3,256,128]{2,1,0:T(8,128)(2,1)S(1)}, u32[]{:S(2)}, u32[]{:S(2)}) collective-permute-start(bf16[3,256,128]{2,1,0:T(8,128)(2,1)S(1)} %get-tuple-element.37), channel_id=1, source_target_pairs={{0,1},{1,0},{2,3},{3,2},{4,5},{5,4},{6,7},{7,6},{8,9},{9,8},{10,11... | collective-permute-start | bytes 589832 | tf_op jit(solution)/shard_map/ppermute | solution.py:350
  30.5 1.9 %collective-permute-start.14 = (bf16[3,256,128]{2,1,0:T(8,128)(2,1)S(1)}, bf16[3,256,128]{2,1,0:T(8,128)(2,1)S(1)}, u32[]{:S(2)}, u32[]{:S(2)}) collective-permute-start(bf16[3,256,128]{2,1,0:T(8,128)(2,1)S(1)} %get-tuple-element.38), channel_id=1, source_target_pairs={{1,2},{2,1},{3,4},{4,3},{5,6},{6,5},{9,10},{10,9},{11,12},{12,11},... | collective-permute-start | bytes 589832 | tf_op jit(solution)/shard_map/ppermute | solution.py:350
  32.5 1.4 %collective-permute-done.11.passing = bf16[3,256,128]{2,1,0:T(8,128)(2,1)S(1)} collective-permute-done((bf16[3,256,128]{2,1,0:T(8,128)(2,1)S(1)}, bf16[3,256,128]{2,1,0:T(8,128)(2,1)S(1)}, u32[]{:S(2)}, u32[]{:S(2)}) %collective-permute-start.11) | collective-permute-done | bytes 196640 | tf_op jit(solution)/shard_map/ppermute | solution.py:347
  33.9 0.7 %collective-permute-start.12 = (bf16[3,256,128]{2,1,0:T(8,128)(2,1)S(1)}, bf16[3,256,128]{2,1,0:T(8,128)(2,1)S(1)}, u32[]{:S(2)}, u32[]{:S(2)}) collective-permute-start(bf16[3,256,128]{2,1,0:T(8,128)(2,1)S(1)} %joined.1), channel_id=1, source_target_pairs={{0,1},{1,0},{2,3},{3,2},{4,5},{5,4},{6,7},{7,6},{8,9},{9,8},{10,11... | collective-permute-start | bytes 589832 | tf_op jit(solution)/shard_map/ppermute | solution.py:357
  34.6 4.0 %collective-permute-done.13.refs_3_ = bf16[3,256,128]{2,1,0:T(8,128)(2,1)S(1)} collective-permute-done((bf16[3,256,128]{2,1,0:T(8,128)(2,1)S(1)}, bf16[3,256,128]{2,1,0:T(8,128)(2,1)S(1)}, u32[]{:S(2)}, u32[]{:S(2)}) %collective-permute-start.13) | collective-permute-done | bytes 196640 | tf_op jit(solution)/shard_map/ppermute | solution.py:350
  38.6 0.6 %collective-permute-done.14.refs_4_ = bf16[3,256,128]{2,1,0:T(8,128)(2,1)S(1)} collective-permute-done((bf16[3,256,128]{2,1,0:T(8,128)(2,1)S(1)}, bf16[3,256,128]{2,1,0:T(8,128)(2,1)S(1)}, u32[]{:S(2)}, u32[]{:S(2)}) %collective-permute-start.14) | collective-permute-done | bytes 196640 | tf_op jit(solution)/shard_map/ppermute | solution.py:350
  39.2 5.1 %collective-permute-done.12.refs_2_ = bf16[3,256,128]{2,1,0:T(8,128)(2,1)S(1)} collective-permute-done((bf16[3,256,128]{2,1,0:T(8,128)(2,1)S(1)}, bf16[3,256,128]{2,1,0:T(8,128)(2,1)S(1)}, u32[]{:S(2)}, u32[]{:S(2)}) %collective-permute-start.12) | collective-permute-done | bytes 196640 | tf_op jit(solution)/shard_map/ppermute | solution.py:357
  44.4 0.8 %summed.1 = bf16[3,256,256]{2,1,0:T(8,128)(2,1)} custom-call(bf16[3,256,128]{2,1,0:T(8,128)(2,1)S(1)} %convert_element_type.3.refs_0_, f32[3,256,128]{2,1,0:T(8,128)S(1)} %get-tuple-element.33.refs_1_, bf16[3,256,128]{2,1,0:T(8,128)(2,1)S(1)} %collective-permute-done.12.refs_2_, bf16[3,256,128]{2,1,0:T(8,128)(2,1)S(1)} %collective-permute-done.13.refs_3_, ...), custom_call_target="tpu_custom_call" | custom-call | tf_op jit(solution)/shard_map/summed/pallas_call | solution.py:293
  (14 shorter events, 0.2 us)
Async XLA Ops:
  0.0 8.6 %collective-permute-start.1 = (bf16[1,3,128,128]{3,2,1,0:T(8,128)(2,1)}, bf16[1,3,128,128]{3,2,1,0:T(8,128)(2,1)S(1)}, u32[]{:S(2)}, u32[]{:S(2)}) collective-permute-start(bf16[1,3,128,128]{3,2,1,0:T(8,128)(2,1)} %bitcast.8), channel_id=1, source_target_pairs={{4,16},{5,17},{6,18},{7,19},{12,24},{13,25},{14,26},{15,27},{16,4}... | collective-permute-start | bytes 294920 | tf_op jit(solution)/shard_map/ppermute | solution.py:58
  2.9 5.8 %collective-permute-start = (bf16[1,3,128,128]{3,2,1,0:T(8,128)(2,1)}, bf16[1,3,128,128]{3,2,1,0:T(8,128)(2,1)S(1)}, u32[]{:S(2)}, u32[]{:S(2)}) collective-permute-start(bf16[1,3,128,128]{3,2,1,0:T(8,128)(2,1)} %bitcast.9), channel_id=1, source_target_pairs={{0,4},{1,5},{2,6},{3,7},{4,20},{5,21},{6,22},{7,23},{8,12},{9,13},... | collective-permute-start | bytes 294920 | tf_op jit(solution)/shard_map/ppermute | solution.py:58
  4.0 12.9 %collective-permute-start.6 = (bf16[784,256]{1,0:T(8,128)(2,1)S(1)}, bf16[784,256]{1,0:T(8,128)(2,1)S(1)}, u32[]{:S(2)}, u32[]{:S(2)}) collective-permute-start(bf16[784,256]{1,0:T(8,128)(2,1)S(1)} %get-tuple-element.27.refs_0_), channel_id=1, source_target_pairs={{0,16},{8,24},{16,0},{24,8},{1,17},{9,25},{17,1},{25,9},{2,18},{10... | collective-permute-start | bytes 1204232 | tf_op jit(solution)/shard_map/ppermute | solution.py:35
  8.7 9.1 %collective-permute-start.3 = (bf16[2,3,128,128]{3,2,1,0:T(8,128)(2,1)S(1)}, bf16[2,3,128,128]{3,2,1,0:T(8,128)(2,1)S(1)}, u32[]{:S(2)}, u32[]{:S(2)}) collective-permute-start(bf16[2,3,128,128]{3,2,1,0:T(8,128)(2,1)S(1)} %pad_maximum_fusion.own), channel_id=1, source_target_pairs={{0,1},{1,0},{2,3},{3,2},{4,5},{5,4},{6,7},{7,6},{8,9},{9,8},{10,11... | collective-permute-start | bytes 589832 | tf_op jit(solution)/shard_map/ppermute | solution.py:39
  10.0 7.8 %collective-permute-start.2 = (bf16[2,3,128,128]{3,2,1,0:T(8,128)(2,1)S(1)}, bf16[2,3,128,128]{3,2,1,0:T(8,128)(2,1)S(1)}, u32[]{:S(2)}, u32[]{:S(2)}) collective-permute-start(bf16[2,3,128,128]{3,2,1,0:T(8,128)(2,1)S(1)} %pad_maximum_fusion.own), channel_id=1, source_target_pairs={{0,2},{1,3},{2,0},{3,1},{4,6},{5,7},{6,4},{7,5},{8,10},{9,11},{10,... | collective-permute-start | bytes 589832 | tf_op jit(solution)/shard_map/ppermute | solution.py:39
  13.3 8.4 %collective-permute-start.7 = (bf16[784,256]{1,0:T(8,128)(2,1)S(1)}, bf16[784,256]{1,0:T(8,128)(2,1)S(1)}, u32[]{:S(2)}, u32[]{:S(2)}) collective-permute-start(bf16[784,256]{1,0:T(8,128)(2,1)S(1)} %get-tuple-element.27.refs_0_), channel_id=1, source_target_pairs={{0,8},{8,0},{16,24},{24,16},{1,9},{9,1},{17,25},{25,17},{2,10},{10... | collective-permute-start | bytes 1204232 | tf_op jit(solution)/shard_map/ppermute | solution.py:35
  16.9 4.8 %collective-permute-start.8 = (bf16[784,256]{1,0:T(8,128)(2,1)S(1)}, bf16[784,256]{1,0:T(8,128)(2,1)S(1)}, u32[]{:S(2)}, u32[]{:S(2)}) collective-permute-start(bf16[784,256]{1,0:T(8,128)(2,1)S(1)} %collective-permute-done.6.refs_1_), channel_id=1, source_target_pairs={{0,8},{8,0},{16,24},{24,16},{1,9},{9,1},{17,25},{25,17},{2,10},{10... | collective-permute-start | bytes 1204232 | tf_op jit(solution)/shard_map/ppermute | solution.py:35
  17.8 5.4 %collective-permute-start.9 = (bf16[2,3,128,128]{3,2,1,0:T(8,128)(2,1)S(1)}, bf16[2,3,128,128]{3,2,1,0:T(8,128)(2,1)S(1)}, u32[]{:S(2)}, u32[]{:S(2)}) collective-permute-start(bf16[2,3,128,128]{3,2,1,0:T(8,128)(2,1)S(1)} %broadcast_select_fusion.1), channel_id=1, source_target_pairs={{0,8},{8,0},{16,24},{24,16},{1,9},{9,1},{17,25},{25,17},{2,10},{10... | collective-permute-start | bytes 589832 | tf_op jit(solution)/shard_map/ppermute | solution.py:35
  19.2 5.1 %collective-permute-start.5 = (bf16[1,3,128,128]{3,2,1,0:T(8,128)(2,1)S(1)}, bf16[1,3,128,128]{3,2,1,0:T(8,128)(2,1)S(1)}, u32[]{:S(2)}, u32[]{:S(2)}) collective-permute-start(bf16[1,3,128,128]{3,2,1,0:T(8,128)(2,1)S(1)} %slice.7), channel_id=1, source_target_pairs={{0,1},{1,0},{2,3},{3,2},{4,5},{5,4},{6,7},{7,6},{8,9},{9,8},{10,11... | collective-permute-start | bytes 294920 | tf_op jit(solution)/shard_map/ppermute | solution.py:39
  19.5 4.8 %collective-permute-start.4 = (bf16[1,3,128,128]{3,2,1,0:T(8,128)(2,1)S(1)}, bf16[1,3,128,128]{3,2,1,0:T(8,128)(2,1)S(1)}, u32[]{:S(2)}, u32[]{:S(2)}) collective-permute-start(bf16[1,3,128,128]{3,2,1,0:T(8,128)(2,1)S(1)} %slice.6), channel_id=1, source_target_pairs={{0,2},{1,3},{2,0},{3,1},{4,6},{5,7},{6,4},{7,5},{8,10},{9,11},{10,... | collective-permute-start | bytes 294920 | tf_op jit(solution)/shard_map/ppermute | solution.py:39
  24.4 3.0 %collective-permute-start.10 = (bf16[2,3,128,128]{3,2,1,0:T(8,128)(2,1)S(1)}, bf16[2,3,128,128]{3,2,1,0:T(8,128)(2,1)S(1)}, u32[]{:S(2)}, u32[]{:S(2)}) collective-permute-start(bf16[2,3,128,128]{3,2,1,0:T(8,128)(2,1)S(1)} %broadcast_select_fusion), channel_id=1, source_target_pairs={{0,8},{8,0},{16,24},{24,16},{1,9},{9,1},{17,25},{25,17},{2,10},{10... | collective-permute-start | bytes 589832 | tf_op jit(solution)/shard_map/ppermute | solution.py:35
  25.5 8.4 %collective-permute-start.11 = (bf16[3,256,128]{2,1,0:T(8,128)(2,1)S(1)}, bf16[3,256,128]{2,1,0:T(8,128)(2,1)S(1)}, u32[]{:S(2)}, u32[]{:S(2)}) collective-permute-start(bf16[3,256,128]{2,1,0:T(8,128)(2,1)S(1)} %get-tuple-element.36), channel_id=1, source_target_pairs={{1,3},{2,0},{3,5},{4,2},{5,7},{6,4},{9,11},{10,8},{11,13},{12,10},... | collective-permute-start | bytes 589832 | tf_op jit(solution)/shard_map/ppermute | solution.py:347
  28.4 10.2 %collective-permute-start.13 = (bf16[3,256,128]{2,1,0:T(8,128)(2,1)S(1)}, bf16[3,256,128]{2,1,0:T(8,128)(2,1)S(1)}, u32[]{:S(2)}, u32[]{:S(2)}) collective-permute-start(bf16[3,256,128]{2,1,0:T(8,128)(2,1)S(1)} %get-tuple-element.37), channel_id=1, source_target_pairs={{0,1},{1,0},{2,3},{3,2},{4,5},{5,4},{6,7},{7,6},{8,9},{9,8},{10,11... | collective-permute-start | bytes 589832 | tf_op jit(solution)/shard_map/ppermute | solution.py:350
  30.5 8.7 %collective-permute-start.14 = (bf16[3,256,128]{2,1,0:T(8,128)(2,1)S(1)}, bf16[3,256,128]{2,1,0:T(8,128)(2,1)S(1)}, u32[]{:S(2)}, u32[]{:S(2)}) collective-permute-start(bf16[3,256,128]{2,1,0:T(8,128)(2,1)S(1)} %get-tuple-element.38), channel_id=1, source_target_pairs={{1,2},{2,1},{3,4},{4,3},{5,6},{6,5},{9,10},{10,9},{11,12},{12,11},... | collective-permute-start | bytes 589832 | tf_op jit(solution)/shard_map/ppermute | solution.py:350
  33.9 10.4 %collective-permute-start.12 = (bf16[3,256,128]{2,1,0:T(8,128)(2,1)S(1)}, bf16[3,256,128]{2,1,0:T(8,128)(2,1)S(1)}, u32[]{:S(2)}, u32[]{:S(2)}) collective-permute-start(bf16[3,256,128]{2,1,0:T(8,128)(2,1)S(1)} %joined.1), channel_id=1, source_target_pairs={{0,1},{1,0},{2,3},{3,2},{4,5},{5,4},{6,7},{7,6},{8,9},{9,8},{10,11... | collective-permute-start | bytes 589832 | tf_op jit(solution)/shard_map/ppermute | solution.py:357
